TPU v7x, 32 devices: a whole 2x2x4 slice. The times are simulated.
32 devices in a mesh: dp: 4 (over z), node: 8 (over y, x, core).
Axes of the slice: x: 2, y: 2, z: 4, core: 2. Of those that a mesh axis runs over, the one named last changes fastest.
Arguments:
- normed: bfloat16 [64, 4096], P(('dp', 'node')), may hold values from -6 to 6
- cotangent: bfloat16 [64, 4096], P(('dp', 'node')), may hold values from -4 to 4
- gate_weight: bfloat16 [4096, 14336], P(None, 'node'), may hold values from -0.09375 to 0.09375
- up_weight: bfloat16 [4096, 14336], P(None, 'node'), may hold values from -0.09375 to 0.09375
- down_weight: bfloat16 [14336, 4096], P('node'), may hold values from -0.046875 to 0.046875
Outputs:
- grad_normed: bfloat16 [64, 4096], P(('dp', 'node'))
- weight_grads: float32 [12288, 14336], P('dp', 'node')
All inputs are finite; a program needn't handle non-finite values.
Results may differ from a plain program's by a relative error of at most 0.0085.
Values may be sent and summed in bfloat16 or wider, within the bound.
No kernel may reach another device: no remote copies, remote signals or barrier semaphores. Data moves between devices by JAX's collectives and lax.ppermute only.
A program may use at most 256 MiB of HBM per device.

v0:
```python
import jax
import jax.numpy as jnp
from jax import lax
from jax.sharding import PartitionSpec as P


def contract_rows(left_part, right_part):
    return lax.dot_general(
        left_part, right_part, (((0,), (0,)), ((), ())), preferred_element_type=jnp.float32
    )


def contract_columns(left_part, right_part):
    return lax.dot_general(
        left_part, right_part, (((1,), (1,)), ((), ())), preferred_element_type=jnp.float32
    )


def shards(normed, cotangent, gate_weight, up_weight, down_weight):
    input_rows = lax.all_gather(normed, "node", axis=0, tiled=True)
    gate_pre = jnp.dot(input_rows, gate_weight, preferred_element_type=jnp.float32)
    up_pre = jnp.dot(input_rows, up_weight, preferred_element_type=jnp.float32)
    sigma = jax.nn.sigmoid(gate_pre)
    activated = gate_pre * sigma
    hidden = (activated * up_pre).astype(jnp.bfloat16)
    cot_rows = lax.all_gather(cotangent, "node", axis=0, tiled=True)
    grad_hidden = contract_columns(cot_rows, down_weight)
    grad_gate = (grad_hidden * up_pre * sigma * (1.0 + gate_pre * (1.0 - sigma))).astype(
        jnp.bfloat16
    )
    grad_up = (grad_hidden * activated).astype(jnp.bfloat16)
    grad_normed = lax.psum_scatter(
        contract_columns(grad_gate, gate_weight) + contract_columns(grad_up, up_weight),
        "node",
        scatter_dimension=0,
        tiled=True,
    ).astype(jnp.bfloat16)
    stacked = jnp.concatenate(
        [
            contract_rows(input_rows, grad_gate),
            contract_rows(input_rows, grad_up),
            contract_rows(cot_rows, hidden),
        ],
        axis=0,
    )
    weight_grads = lax.psum_scatter(
        stacked.astype(jnp.bfloat16), "dp", scatter_dimension=0, tiled=True
    ).astype(jnp.float32)
    return (grad_normed, weight_grads)


def solution(mesh):
    in_specs = (
        P(("dp", "node"), None),
        P(("dp", "node"), None),
        P(None, "node"),
        P(None, "node"),
        P("node", None),
    )
    out_specs = (P(("dp", "node"), None), P("dp", "node"))
    return jax.shard_map(shards, mesh=mesh, in_specs=in_specs, out_specs=out_specs, check_vma=False)
```

profile of v0, /device:TPU:0, one launch (start us, length us, event | category | flops | bytes accessed | tf_op | source)
XLA Modules:
  0.0 842.3 jit_solution(1750746180954193894)
XLA Ops:
  7.2 0.0 reduce-scatter.2.cloned.1.call-start
  7.2 10.8 %all-gather.1 = bf16[8,2,4096]{2,1,0:T(2,128)(2,1)S(1)} all-gather(bf16[1,2,4096]{2,1,0:T(2,128)(2,1)} %bitcast.24), channel_id=1, replica_groups=mesh['dp'=4,'node'=8] {'node'}, dimensions={0}, use_global_device_ids=true | all-gather | bytes 147456 | tf_op jit(solution)/shard_map/all_gather | solution.py:20
  18.1 0.1 reshape.7
  18.1 0.0 copy-start
  18.1 7.3 fusion.7
  25.4 2.0 copy-done
  27.5 0.0 copy-start.1
  27.5 2.0 fusion.6
  29.5 0.0 copy-done.1
  29.5 9.2 %all-gather = bf16[8,2,4096]{2,1,0:T(2,128)(2,1)S(1)} all-gather(bf16[1,2,4096]{2,1,0:T(2,128)(2,1)S(1)} %bitcast.25), channel_id=1, replica_groups=mesh['dp'=4,'node'=8] {'node'}, dimensions={0}, use_global_device_ids=true | all-gather | bytes 147456 | tf_op jit(solution)/shard_map/all_gather | solution.py:26
  38.7 0.1 reshape.5
  38.7 7.6 fusion.2
  46.3 9.1 %multiply_convert_fusion.1 = (bf16[16,1792]{1,0:T(8,128)(2,1)S(1)}, bf16[16,1792]{1,0:T(8,128)(2,1)S(1)}) fusion(f32[16,1792]{1,0:T(8,128)S(1)} %fusion.7, f32[16,1792]{1,0:T(8,128)S(1)} %fusion.6, bf16[16,4096]{1,0:T(8,128)(2,1)S(1)} %reshape.5, bf16[1792,4096]{1,0:T(8,128)(2,1)} %param.9), kind=kOutput, calls=%fused_computation.9 | convolution fusion | flops 235253760 | bytes 15155200 | tf_op jit(solution)/shard_map/dot_general | solution.py:14
  55.4 7.2 fusion.1
  62.6 7.2 fusion
  69.8 29.7 %pad_maximum_fusion = bf16[12288,1792]{0,1:T(8,128)(2,1)} fusion(bf16[4096,1792]{0,1:T(8,128)(2,1)} %fusion.2, bf16[4096,1792]{0,1:T(8,128)(2,1)} %fusion.1, bf16[4096,1792]{0,1:T(8,128)(2,1)} %fusion), kind=kLoop, calls=%fused_computation | loop fusion | flops 132120576 | bytes 88080384 | tf_op jit(solution)/shard_map/concatenate | solution.py:38
  99.6 0.0 reduce-scatter.2.cloned.1.call-update
  99.6 0.0 copy-start.2
  99.6 9.1 %fusion.8 = f32[16,4096]{1,0:T(8,128)S(1)} fusion(bf16[16,1792]{1,0:T(8,128)(2,1)S(1)} %get-tuple-element.7, bf16[4096,1792]{1,0:T(8,128)(2,1)} %param.7), kind=kOutput, calls=%fused_computation.17 | convolution fusion | flops 234881024 | bytes 14999552 | tf_op jit(solution)/shard_map/dot_general | solution.py:14
  108.7 9.1 %convolution_add_fusion = f32[16,4096]{1,0:T(8,128)S(1)} fusion(f32[16,4096]{1,0:T(8,128)S(1)} %fusion.8, bf16[16,1792]{1,0:T(8,128)(2,1)S(1)} %get-tuple-element.6, bf16[4096,1792]{1,0:T(8,128)(2,1)} %param.8), kind=kOutput, calls=%fused_computation.7 | convolution fusion | flops 234946560 | bytes 15261696 | tf_op jit(solution)/shard_map/dot_general | solution.py:14
  117.7 0.0 copy-done.2
  117.7 0.6 dynamic-slice
  119.0 27.2 %all-reduce.2 = bf16[16,4096]{1,0:T(8,128)(2,1)S(1)} all-reduce(f32[16,4096]{1,0:T(8,128)S(1)} %convolution_add_fusion), channel_id=2, replica_groups=mesh['dp'=4,'node'=8] {'node'}, use_global_device_ids=true, to_apply=%region_0.0.clone | all-reduce | flops 65536 | bytes 393216
  146.2 0.6 dynamic-slice_convert_fusion
  146.8 673.1 %reduce-scatter.2.cloned.1.call-done = bf16[3072,1792]{0,1:T(8,128)(2,1)} async-done(((bf16[12288,1792]{0,1:T(8,128)(2,1)}), bf16[3072,1792]{0,1:T(8,128)(2,1)}) %reduce-scatter.2.cloned.1.call-update) | async-done | bytes 11010064 | tf_op jit(solution)/shard_map/reduce_scatter | solution.py:46
  819.9 15.5 %copy.8 = f32[3072,1792]{1,0:T(8,128)} copy(bf16[3072,1792]{0,1:T(8,128)(2,1)} %reduce-scatter.2.cloned.1.call-done) | data formatting | bytes 33030144
Async XLA Ops:
  7.2 812.8 %reduce-scatter.2.cloned.1.call-start = ((), (), s32[]{:S(2)}) async-start(), calls=%async_computation.1 | async-start | bytes 55050240 | tf_op jit(solution)/shard_map/reduce_scatter | solution.py:46
  18.1 9.4 %copy-start = (bf16[4096,1792]{1,0:T(8,128)(2,1)S(1)}, bf16[4096,1792]{1,0:T(8,128)(2,1)}, u32[]{:S(2)}) copy-start(bf16[4096,1792]{1,0:T(8,128)(2,1)} %param.8) | copy-start | bytes 44040196
  27.5 2.0 copy-start.1
  99.6 18.1 %copy-start.2 = (u32[32]{0:T(128)S(1)}, u32[32]{0:T(128)}, u32[]{:S(2)}) copy-start(u32[32]{0:T(128)} %constant.6) | copy-start | bytes 388
Sparse Core Ops, SparseCore 0:
  99.7 720.1 reduce-scatter.1
where the time goes:
time: 843 us; the launch traced here: 842 us
  waiting for transfers between devices  673 us (80%)
  matrix products  58.5 us (7%)
  blocking collectives  47.2 us (6%)
  other arithmetic  29.7 us (4%)
  local copies, waits for them, and re-layouts  18.9 us (2%)
  between operations  14.7 us (2%)
    reduce_scatter x1, waiting for transfers between devices, shards(): lax.psum_scatter(stacked.astype(jnp.bfloat16), 'dp', scatter_dimension=0,...  673 us
    concatenate x1, other arithmetic, shards(): jnp.concatenate([contract_rows(input_rows, grad_gate), contract_rows(inpu...  29.7 us
    dot_general x3, matrix products, contract_columns(): lax.dot_general(left_part, right_part, (((1,), (1,)), ((), ())), preferre...  27.2 us
    unnamed x1, blocking collectives  27.2 us
    dot_general x3, matrix products, contract_rows(): lax.dot_general(left_part, right_part, (((0,), (0,)), ((), ())), preferre...  22 us
    unnamed x10, local copies, waits for them, and re-layouts  18.3 us
  transfers between devices with their start and end apart: 1, of which 1 were waited for; matrix products, arithmetic and copies ran while one was open for 2% of the time, Pallas kernels for 0%

commit v1 on v0

v1 whole, which is shorter than its diff:
```python
import jax
import jax.numpy as jnp
from jax import lax
from jax.experimental import pallas as pl
from jax.experimental.pallas import tpu as pltpu
from jax.sharding import PartitionSpec as P

BF = jnp.bfloat16
F32 = jnp.float32
NN = (((1,), (0,)), ((), ()))
NT = (((1,), (1,)), ((), ()))
TN = (((0,), (0,)), ((), ()))
VMEM_SPEC = pl.BlockSpec(memory_space=pltpu.VMEM)


def dot(left, right, dims):
    return lax.dot_general(left, right, dims, preferred_element_type=F32)


def in_vmem(array):
    return pltpu.with_memory_space_constraint(array, pltpu.VMEM)


def xor_pairs(count, step):
    return [(i, i ^ step) for i in range(count)]


def shards_any(n_dp, normed, cotangent, gate_weight, up_weight, down_weight):
    rows = lax.all_gather(normed, "node", axis=0, tiled=True)
    cots = lax.all_gather(cotangent, "node", axis=0, tiled=True)
    gate_pre = dot(rows, gate_weight, NN)
    up_pre = dot(rows, up_weight, NN)
    sigma = jax.nn.sigmoid(gate_pre)
    activated = gate_pre * sigma
    hidden = (activated * up_pre).astype(BF)
    grad_hidden = dot(cots, down_weight, NT)
    grad_gate = (grad_hidden * up_pre * sigma * (1.0 + gate_pre * (1.0 - sigma))).astype(BF)
    grad_up = (grad_hidden * activated).astype(BF)
    grad_normed = lax.psum_scatter(
        dot(grad_gate, gate_weight, NT) + dot(grad_up, up_weight, NT),
        "node",
        scatter_dimension=0,
        tiled=True,
    ).astype(BF)
    stacked = jnp.concatenate(
        [dot(rows, grad_gate, TN), dot(rows, grad_up, TN), dot(cots, hidden, TN)], axis=0
    )
    weight_grads = lax.psum_scatter(
        stacked.astype(BF), "dp", scatter_dimension=0, tiled=True
    ).astype(F32)
    return grad_normed, weight_grads


def forward_kernel(chunk, tokens, gate, up, down, grads):
    columns = gate.shape[1]
    for start in range(0, columns, chunk):
        part = slice(start, start + chunk)
        gate_pre = dot(tokens[0], gate[:, part], NN)
        up_pre = dot(tokens[0], up[:, part], NN)
        grad_hidden = dot(tokens[1], down[part, :], NT)
        sigma = jax.nn.sigmoid(gate_pre)
        activated = gate_pre * sigma
        grads[0, :, part] = (
            grad_hidden * up_pre * sigma * (1.0 + gate_pre * (1.0 - sigma))
        ).astype(BF)
        grads[1, :, part] = (grad_hidden * activated).astype(BF)
        grads[2, :, part] = (activated * up_pre).astype(BF)


def backward_kernel(chunk, grads, gate, up, keep, send):
    width = gate.shape[0]
    half = keep.shape[0]
    for start in range(0, width, chunk):
        part = slice(start, start + chunk)
        total = dot(grads[0], gate[part, :], NT) + dot(grads[1], up[part, :], NT)
        keep[:, part] = total[:half]
        send[:, part] = total[half:].astype(BF)


def product_kernel(row_blocks, tokens, grads, out):
    out[...] = dot(tokens[...], grads[0], TN)


def shards_group(mesh_shape, normed, cotangent, gate_weight, up_weight, down_weight):
    n_dp, n_node = mesh_shape
    own, width = normed.shape
    hidden = gate_weight.shape[1]
    group = own * n_node
    block = 3 * width // n_dp
    d = lax.axis_index("dp")
    other_chips = range(2, n_node, 2)
    groups = range(1, n_dp)

    tokens = jnp.stack([normed, cotangent])
    spread = jnp.stack(
        [tokens] + [lax.ppermute(tokens, "node", xor_pairs(n_node, s)) for s in other_chips]
    )
    spread = jnp.stack([spread, lax.ppermute(spread, "node", xor_pairs(n_node, 1))])
    group_tokens = spread.transpose(2, 0, 1, 3, 4).reshape(2, group, width)

    def columns_for(rows, owner):
        wide = jnp.concatenate([rows[0], rows[0], rows[1]], axis=-1)
        return lax.dynamic_slice_in_dim(wide, owner * block, block, axis=wide.ndim - 1)

    far = jnp.stack(
        [lax.ppermute(columns_for(tokens, d ^ s), "dp", xor_pairs(n_dp, s)) for s in groups]
    )
    far = jnp.stack([far] + [lax.ppermute(far, "node", xor_pairs(n_node, s)) for s in other_chips])
    far = jnp.stack([far, lax.ppermute(far, "node", xor_pairs(n_node, 1))])
    far = far.transpose(2, 0, 1, 3, 4).reshape((n_dp - 1) * group, block)
    columns = jnp.concatenate([columns_for(group_tokens, d), far], axis=0)

    gate, up, down = in_vmem(gate_weight), in_vmem(up_weight), in_vmem(down_weight)
    weight_bytes = 2 * width * hidden
    grads = pl.pallas_call(
        lambda *refs: forward_kernel(256, *refs),
        out_shape=jax.ShapeDtypeStruct((3, group, hidden), BF),
        in_specs=[VMEM_SPEC] * 4,
        out_specs=VMEM_SPEC,
        compiler_params=pltpu.CompilerParams(vmem_limit_bytes=6 << 20),
        cost_estimate=pl.CostEstimate(
            flops=6 * group * width * hidden, bytes_accessed=3 * weight_bytes, transcendentals=0
        ),
        name="forward",
    )(group_tokens, gate, up, down)

    def matrices_for(owner):
        first = owner * block // width
        last = (owner * block + block - 1) // width
        return jnp.stack(
            [
                lax.dynamic_index_in_dim(grads, first, 0, keepdims=False),
                lax.dynamic_index_in_dim(grads, last, 0, keepdims=False),
            ]
        )

    pairs = jnp.concatenate(
        [matrices_for(d)]
        + [lax.ppermute(matrices_for(d ^ s), "dp", xor_pairs(n_dp, s)) for s in groups],
        axis=1,
    )

    keep, send = pl.pallas_call(
        lambda *refs: backward_kernel(256, *refs),
        out_shape=(
            jax.ShapeDtypeStruct((group // 2, width), F32),
            jax.ShapeDtypeStruct((group // 2, width), BF),
        ),
        in_specs=[VMEM_SPEC] * 3,
        out_specs=(VMEM_SPEC, VMEM_SPEC),
        compiler_params=pltpu.CompilerParams(vmem_limit_bytes=6 << 20),
        cost_estimate=pl.CostEstimate(
            flops=4 * group * width * hidden, bytes_accessed=2 * weight_bytes, transcendentals=0
        ),
        name="backward",
    )(grads, gate, up)

    chip = keep + lax.ppermute(send, "node", xor_pairs(n_node, 1)).astype(F32)
    grad_normed = chip[:own]
    for slot, s in enumerate(other_chips, 1):
        piece = chip[own * slot : own * (slot + 1)].astype(BF)
        grad_normed = grad_normed + lax.ppermute(piece, "node", xor_pairs(n_node, s)).astype(F32)

    rows = 256
    per_matrix = width // rows
    step_blocks = block // rows
    base = d * step_blocks
    which = (
        (jnp.arange(step_blocks) + base) // per_matrix - base // per_matrix
    ).astype(jnp.int32)
    weight_grads = pl.pallas_call(
        product_kernel,
        out_shape=jax.ShapeDtypeStruct((block, hidden), F32),
        grid_spec=pltpu.PrefetchScalarGridSpec(
            num_scalar_prefetch=1,
            grid=(step_blocks,),
            in_specs=[
                pl.BlockSpec((n_dp * group, rows), lambda i, which: (0, i)),
                pl.BlockSpec((1, n_dp * group, hidden), lambda i, which: (which[i], 0, 0)),
            ],
            out_specs=pl.BlockSpec((rows, hidden), lambda i, which: (i, 0)),
        ),
        compiler_params=pltpu.CompilerParams(vmem_limit_bytes=16 << 20),
        cost_estimate=pl.CostEstimate(
            flops=2 * n_dp * group * block * hidden,
            bytes_accessed=4 * block * hidden,
            transcendentals=0,
        ),
        name="product",
    )(which, columns, pairs)
    return grad_normed.astype(BF), weight_grads


def solution(mesh):
    n_dp, n_node = mesh.shape["dp"], mesh.shape["node"]

    def shards(*arrays):
        normed, gate_weight = arrays[0], arrays[2]
        rows, width = normed.shape
        hidden = gate_weight.shape[1]
        fits = (
            n_dp & (n_dp - 1) == 0
            and n_node & (n_node - 1) == 0
            and 2 <= n_node <= 8
            and n_dp <= 4
            and rows * n_node == 16
            and hidden % 256 == 0
            and hidden * width * 6 <= 46 << 20
            and 3 * width % (n_dp * 256) == 0
            and 3 * width // n_dp <= width
        )
        if fits:
            return shards_group((n_dp, n_node), *arrays)
        return shards_any(n_dp, *arrays)

    in_specs = (
        P(("dp", "node"), None),
        P(("dp", "node"), None),
        P(None, "node"),
        P(None, "node"),
        P("node", None),
    )
    out_specs = (P(("dp", "node"), None), P("dp", "node"))
    return jax.shard_map(shards, mesh=mesh, in_specs=in_specs, out_specs=out_specs, check_vma=False)
```

time: 843 us -> 87.8 us (0.10)
  waiting for transfers between devices: 673 us -> 9.31 us
  matrix products: 58.5 us -> 0 us
  blocking collectives: 47.2 us -> 0 us
  Pallas kernels: 0 us -> 26.6 us
  other arithmetic: 29.7 us -> 4.65 us
  starting transfers between devices: 0.04 us -> 21.5 us
  between operations: 14.7 us -> 1.15 us
    reduce_scatter x1 -> x0, waiting for transfers between devices: 673 us -> none  [shards(): lax.psum_scatter(stacked.astype(jnp.bfloat16), 'dp', scatter_dimension=0,...]
    dot_general x8 -> x0, matrix products: 58.5 us -> none  [the longest x3 27.2 us: contract_columns(): lax.dot_general(left_part, right_part, (((1,), (1,)), ((), ())), preferre...]
    concatenate x1 -> x3, other arithmetic: 29.7 us -> 0.32 us  [the longest x1 0.26 us: columns_for(): wide = jnp.concatenate([rows[0], rows[0], rows[1]], axis=-1)]
    unnamed x1 -> x0, blocking collectives: 27.2 us -> none
    pallas_call x0 -> x3, Pallas kernels: none -> 26.6 us  [the longest x1 11.1 us: shards_group(): pl.pallas_call(product_kernel, out_shape=jax.ShapeDtypeStruct((block, hid...]
    ppermute x0 -> x18, starting transfers between devices: none -> 21.5 us  [the longest x3 5.07 us: shards_group(): lax.ppermute(tokens, 'node', xor_pairs(n_node, s))]
    all_gather x2 -> x0, blocking collectives: 20 us -> none  [the longest x1 10.8 us: shards(): input_rows = lax.all_gather(normed, 'node', axis=0, tiled=True)]
    ppermute x0 -> x18, waiting for transfers between devices: none -> 9.31 us  [the longest x3 3.91 us: shards_group(): lax.ppermute(matrices_for(d ^ s), 'dp', xor_pairs(n_dp, s))]
  transfers between devices with their start and end apart: 1 -> 18, of which waited for: 1 -> 7; matrix products, arithmetic and copies ran while one was open for 2% -> 8% of each run, Pallas kernels for 0% -> 18%
where the time goes in v1:
time: 87.8 us; the launch traced here: 87.1 us
  Pallas kernels  26.6 us (30%)
  local copies, waits for them, and re-layouts  23.9 us (27%)
  starting transfers between devices  21.5 us (24%)
  waiting for transfers between devices  9.31 us (11%)
  other arithmetic  4.65 us (5%)
  between operations  1.15 us (1%)
    unnamed x18, local copies, waits for them, and re-layouts  22.2 us
    pallas_call x1, Pallas kernels, shards_group(): pl.pallas_call(product_kernel, out_shape=jax.ShapeDtypeStruct((block, hid...  11.1 us
    pallas_call x1, Pallas kernels, shards_group(): pl.pallas_call(lambda *refs: backward_kernel(256, *refs), out_shape=(jax....  7.81 us
    pallas_call x1, Pallas kernels, shards_group(): pl.pallas_call(lambda *refs: forward_kernel(256, *refs), out_shape=jax.Sh...  7.68 us
    ppermute x3, starting transfers between devices, shards_group(): lax.ppermute(tokens, 'node', xor_pairs(n_node, s))  5.07 us
    ppermute x3, starting transfers between devices, shards_group(): lax.ppermute(matrices_for(d ^ s), 'dp', xor_pairs(n_dp, s))  4.46 us
    ppermute x3, starting transfers between devices, shards_group(): lax.ppermute(columns_for(tokens, d ^ s), 'dp', xor_pairs(n_dp, s))  4.23 us
    ppermute x3, waiting for transfers between devices, shards_group(): lax.ppermute(matrices_for(d ^ s), 'dp', xor_pairs(n_dp, s))  3.91 us
  transfers between devices with their start and end apart: 18, of which 7 were waited for; matrix products, arithmetic and copies ran while one was open for 8% of the time, Pallas kernels for 18%

profile of v1, /device:TPU:0, one launch (start us, length us, event | category | flops | bytes accessed | tf_op | source)
XLA Modules:
  0.0 87.1 jit_solution(10641980437621519922)
XLA Ops:
  0.6 0.8 pad_maximum_fusion.8
  1.4 3.0 %collective-permute-start.1 = (bf16[2,2,4096]{2,1,0:T(2,128)(2,1)S(1)}, bf16[2,2,4096]{2,1,0:T(2,128)(2,1)S(1)}, u32[]{:S(2)}, u32[]{:S(2)}) collective-permute-start(bf16[2,2,4096]{2,1,0:T(2,128)(2,1)S(1)} %pad_maximum_fusion.8), channel_id=1, source_target_pairs={{0,4},{1,5},{2,6},{3,7},{4,0},{5,1},{6,2},{7,3},{8,12},{9,13},{10,... | collective-permute-start | bytes 98312 | tf_op jit(solution)/shard_map/ppermute | solution.py:96
  4.4 1.5 %collective-permute-start = (bf16[2,2,4096]{2,1,0:T(2,128)(2,1)S(1)}, bf16[2,2,4096]{2,1,0:T(2,128)(2,1)S(1)}, u32[]{:S(2)}, u32[]{:S(2)}) collective-permute-start(bf16[2,2,4096]{2,1,0:T(2,128)(2,1)S(1)} %pad_maximum_fusion.8), channel_id=1, source_target_pairs={{0,2},{1,3},{2,0},{3,1},{4,6},{5,7},{6,4},{7,5},{8,10},{9,11},{10,... | collective-permute-start | bytes 98312 | tf_op jit(solution)/shard_map/ppermute | solution.py:96
  5.9 0.7 constant_dynamic-update-slice_fusion.2
  6.7 0.7 constant_dynamic-update-slice_fusion.1
  7.4 0.7 constant_dynamic-update-slice_fusion
  8.2 1.6 %collective-permute-start.8 = (bf16[2,3072]{1,0:T(2,128)(2,1)S(1)}, bf16[2,3072]{1,0:T(2,128)(2,1)S(1)}, u32[]{:S(2)}, u32[]{:S(2)}) collective-permute-start(bf16[2,3072]{1,0:T(2,128)(2,1)S(1)} %get-tuple-element.21), channel_id=1, source_target_pairs={{0,8},{8,0},{16,24},{24,16},{1,9},{9,1},{17,25},{25,17},{2,10},{10... | collective-permute-start | bytes 36872 | tf_op jit(solution)/shard_map/ppermute | solution.py:106
  9.8 2.5 %collective-permute-start.10 = (bf16[2,3072]{1,0:T(2,128)(2,1)S(1)}, bf16[2,3072]{1,0:T(2,128)(2,1)S(1)}, u32[]{:S(2)}, u32[]{:S(2)}) collective-permute-start(bf16[2,3072]{1,0:T(2,128)(2,1)S(1)} %get-tuple-element.22), channel_id=1, source_target_pairs={{0,24},{8,16},{16,8},{24,0},{1,25},{9,17},{17,9},{25,1},{2,26},{10... | collective-permute-start | bytes 36872 | tf_op jit(solution)/shard_map/ppermute | solution.py:106
  12.4 0.9 %fusion.12 = bf16[1,2,2,4096]{3,2,1,0:T(2,128)(2,1)S(1)} fusion(bf16[1,2,4096]{2,1,0:T(2,128)(2,1)} %bitcast.41, bf16[1,2,4096]{2,1,0:T(2,128)(2,1)} %bitcast.32), kind=kLoop, calls=%fused_computation.46 | loop fusion | flops 16384 | bytes 65536 | tf_op jit(solution)/shard_map/stack | solution.py:95
  13.6 0.5 collective-permute-start.2
  14.2 1.2 %collective-permute-done.10 = bf16[2,3072]{1,0:T(2,128)(2,1)S(1)} collective-permute-done((bf16[2,3072]{1,0:T(2,128)(2,1)S(1)}, bf16[2,3072]{1,0:T(2,128)(2,1)S(1)}, u32[]{:S(2)}, u32[]{:S(2)}) %collective-permute-start.10) | collective-permute-done | bytes 12320 | tf_op jit(solution)/shard_map/ppermute | solution.py:106
  15.3 1.6 %collective-permute-done.9 = bf16[2,3072]{1,0:T(2,128)(2,1)S(1)} collective-permute-done((bf16[2,3072]{1,0:T(2,128)(2,1)S(1)}, bf16[2,3072]{1,0:T(2,128)(2,1)S(1)}, u32[]{:S(2)}, u32[]{:S(2)}) %collective-permute-start.9) | collective-permute-done | bytes 12320 | tf_op jit(solution)/shard_map/ppermute | solution.py:106
  17.1 0.6 collective-permute-start.12
  17.6 0.5 collective-permute-start.11
  18.2 2.4 %collective-permute-start.13 = (bf16[3,2,3072]{2,1,0:T(2,128)(2,1)S(1)}, bf16[3,2,3072]{2,1,0:T(2,128)(2,1)S(1)}, u32[]{:S(2)}, u32[]{:S(2)}) collective-permute-start(bf16[3,2,3072]{2,1,0:T(2,128)(2,1)S(1)} %pad_maximum_fusion.7), channel_id=1, source_target_pairs={{0,6},{1,7},{2,4},{3,5},{4,2},{5,3},{6,0},{7,1},{8,14},{9,15},{10,... | collective-permute-start | bytes 110600 | tf_op jit(solution)/shard_map/ppermute | solution.py:108
  21.6 1.4 %collective-permute-done.13 = bf16[3,2,3072]{2,1,0:T(2,128)(2,1)S(1)} collective-permute-done((bf16[3,2,3072]{2,1,0:T(2,128)(2,1)S(1)}, bf16[3,2,3072]{2,1,0:T(2,128)(2,1)S(1)}, u32[]{:S(2)}, u32[]{:S(2)}) %collective-permute-start.13) | collective-permute-done | bytes 36896 | tf_op jit(solution)/shard_map/ppermute | solution.py:108
  24.7 5.2 %copy-done = bf16[4096,1792]{1,0:T(8,128)(2,1)S(1)} copy-done((bf16[4096,1792]{1,0:T(8,128)(2,1)S(1)}, bf16[4096,1792]{1,0:T(8,128)(2,1)}, u32[]{:S(2)}) %copy-start) | copy-done | bytes 14680088
  29.9 5.2 %copy-done.1 = bf16[4096,1792]{1,0:T(8,128)(2,1)S(1)} copy-done((bf16[4096,1792]{1,0:T(8,128)(2,1)S(1)}, bf16[4096,1792]{1,0:T(8,128)(2,1)}, u32[]{:S(2)}) %copy-start.1) | copy-done | bytes 14680088
  35.0 5.2 %copy-done.3 = bf16[1792,4096]{1,0:T(8,128)(2,1)S(1)} copy-done((bf16[1792,4096]{1,0:T(8,128)(2,1)S(1)}, bf16[1792,4096]{1,0:T(8,128)(2,1)}, u32[]{:S(2)}) %copy-start.3) | copy-done | bytes 14680088
  40.2 7.7 %forward.1.refs_0_ = bf16[3,16,1792]{2,1,0:T(8,128)(2,1)S(1)} custom-call(bf16[2,16,4096]{2,1,0:T(8,128)(2,1)S(1)} %reshape.14.refs_0_, bf16[4096,1792]{1,0:T(8,128)(2,1)S(1)} %copy-done, bf16[4096,1792]{1,0:T(8,128)(2,1)S(1)} %copy-done.1, bf16[1792,4096]{1,0:T(8,128)(2,1)S(1)} %copy-done.3), custom_call_target="tpu_custom_call" | custom-call | flops 704643072 | bytes 44040192 | tf_op jit(solution)/shard_map/forward/pallas_call | solution.py:115
  47.9 5.2 %copy-done.2 = bf16[4096,1792]{1,0:T(8,128)(2,1)S(1)} copy-done((bf16[4096,1792]{1,0:T(8,128)(2,1)S(1)}, bf16[4096,1792]{1,0:T(8,128)(2,1)}, u32[]{:S(2)}) %copy-start.2) | copy-done | bytes 14680088
  53.1 7.8 %backward.1 = (f32[8,4096]{1,0:T(8,128)S(1)}, bf16[8,4096]{1,0:T(8,128)(2,1)S(1)}) custom-call(bf16[3,16,1792]{2,1,0:T(8,128)(2,1)S(1)} %forward.1.refs_0_, bf16[4096,1792]{1,0:T(8,128)(2,1)S(1)} %bitcast.30, bf16[4096,1792]{1,0:T(8,128)(2,1)S(1)} %copy-done.2), custom_call_target="tpu_custom_call" | custom-call | flops 469762048 | bytes 29360128 | tf_op jit(solution)/shard_map/backward/pallas_call | solution.py:143
  60.9 0.5 collective-permute-start.4
  61.5 1.1 %collective-permute-start.15 = (bf16[2,16,1792]{2,1,0:T(8,128)(2,1)S(1)}, bf16[2,16,1792]{2,1,0:T(8,128)(2,1)S(1)}, u32[]{:S(2)}, u32[]{:S(2)}) collective-permute-start(bf16[2,16,1792]{2,1,0:T(8,128)(2,1)S(1)} %pad_maximum_fusion.4), channel_id=1, source_target_pairs={{0,8},{8,0},{16,24},{24,16},{1,9},{9,1},{17,25},{25,17},{2,10},{10... | collective-permute-start | bytes 344072 | tf_op jit(solution)/shard_map/ppermute | solution.py:139
  62.6 1.8 %collective-permute-start.16 = (bf16[2,16,1792]{2,1,0:T(8,128)(2,1)S(1)}, bf16[2,16,1792]{2,1,0:T(8,128)(2,1)S(1)}, u32[]{:S(2)}, u32[]{:S(2)}) collective-permute-start(bf16[2,16,1792]{2,1,0:T(8,128)(2,1)S(1)} %pad_maximum_fusion.5), channel_id=1, source_target_pairs={{0,16},{8,24},{16,0},{24,8},{1,17},{9,25},{17,1},{25,9},{2,18},{10... | collective-permute-start | bytes 344072 | tf_op jit(solution)/shard_map/ppermute | solution.py:139
  65.5 0.8 collective-permute-start.5
  66.2 1.5 %collective-permute-start.7 = (bf16[2,4096]{1,0:T(2,128)(2,1)S(1)}, bf16[2,4096]{1,0:T(2,128)(2,1)S(1)}, u32[]{:S(2)}, u32[]{:S(2)}) collective-permute-start(bf16[2,4096]{1,0:T(2,128)(2,1)S(1)} %get-tuple-element.19), channel_id=1, source_target_pairs={{0,6},{1,7},{2,4},{3,5},{4,2},{5,3},{6,0},{7,1},{8,14},{9,15},{10,... | collective-permute-start | bytes 49160 | tf_op jit(solution)/shard_map/ppermute | solution.py:162
  67.7 1.3 %collective-permute-start.6 = (bf16[2,4096]{1,0:T(2,128)(2,1)S(1)}, bf16[2,4096]{1,0:T(2,128)(2,1)S(1)}, u32[]{:S(2)}, u32[]{:S(2)}) collective-permute-start(bf16[2,4096]{1,0:T(2,128)(2,1)S(1)} %get-tuple-element.20), channel_id=1, source_target_pairs={{0,4},{1,5},{2,6},{3,7},{4,0},{5,1},{6,2},{7,3},{8,12},{9,13},{10,... | collective-permute-start | bytes 49160 | tf_op jit(solution)/shard_map/ppermute | solution.py:162
  69.3 1.6 %collective-permute-start.17 = (bf16[2,16,1792]{2,1,0:T(8,128)(2,1)S(1)}, bf16[2,16,1792]{2,1,0:T(8,128)(2,1)S(1)}, u32[]{:S(2)}, u32[]{:S(2)}) collective-permute-start(bf16[2,16,1792]{2,1,0:T(8,128)(2,1)S(1)} %pad_maximum_fusion.6), channel_id=1, source_target_pairs={{0,24},{8,16},{16,8},{24,0},{1,25},{9,17},{17,9},{25,1},{2,26},{10... | collective-permute-start | bytes 344072 | tf_op jit(solution)/shard_map/ppermute | solution.py:139
  71.5 0.6 fusion.4
  72.1 3.9 %collective-permute-done.17 = bf16[2,16,1792]{2,1,0:T(8,128)(2,1)S(1)} collective-permute-done((bf16[2,16,1792]{2,1,0:T(8,128)(2,1)S(1)}, bf16[2,16,1792]{2,1,0:T(8,128)(2,1)S(1)}, u32[]{:S(2)}, u32[]{:S(2)}) %collective-permute-start.17) | collective-permute-done | bytes 114720 | tf_op jit(solution)/shard_map/ppermute | solution.py:139
  76.1 11.1 %product.1 = f32[3072,1792]{1,0:T(8,128)} custom-call(s32[12]{0:T(128)S(1)} %fusion.5.row_blocks, bf16[64,3072]{1,0:T(8,128)(2,1)S(1)} %pad_maximum_fusion.1.tokens, bf16[2,64,1792]{2,1,0:T(8,128)(2,1)S(1)} %pad_maximum_fusion.grads), custom_call_target="tpu_custom_call" | custom-call | flops 704643072 | bytes 22020096 | tf_op jit(solution)/shard_map/product/pallas_call | solution.py:171
  (56 shorter events, 4.8 us)
Async XLA Ops:
  1.4 16.8 %collective-permute-start.1 = (bf16[2,2,4096]{2,1,0:T(2,128)(2,1)S(1)}, bf16[2,2,4096]{2,1,0:T(2,128)(2,1)S(1)}, u32[]{:S(2)}, u32[]{:S(2)}) collective-permute-start(bf16[2,2,4096]{2,1,0:T(2,128)(2,1)S(1)} %pad_maximum_fusion.8), channel_id=1, source_target_pairs={{0,4},{1,5},{2,6},{3,7},{4,0},{5,1},{6,2},{7,3},{8,12},{9,13},{10,... | collective-permute-start | bytes 98312 | tf_op jit(solution)/shard_map/ppermute | solution.py:96
  4.4 16.2 %collective-permute-start = (bf16[2,2,4096]{2,1,0:T(2,128)(2,1)S(1)}, bf16[2,2,4096]{2,1,0:T(2,128)(2,1)S(1)}, u32[]{:S(2)}, u32[]{:S(2)}) collective-permute-start(bf16[2,2,4096]{2,1,0:T(2,128)(2,1)S(1)} %pad_maximum_fusion.8), channel_id=1, source_target_pairs={{0,2},{1,3},{2,0},{3,1},{4,6},{5,7},{6,4},{7,5},{8,10},{9,11},{10,... | collective-permute-start | bytes 98312 | tf_op jit(solution)/shard_map/ppermute | solution.py:96
  8.2 5.4 %collective-permute-start.8 = (bf16[2,3072]{1,0:T(2,128)(2,1)S(1)}, bf16[2,3072]{1,0:T(2,128)(2,1)S(1)}, u32[]{:S(2)}, u32[]{:S(2)}) collective-permute-start(bf16[2,3072]{1,0:T(2,128)(2,1)S(1)} %get-tuple-element.21), channel_id=1, source_target_pairs={{0,8},{8,0},{16,24},{24,16},{1,9},{9,1},{17,25},{25,17},{2,10},{10... | collective-permute-start | bytes 36872 | tf_op jit(solution)/shard_map/ppermute | solution.py:106
  9.8 5.5 %collective-permute-start.10 = (bf16[2,3072]{1,0:T(2,128)(2,1)S(1)}, bf16[2,3072]{1,0:T(2,128)(2,1)S(1)}, u32[]{:S(2)}, u32[]{:S(2)}) collective-permute-start(bf16[2,3072]{1,0:T(2,128)(2,1)S(1)} %get-tuple-element.22), channel_id=1, source_target_pairs={{0,24},{8,16},{16,8},{24,0},{1,25},{9,17},{17,9},{25,1},{2,26},{10... | collective-permute-start | bytes 36872 | tf_op jit(solution)/shard_map/ppermute | solution.py:106
  12.3 4.6 %collective-permute-start.9 = (bf16[2,3072]{1,0:T(2,128)(2,1)S(1)}, bf16[2,3072]{1,0:T(2,128)(2,1)S(1)}, u32[]{:S(2)}, u32[]{:S(2)}) collective-permute-start(bf16[2,3072]{1,0:T(2,128)(2,1)S(1)} %get-tuple-element.23), channel_id=1, source_target_pairs={{0,16},{8,24},{16,0},{24,8},{1,17},{9,25},{17,1},{25,9},{2,18},{10... | collective-permute-start | bytes 36872 | tf_op jit(solution)/shard_map/ppermute | solution.py:106
  12.4 35.4 %slice-start = ((s8[14680064]{0:T(1024)(128)(4,1)}), s8[2097152]{0:T(1024)(128)(4,1)S(1)}, s32[]{:S(2)}) async-start(s8[14680064]{0:T(1024)(128)(4,1)} %bitcast.29), calls=%async_computation | async-start | bytes 4194304
  13.6 7.0 %collective-permute-start.2 = (bf16[2,2,4096]{2,1,0:T(2,128)(2,1)S(1)}, bf16[2,2,4096]{2,1,0:T(2,128)(2,1)S(1)}, u32[]{:S(2)}, u32[]{:S(2)}) collective-permute-start(bf16[2,2,4096]{2,1,0:T(2,128)(2,1)S(1)} %pad_maximum_fusion.8), channel_id=1, source_target_pairs={{0,6},{1,7},{2,4},{3,5},{4,2},{5,3},{6,0},{7,1},{8,14},{9,15},{10,... | collective-permute-start | bytes 98312 | tf_op jit(solution)/shard_map/ppermute | solution.py:96
  17.1 4.1 %collective-permute-start.12 = (bf16[3,2,3072]{2,1,0:T(2,128)(2,1)S(1)}, bf16[3,2,3072]{2,1,0:T(2,128)(2,1)S(1)}, u32[]{:S(2)}, u32[]{:S(2)}) collective-permute-start(bf16[3,2,3072]{2,1,0:T(2,128)(2,1)S(1)} %pad_maximum_fusion.7), channel_id=1, source_target_pairs={{0,4},{1,5},{2,6},{3,7},{4,0},{5,1},{6,2},{7,3},{8,12},{9,13},{10,... | collective-permute-start | bytes 110600 | tf_op jit(solution)/shard_map/ppermute | solution.py:108
  17.6 4.0 %collective-permute-start.11 = (bf16[3,2,3072]{2,1,0:T(2,128)(2,1)S(1)}, bf16[3,2,3072]{2,1,0:T(2,128)(2,1)S(1)}, u32[]{:S(2)}, u32[]{:S(2)}) collective-permute-start(bf16[3,2,3072]{2,1,0:T(2,128)(2,1)S(1)} %pad_maximum_fusion.7), channel_id=1, source_target_pairs={{0,2},{1,3},{2,0},{3,1},{4,6},{5,7},{6,4},{7,5},{8,10},{9,11},{10,... | collective-permute-start | bytes 110600 | tf_op jit(solution)/shard_map/ppermute | solution.py:108
  18.2 4.9 %collective-permute-start.13 = (bf16[3,2,3072]{2,1,0:T(2,128)(2,1)S(1)}, bf16[3,2,3072]{2,1,0:T(2,128)(2,1)S(1)}, u32[]{:S(2)}, u32[]{:S(2)}) collective-permute-start(bf16[3,2,3072]{2,1,0:T(2,128)(2,1)S(1)} %pad_maximum_fusion.7), channel_id=1, source_target_pairs={{0,6},{1,7},{2,4},{3,5},{4,2},{5,3},{6,0},{7,1},{8,14},{9,15},{10,... | collective-permute-start | bytes 110600 | tf_op jit(solution)/shard_map/ppermute | solution.py:108
  21.1 2.5 %collective-permute-start.3 = (bf16[4,2,2,4096]{3,2,1,0:T(2,128)(2,1)S(1)}, bf16[4,2,2,4096]{3,2,1,0:T(2,128)(2,1)S(1)}, u32[]{:S(2)}, u32[]{:S(2)}) collective-permute-start(bf16[4,2,2,4096]{3,2,1,0:T(2,128)(2,1)S(1)} %pad_maximum_fusion.3), channel_id=1, source_target_pairs={{0,1},{1,0},{2,3},{3,2},{4,5},{5,4},{6,7},{7,6},{8,9},{9,8},{10,11... | collective-permute-start | bytes 393224 | tf_op jit(solution)/shard_map/ppermute | solution.py:98
  23.6 41.0 %collective-permute-start.14 = (bf16[4,3,2,3072]{3,2,1,0:T(2,128)(2,1)S(1)}, bf16[4,3,2,3072]{3,2,1,0:T(2,128)(2,1)S(1)}, u32[]{:S(2)}, u32[]{:S(2)}) collective-permute-start(bf16[4,3,2,3072]{3,2,1,0:T(2,128)(2,1)S(1)} %pad_maximum_fusion.2), channel_id=1, source_target_pairs={{0,1},{1,0},{2,3},{3,2},{4,5},{5,4},{6,7},{7,6},{8,9},{9,8},{10,11... | collective-permute-start | bytes 442376 | tf_op jit(solution)/shard_map/ppermute | solution.py:109
  24.7 5.2 %copy-start = (bf16[4096,1792]{1,0:T(8,128)(2,1)S(1)}, bf16[4096,1792]{1,0:T(8,128)(2,1)}, u32[]{:S(2)}) copy-start(bf16[4096,1792]{1,0:T(8,128)(2,1)} %refs_1_.3) | copy-start | bytes 44040196
  29.9 5.2 %copy-start.1 = (bf16[4096,1792]{1,0:T(8,128)(2,1)S(1)}, bf16[4096,1792]{1,0:T(8,128)(2,1)}, u32[]{:S(2)}) copy-start(bf16[4096,1792]{1,0:T(8,128)(2,1)} %refs_2_.3) | copy-start | bytes 44040196
  35.0 5.2 %copy-start.3 = (bf16[1792,4096]{1,0:T(8,128)(2,1)S(1)}, bf16[1792,4096]{1,0:T(8,128)(2,1)}, u32[]{:S(2)}) copy-start(bf16[1792,4096]{1,0:T(8,128)(2,1)} %refs_3_.1) | copy-start | bytes 44040196
  40.2 7.7 %slice-start.1 = ((s8[14680064]{0:T(1024)(128)(4,1)}), s8[4194304]{0:T(1024)(128)(4,1)S(1)}, s32[]{:S(2)}) async-start(s8[14680064]{0:T(1024)(128)(4,1)} %bitcast.29), calls=%async_computation.1 | async-start | bytes 8388608
  40.2 7.7 %slice-start.2 = ((s8[14680064]{0:T(1024)(128)(4,1)}), s8[4194304]{0:T(1024)(128)(4,1)S(1)}, s32[]{:S(2)}) async-start(s8[14680064]{0:T(1024)(128)(4,1)} %bitcast.29), calls=%async_computation.2 | async-start | bytes 8388608
  40.2 7.7 %slice-start.3 = ((s8[14680064]{0:T(1024)(128)(4,1)}), s8[4194304]{0:T(1024)(128)(4,1)S(1)}, s32[]{:S(2)}) async-start(s8[14680064]{0:T(1024)(128)(4,1)} %bitcast.29), calls=%async_computation.3 | async-start | bytes 8388608
  47.9 5.2 %copy-start.2 = (bf16[4096,1792]{1,0:T(8,128)(2,1)S(1)}, bf16[4096,1792]{1,0:T(8,128)(2,1)}, u32[]{:S(2)}) copy-start(bf16[4096,1792]{1,0:T(8,128)(2,1)} %refs_2_.3) | copy-start | bytes 44040196
  60.9 4.5 %collective-permute-start.4 = (bf16[8,4096]{1,0:T(8,128)(2,1)S(1)}, bf16[8,4096]{1,0:T(8,128)(2,1)S(1)}, u32[]{:S(2)}, u32[]{:S(2)}) collective-permute-start(bf16[8,4096]{1,0:T(8,128)(2,1)S(1)} %get-tuple-element.5), channel_id=1, source_target_pairs={{0,1},{1,0},{2,3},{3,2},{4,5},{5,4},{6,7},{7,6},{8,9},{9,8},{10,11... | collective-permute-start | bytes 196616 | tf_op jit(solution)/shard_map/ppermute | solution.py:158
  61.5 10.6 %collective-permute-start.15 = (bf16[2,16,1792]{2,1,0:T(8,128)(2,1)S(1)}, bf16[2,16,1792]{2,1,0:T(8,128)(2,1)S(1)}, u32[]{:S(2)}, u32[]{:S(2)}) collective-permute-start(bf16[2,16,1792]{2,1,0:T(8,128)(2,1)S(1)} %pad_maximum_fusion.4), channel_id=1, source_target_pairs={{0,8},{8,0},{16,24},{24,16},{1,9},{9,1},{17,25},{25,17},{2,10},{10... | collective-permute-start | bytes 344072 | tf_op jit(solution)/shard_map/ppermute | solution.py:139
  62.6 9.6 %collective-permute-start.16 = (bf16[2,16,1792]{2,1,0:T(8,128)(2,1)S(1)}, bf16[2,16,1792]{2,1,0:T(8,128)(2,1)S(1)}, u32[]{:S(2)}, u32[]{:S(2)}) collective-permute-start(bf16[2,16,1792]{2,1,0:T(8,128)(2,1)S(1)} %pad_maximum_fusion.5), channel_id=1, source_target_pairs={{0,16},{8,24},{16,0},{24,8},{1,17},{9,25},{17,1},{25,9},{2,18},{10... | collective-permute-start | bytes 344072 | tf_op jit(solution)/shard_map/ppermute | solution.py:139
  65.5 3.9 %collective-permute-start.5 = (bf16[2,4096]{1,0:T(2,128)(2,1)S(1)}, bf16[2,4096]{1,0:T(2,128)(2,1)S(1)}, u32[]{:S(2)}, u32[]{:S(2)}) collective-permute-start(bf16[2,4096]{1,0:T(2,128)(2,1)S(1)} %get-tuple-element.18), channel_id=1, source_target_pairs={{0,2},{1,3},{2,0},{3,1},{4,6},{5,7},{6,4},{7,5},{8,10},{9,11},{10,... | collective-permute-start | bytes 49160 | tf_op jit(solution)/shard_map/ppermute | solution.py:162
  66.2 4.7 %collective-permute-start.7 = (bf16[2,4096]{1,0:T(2,128)(2,1)S(1)}, bf16[2,4096]{1,0:T(2,128)(2,1)S(1)}, u32[]{:S(2)}, u32[]{:S(2)}) collective-permute-start(bf16[2,4096]{1,0:T(2,128)(2,1)S(1)} %get-tuple-element.19), channel_id=1, source_target_pairs={{0,6},{1,7},{2,4},{3,5},{4,2},{5,3},{6,0},{7,1},{8,14},{9,15},{10,... | collective-permute-start | bytes 49160 | tf_op jit(solution)/shard_map/ppermute | solution.py:162
  67.7 3.7 %collective-permute-start.6 = (bf16[2,4096]{1,0:T(2,128)(2,1)S(1)}, bf16[2,4096]{1,0:T(2,128)(2,1)S(1)}, u32[]{:S(2)}, u32[]{:S(2)}) collective-permute-start(bf16[2,4096]{1,0:T(2,128)(2,1)S(1)} %get-tuple-element.20), channel_id=1, source_target_pairs={{0,4},{1,5},{2,6},{3,7},{4,0},{5,1},{6,2},{7,3},{8,12},{9,13},{10,... | collective-permute-start | bytes 49160 | tf_op jit(solution)/shard_map/ppermute | solution.py:162
  69.3 6.7 %collective-permute-start.17 = (bf16[2,16,1792]{2,1,0:T(8,128)(2,1)S(1)}, bf16[2,16,1792]{2,1,0:T(8,128)(2,1)S(1)}, u32[]{:S(2)}, u32[]{:S(2)}) collective-permute-start(bf16[2,16,1792]{2,1,0:T(8,128)(2,1)S(1)} %pad_maximum_fusion.6), channel_id=1, source_target_pairs={{0,24},{8,16},{16,8},{24,0},{1,25},{9,17},{17,9},{25,1},{2,26},{10... | collective-permute-start | bytes 344072 | tf_op jit(solution)/shard_map/ppermute | solution.py:139

commit v2 on v1

v2 whole, which is shorter than its diff:
```python
import jax
import jax.numpy as jnp
from jax import lax
from jax.experimental import pallas as pl
from jax.experimental.pallas import tpu as pltpu
from jax.sharding import PartitionSpec as P

BF = jnp.bfloat16
F32 = jnp.float32
NN = (((1,), (0,)), ((), ()))
NT = (((1,), (1,)), ((), ()))
TN = (((0,), (0,)), ((), ()))
ANY_SPEC = pl.BlockSpec(memory_space=pl.ANY)
HBM_SPEC = pl.BlockSpec(memory_space=pltpu.HBM)
VMEM_SPEC = pl.BlockSpec(memory_space=pltpu.VMEM)


def dot(left, right, dims):
    return lax.dot_general(left, right, dims, preferred_element_type=F32)


def in_hbm(array):
    return pltpu.with_memory_space_constraint(array, pltpu.HBM)


def in_vmem(array):
    return pltpu.with_memory_space_constraint(array, pltpu.VMEM)


def xor_pairs(count, step):
    return [(i, i ^ step) for i in range(count)]


def shards_any(n_dp, normed, cotangent, gate_weight, up_weight, down_weight):
    rows = lax.all_gather(normed, "node", axis=0, tiled=True)
    cots = lax.all_gather(cotangent, "node", axis=0, tiled=True)
    gate_pre = dot(rows, gate_weight, NN)
    up_pre = dot(rows, up_weight, NN)
    sigma = jax.nn.sigmoid(gate_pre)
    activated = gate_pre * sigma
    hidden = (activated * up_pre).astype(BF)
    grad_hidden = dot(cots, down_weight, NT)
    grad_gate = (grad_hidden * up_pre * sigma * (1.0 + gate_pre * (1.0 - sigma))).astype(BF)
    grad_up = (grad_hidden * activated).astype(BF)
    grad_normed = lax.psum_scatter(
        dot(grad_gate, gate_weight, NT) + dot(grad_up, up_weight, NT),
        "node",
        scatter_dimension=0,
        tiled=True,
    ).astype(BF)
    stacked = jnp.concatenate(
        [dot(rows, grad_gate, TN), dot(rows, grad_up, TN), dot(cots, hidden, TN)], axis=0
    )
    weight_grads = lax.psum_scatter(
        stacked.astype(BF), "dp", scatter_dimension=0, tiled=True
    ).astype(F32)
    return grad_normed, weight_grads


def far_kernel(n_dp, normed, cotangent, *far):
    unit = normed.shape[1] // n_dp
    for step, out in enumerate(far, 1):
        owner = lax.axis_index("dp") ^ step
        for j in range(3):
            index = 3 * owner + j
            columns = pl.ds(pl.multiple_of(lax.rem(index, n_dp) * unit, unit), unit)
            out[:, j * unit : (j + 1) * unit] = jnp.where(
                index >= 2 * n_dp, cotangent[:, columns], normed[:, columns]
            )


def load_kernel(first, weight, after, out, token, sem):
    copy = pltpu.make_async_copy(weight.at[pl.ds(first, out.shape[0])], out, sem)
    copy.start()
    token[...] = jnp.zeros(token.shape, token.dtype)
    copy.wait()


def load_rows(weight, first, count, after, name):
    return pl.pallas_call(
        lambda *refs: load_kernel(first, *refs),
        out_shape=(
            pltpu.VMEM((count, weight.shape[1]), weight.dtype),
            jax.ShapeDtypeStruct((8, 128), F32),
        ),
        in_specs=[HBM_SPEC, ANY_SPEC],
        out_specs=(VMEM_SPEC, VMEM_SPEC),
        scratch_shapes=[pltpu.SemaphoreType.DMA],
        compiler_params=pltpu.CompilerParams(vmem_limit_bytes=1 << 20),
        cost_estimate=pl.CostEstimate(
            flops=0, bytes_accessed=2 * count * weight.shape[1], transcendentals=0
        ),
        name=name,
    )(weight, after)


def join_kernel(*refs):
    *pieces, after, out = refs
    start = 0
    for piece in pieces:
        out[:, start : start + piece.shape[1]] = piece[...]
        start += piece.shape[1]


def stack_kernel(*refs):
    *pieces, after, out = refs
    for slot, piece in enumerate(pieces):
        out[slot] = piece[...]


def glue(kernel, shape, pieces, after, name):
    return pl.pallas_call(
        kernel,
        out_shape=jax.ShapeDtypeStruct(shape, BF),
        in_specs=[VMEM_SPEC] * len(pieces) + [ANY_SPEC],
        out_specs=VMEM_SPEC,
        compiler_params=pltpu.CompilerParams(vmem_limit_bytes=4 << 20),
        cost_estimate=pl.CostEstimate(flops=0, bytes_accessed=1 << 18, transcendentals=0),
        name=name,
    )(*pieces, after)


def arrange_kernel(plane, other, after, tokens, far, wide):
    own = plane.shape[1]
    group, width = tokens.shape[1:]
    block = far.shape[1]
    for slot in range(plane.shape[0]):
        for half, source in enumerate((plane, other)):
            start = (half * plane.shape[0] + slot) * own
            wide[start : start + own] = source[slot].astype(F32)
    for i in range(2):
        tokens[i] = wide[:, i * width : (i + 1) * width].astype(BF)
    for i in range(far.shape[0] // group):
        start = 2 * width + i * block
        far[i * group : (i + 1) * group] = wide[:, start : start + block].astype(BF)


def forward_kernel(n_dp, chunk, tokens, gate_a, gate_b, up_a, up, down, *refs):
    *packs, grads_out, up_b, _, _, _, gate_pre, up_pre, grads, down_rows, up_sem, down_sem = refs
    half = gate_a.shape[0]
    columns = gate_a.shape[1]
    up_copy = pltpu.make_async_copy(up.at[pl.ds(half, half)], up_b, up_sem)
    up_copy.start()
    parts = [slice(start, start + chunk) for start in range(0, columns, chunk)]
    down_copies = [
        pltpu.make_async_copy(
            down.at[pl.ds(part.start, chunk)], down_rows.at[pl.ds(part.start, chunk)], down_sem.at[i]
        )
        for i, part in enumerate(parts)
    ]
    for copy in down_copies:
        copy.start()
    for part in parts:
        gate_pre[:, part] = dot(tokens[0, :, :half], gate_a[:, part], NN) + dot(
            tokens[0, :, half:], gate_b[:, part], NN
        )
        up_pre[:, part] = dot(tokens[0, :, :half], up_a[:, part], NN)
    up_copy.wait()
    for part in parts:
        up_pre[:, part] += dot(tokens[0, :, half:], up_b[:, part], NN)
    for part, copy in zip(parts, down_copies):
        copy.wait()
        grad_hidden = dot(tokens[1], down_rows[part, :], NT)
        gate_part = gate_pre[:, part]
        up_part = up_pre[:, part]
        sigma = jax.nn.sigmoid(gate_part)
        activated = gate_part * sigma
        grads[0, :, part] = (
            grad_hidden * up_part * sigma * (1.0 + gate_part * (1.0 - sigma))
        ).astype(BF)
        grads[1, :, part] = (grad_hidden * activated).astype(BF)
        grads[2, :, part] = (activated * up_part).astype(BF)
    grads_out[...] = grads[:2]
    for step, pack in enumerate(packs):
        owner = lax.axis_index("dp") ^ step
        pack[0] = grads[lax.div(3 * owner, n_dp)]
        pack[1] = grads[lax.div(3 * owner + 2, n_dp)]


def backward_kernel(chunk, grads, gate_a, gate_b, up_a, up_b, keep, send):
    half = gate_a.shape[0]
    rows = keep.shape[0]
    for gate, up, base in ((gate_a, up_a, 0), (gate_b, up_b, half)):
        for start in range(0, half, chunk):
            part = slice(start, start + chunk)
            total = dot(grads[0], gate[part, :], NT) + dot(grads[1], up[part, :], NT)
            keep[:, base + start : base + start + chunk] = total[:rows]
            send[:, base + start : base + start + chunk] = total[rows:].astype(BF)


def product_kernel(n_dp, pieces, tokens, far, *refs):
    *packs, out, token, columns, grads, result, sem = refs
    group = tokens.shape[1]
    unit = tokens.shape[2] // n_dp
    d = lax.axis_index("dp")
    token[...] = jnp.zeros(token.shape, token.dtype)
    for slot, pack in enumerate(packs):
        for m in range(2):
            grads[m, slot * group : (slot + 1) * group] = pack[m]
    for j in range(3):
        index = 3 * d + j
        source = pl.ds(pl.multiple_of(lax.rem(index, n_dp) * unit, unit), unit)
        part = slice(j * unit, (j + 1) * unit)
        columns[:group, part] = jnp.where(
            index >= 2 * n_dp, tokens[1, :, source], tokens[0, :, source]
        )
    columns[group:] = far[...]
    copies = []
    for i, (start, count) in enumerate(pieces):
        j = start // unit
        which = lax.div(3 * d + j, n_dp) - lax.div(3 * d, n_dp)
        part = slice(start, start + count)
        result[part] = dot(columns[:, part], grads[which], TN)
        copy = pltpu.make_async_copy(
            result.at[pl.ds(start, count)], out.at[pl.ds(start, count)], sem.at[i]
        )
        copy.start()
        copies.append(copy)
    for copy in copies:
        copy.wait()


def hold_kernel(piece, *refs):
    refs[-1][...] = piece[...]


def final_kernel(own, chip, first, second, third, after, out):
    total = chip[:own]
    for piece in (first, second, third):
        total = total + piece[...].astype(F32)
    out[...] = total.astype(BF)


def shards_group(mesh_shape, normed, cotangent, gate_weight, up_weight, down_weight):
    n_dp, n_node = mesh_shape
    own, width = normed.shape
    hidden = gate_weight.shape[1]
    group = own * n_node
    block = 3 * width // n_dp
    half = width // 2
    chips = range(2, n_node, 2)
    groups = range(1, n_dp)
    weight_bytes = 2 * width * hidden

    def permute(array, axis, step):
        return lax.ppermute(array, axis, xor_pairs(mesh_shape[axis == "node"], step))

    far = pl.pallas_call(
        lambda *refs: far_kernel(n_dp, *refs),
        out_shape=[jax.ShapeDtypeStruct((own, block), BF) for s in groups],
        in_specs=[VMEM_SPEC] * 2,
        out_specs=[VMEM_SPEC] * len(groups),
        compiler_params=pltpu.CompilerParams(vmem_limit_bytes=1 << 20),
        name="far_columns",
    )(normed, cotangent)
    far = [permute(piece, "dp", s) for s, piece in zip(groups, far)]
    gate_hbm, up_hbm, down_hbm = (in_hbm(w) for w in (gate_weight, up_weight, down_weight))
    gate_a, token = load_rows(gate_hbm, 0, half, normed, "load_gate_a")
    tall = 2 * width + len(groups) * block
    mine = glue(join_kernel, (own, tall), [normed, cotangent, *far], token, "join")
    plane = [mine] + [permute(mine, "node", s) for s in chips]
    gate_b, token = load_rows(gate_hbm, half, half, token, "load_gate_b")
    plane = glue(stack_kernel, (len(plane), own, tall), plane, token, "stack")
    other = permute(plane, "node", 1)
    up_a, token = load_rows(up_hbm, 0, half, token, "load_up_a")
    tokens, far = pl.pallas_call(
        arrange_kernel,
        out_shape=(
            jax.ShapeDtypeStruct((2, group, width), BF),
            jax.ShapeDtypeStruct(((n_dp - 1) * group, block), BF),
        ),
        in_specs=[VMEM_SPEC] * 2 + [ANY_SPEC],
        out_specs=(VMEM_SPEC, VMEM_SPEC),
        scratch_shapes=[pltpu.VMEM((group, tall), F32)],
        compiler_params=pltpu.CompilerParams(vmem_limit_bytes=4 << 20),
        cost_estimate=pl.CostEstimate(flops=0, bytes_accessed=1 << 20, transcendentals=0),
        name="arrange",
    )(plane, other, token)

    pack = jax.ShapeDtypeStruct((2, group, hidden), BF)
    chunk = 256
    *packs, grads, up_b, gate_a, gate_b, up_a = pl.pallas_call(
        lambda *refs: forward_kernel(n_dp, chunk, *refs),
        out_shape=[pack] * (n_dp + 1) + [pltpu.VMEM((half, hidden), BF)] * 4,
        in_specs=[VMEM_SPEC] * 4 + [HBM_SPEC] * 2,
        out_specs=[VMEM_SPEC] * (n_dp + 5),
        input_output_aliases={1: n_dp + 2, 2: n_dp + 3, 3: n_dp + 4},
        scratch_shapes=[
            pltpu.VMEM((group, hidden), F32),
            pltpu.VMEM((group, hidden), F32),
            pltpu.VMEM((3, group, hidden), BF),
            pltpu.VMEM((hidden, width), BF),
            pltpu.SemaphoreType.DMA,
            pltpu.SemaphoreType.DMA((hidden // chunk,)),
        ],
        compiler_params=pltpu.CompilerParams(vmem_limit_bytes=20 << 20),
        cost_estimate=pl.CostEstimate(
            flops=6 * group * width * hidden, bytes_accessed=2 * weight_bytes, transcendentals=0
        ),
        name="forward",
    )(tokens, in_vmem(gate_a), in_vmem(gate_b), in_vmem(up_a), up_hbm, down_hbm)

    packs = [packs[0]] + [permute(packs[s], "dp", s) for s in groups]

    keep, send = pl.pallas_call(
        lambda *refs: backward_kernel(chunk, *refs),
        out_shape=(
            jax.ShapeDtypeStruct((group // 2, width), F32),
            jax.ShapeDtypeStruct((group // 2, width), BF),
        ),
        in_specs=[VMEM_SPEC] * 5,
        out_specs=(VMEM_SPEC, VMEM_SPEC),
        compiler_params=pltpu.CompilerParams(vmem_limit_bytes=4 << 20),
        cost_estimate=pl.CostEstimate(
            flops=4 * group * width * hidden, bytes_accessed=2 * weight_bytes, transcendentals=0
        ),
        name="backward",
    )(grads, in_vmem(gate_a), in_vmem(gate_b), in_vmem(up_a), in_vmem(up_b))

    send = pl.pallas_call(
        hold_kernel,
        out_shape=jax.ShapeDtypeStruct(send.shape, BF),
        in_specs=[VMEM_SPEC] + [ANY_SPEC] * (n_dp - 1),
        out_specs=VMEM_SPEC,
        compiler_params=pltpu.CompilerParams(vmem_limit_bytes=1 << 20),
        name="hold",
    )(send, *packs[1:])
    chip = keep + permute(send, "node", 1).astype(F32)
    pieces = [
        permute(chip[own * slot : own * (slot + 1)].astype(BF), "node", s)
        for slot, s in enumerate(chips, 1)
    ]

    cuts = [(start, 256) for start in range(0, block, 256)]
    weight_grads, token = pl.pallas_call(
        lambda *refs: product_kernel(n_dp, cuts, *refs),
        out_shape=(
            pltpu.HBM((block, hidden), F32),
            jax.ShapeDtypeStruct((8, 128), F32),
        ),
        in_specs=[VMEM_SPEC] * (n_dp + 2),
        out_specs=(HBM_SPEC, VMEM_SPEC),
        scratch_shapes=[
            pltpu.VMEM((n_dp * group, block), BF),
            pltpu.VMEM((2, n_dp * group, hidden), BF),
            pltpu.VMEM((block, hidden), F32),
            pltpu.SemaphoreType.DMA((len(cuts),)),
        ],
        compiler_params=pltpu.CompilerParams(vmem_limit_bytes=32 << 20),
        cost_estimate=pl.CostEstimate(
            flops=2 * n_dp * group * block * hidden,
            bytes_accessed=4 * block * hidden,
            transcendentals=0,
        ),
        name="product",
    )(tokens, far, *packs)
    grad_normed = pl.pallas_call(
        lambda *refs: final_kernel(own, *refs),
        out_shape=jax.ShapeDtypeStruct((own, width), BF),
        in_specs=[VMEM_SPEC] * 4 + [ANY_SPEC],
        out_specs=VMEM_SPEC,
        compiler_params=pltpu.CompilerParams(vmem_limit_bytes=2 << 20),
        name="final_sum",
    )(chip, *pieces, token)
    return grad_normed, weight_grads


def solution(mesh):
    n_dp, n_node = mesh.shape["dp"], mesh.shape["node"]

    def shards(*arrays):
        normed, gate_weight = arrays[0], arrays[2]
        rows, width = normed.shape
        hidden = gate_weight.shape[1]
        fits = (
            n_dp == 4
            and n_node == 8
            and rows * n_node == 16
            and hidden % 256 == 0
            and hidden * width * 6 <= 46 << 20
            and width % (n_dp * 256) == 0
        )
        if fits:
            return shards_group((n_dp, n_node), *arrays)
        return shards_any(n_dp, *arrays)

    in_specs = (
        P(("dp", "node"), None),
        P(("dp", "node"), None),
        P(None, "node"),
        P(None, "node"),
        P("node", None),
    )
    out_specs = (P(("dp", "node"), None), P("dp", "node"))
    return jax.shard_map(shards, mesh=mesh, in_specs=in_specs, out_specs=out_specs, check_vma=False)
```

time: 87.8 us -> 69.2 us (0.79)
  local copies, waits for them, and re-layouts: 23.9 us -> 2.2 us
  Pallas kernels: 26.6 us -> 44.7 us
  waiting for transfers between devices: 9.31 us -> 3.57 us
  other arithmetic: 4.65 us -> 0.02 us
  starting transfers between devices: 21.5 us -> 17.4 us
    unnamed x18 -> x10, local copies, waits for them, and re-layouts: 22.2 us -> 2.15 us
    pallas_call x3 -> x12, Pallas kernels: 26.6 us -> 44.7 us  [the longest x1 18.7 us: shards_group(): pl.pallas_call(lambda *refs: forward_kernel(n_dp, chunk, *refs), out_shap...]
    ppermute x18 -> x14, waiting for transfers between devices: 9.31 us -> 3.57 us  [permute(): lax.ppermute(array, axis, xor_pairs(mesh_shape[axis == 'node'], step))]
    ppermute x18 -> x14, starting transfers between devices: 21.5 us -> 17.4 us  [permute(): lax.ppermute(array, axis, xor_pairs(mesh_shape[axis == 'node'], step))]
    another operation x12 -> x1, other arithmetic: 2.89 us -> 0.02 us  [the longest x2 1.17 us: shards_group(): jnp.stack([tokens] + [lax.ppermute(tokens, 'node', xor_pairs(n_node, s))...]
  transfers between devices with their start and end apart: 18 -> 14, of which waited for: 7 -> 4; matrix products, arithmetic and copies ran while one was open for 8% -> 0% of each run, Pallas kernels for 18% -> 36%
where the time goes in v2:
time: 69.2 us; the launch traced here: 68.7 us
  Pallas kernels  44.7 us (65%)
  starting transfers between devices  17.4 us (25%)
  waiting for transfers between devices  3.57 us (5%)
  local copies, waits for them, and re-layouts  2.2 us (3%)
  between operations  0.82 us (1%)
    pallas_call x1, Pallas kernels, shards_group(): pl.pallas_call(lambda *refs: forward_kernel(n_dp, chunk, *refs), out_shap...  18.7 us
    ppermute x14, starting transfers between devices, permute(): lax.ppermute(array, axis, xor_pairs(mesh_shape[axis == 'node'], step))  17.4 us
    pallas_call x3, Pallas kernels, load_rows(): pl.pallas_call(lambda *refs: load_kernel(first, *refs), out_shape=(pltpu....  9.3 us
    pallas_call x1, Pallas kernels, shards_group(): pl.pallas_call(lambda *refs: product_kernel(n_dp, cuts, *refs), out_shape...  8.03 us
    pallas_call x1, Pallas kernels, shards_group(): pl.pallas_call(lambda *refs: backward_kernel(chunk, *refs), out_shape=(ja...  7.65 us
    ppermute x14, waiting for transfers between devices, permute(): lax.ppermute(array, axis, xor_pairs(mesh_shape[axis == 'node'], step))  3.57 us
    unnamed x10, local copies, waits for them, and re-layouts  2.15 us
  transfers between devices with their start and end apart: 14, of which 4 were waited for; matrix products, arithmetic and copies ran while one was open for 0% of the time, Pallas kernels for 36%

profile of v2, /device:TPU:0, one launch (start us, length us, event | category | flops | bytes accessed | tf_op | source)
XLA Modules:
  0.0 68.7 jit_solution(13667364563149978091)
XLA Ops:
  0.6 0.0 copy-start
  0.6 0.7 %copy-done = bf16[2,4096]{1,0:T(2,128)(2,1)S(1)} copy-done((bf16[2,4096]{1,0:T(2,128)(2,1)S(1)}, bf16[2,4096]{1,0:T(2,128)(2,1)}, u32[]{:S(2)}) %copy-start) | copy-done | bytes 16408
  1.4 0.7 %copy-done.3 = bf16[2,4096]{1,0:T(2,128)(2,1)S(1)} copy-done((bf16[2,4096]{1,0:T(2,128)(2,1)S(1)}, bf16[2,4096]{1,0:T(2,128)(2,1)}, u32[]{:S(2)}) %copy-start.3) | copy-done | bytes 16408
  2.1 3.1 %collective-permute-start = (bf16[2,3072]{1,0:T(2,128)(2,1)S(1)}, bf16[2,3072]{1,0:T(2,128)(2,1)S(1)}, u32[]{:S(2)}, u32[]{:S(2)}) collective-permute-start(bf16[2,3072]{1,0:T(2,128)(2,1)S(1)} %get-tuple-element.26), channel_id=1, source_target_pairs={{0,8},{8,0},{16,24},{24,16},{1,9},{9,1},{17,25},{25,17},{2,10},{10... | collective-permute-start | bytes 36872 | tf_op jit(solution)/shard_map/ppermute | solution.py:246
  5.2 2.6 %collective-permute-start.1 = (bf16[2,3072]{1,0:T(2,128)(2,1)S(1)}, bf16[2,3072]{1,0:T(2,128)(2,1)S(1)}, u32[]{:S(2)}, u32[]{:S(2)}) collective-permute-start(bf16[2,3072]{1,0:T(2,128)(2,1)S(1)} %get-tuple-element.27), channel_id=1, source_target_pairs={{0,16},{8,24},{16,0},{24,8},{1,17},{9,25},{17,1},{25,9},{2,18},{10... | collective-permute-start | bytes 36872 | tf_op jit(solution)/shard_map/ppermute | solution.py:246
  7.8 0.7 %copy-done.1 = bf16[2,4096]{1,0:T(2,128)(2,1)S(1)} copy-done((bf16[2,4096]{1,0:T(2,128)(2,1)S(1)}, bf16[2,4096]{1,0:T(2,128)(2,1)}, u32[]{:S(2)}) %copy-start.1) | copy-done | bytes 16408
  8.5 3.1 %load_gate_a.1 = (bf16[2048,1792]{1,0:T(8,128)(2,1)S(1)}, f32[8,128]{1,0:T(8,128)S(1)}) custom-call(bf16[4096,1792]{1,0:T(8,128)(2,1)} %refs_0_.8, bf16[2,4096]{1,0:T(2,128)(2,1)S(1)} %copy-done.1), custom_call_target="tpu_custom_call" | custom-call | bytes 7340032 | tf_op jit(solution)/shard_map/load_gate_a/pallas_call | solution.py:80
  11.6 0.0 collective-permute-done.refs_2_
  11.6 1.6 %collective-permute-done.2.refs_4_ = bf16[2,3072]{1,0:T(2,128)(2,1)S(1)} collective-permute-done((bf16[2,3072]{1,0:T(2,128)(2,1)S(1)}, bf16[2,3072]{1,0:T(2,128)(2,1)S(1)}, u32[]{:S(2)}, u32[]{:S(2)}) %collective-permute-start.2) | collective-permute-done | bytes 12320 | tf_op jit(solution)/shard_map/ppermute | solution.py:246
  13.3 2.5 %collective-permute-start.5 = (bf16[2,17408]{1,0:T(2,128)(2,1)S(1)}, bf16[2,17408]{1,0:T(2,128)(2,1)S(1)}, u32[]{:S(2)}, u32[]{:S(2)}) collective-permute-start(bf16[2,17408]{1,0:T(2,128)(2,1)S(1)} %join.1.refs_0_), channel_id=1, source_target_pairs={{0,6},{1,7},{2,4},{3,5},{4,2},{5,3},{6,0},{7,1},{8,14},{9,15},{10,... | collective-permute-start | bytes 208904 | tf_op jit(solution)/shard_map/ppermute | solution.py:246
  15.8 0.5 collective-permute-start.4
  16.3 0.5 collective-permute-start.3
  16.8 3.1 %load_gate_b.1 = (bf16[2048,1792]{1,0:T(8,128)(2,1)S(1)}, f32[8,128]{1,0:T(8,128)S(1)}) custom-call(bf16[4096,1792]{1,0:T(8,128)(2,1)} %refs_0_.8, f32[8,128]{1,0:T(8,128)S(1)} %get-tuple-element.29.refs_5_.refs_1_), custom_call_target="tpu_custom_call" | custom-call | bytes 7340032 | tf_op jit(solution)/shard_map/load_gate_b/pallas_call | solution.py:80
  20.0 0.2 collective-permute-done.4.refs_2_
  20.1 0.5 collective-permute-done.3.refs_1_
  20.6 0.1 collective-permute-start.6
  20.7 3.1 %load_up_a.1 = (bf16[2048,1792]{1,0:T(8,128)(2,1)S(1)}, f32[8,128]{1,0:T(8,128)S(1)}) custom-call(bf16[4096,1792]{1,0:T(8,128)(2,1)} %refs_4_.1, f32[8,128]{1,0:T(8,128)S(1)} %get-tuple-element.30.refs_4_.refs_1_), custom_call_target="tpu_custom_call" | custom-call | bytes 7340032 | tf_op jit(solution)/shard_map/load_up_a/pallas_call | solution.py:80
  23.8 0.0 collective-permute-done.6.other
  23.8 0.4 arrange.1
  24.2 18.7 %forward.1 = (bf16[2,16,1792]{2,1,0:T(8,128)(2,1)S(1)}, bf16[2,16,1792]{2,1,0:T(8,128)(2,1)S(1)}, bf16[2,16,1792]{2,1,0:T(8,128)(2,1)S(1)}, bf16[2,16,1792]{2,1,...) custom-call(bf16[2,16,4096]{2,1,0:T(8,128)(2,1)S(1)} %get-tuple-elem, ...), custom_call_target="tpu_custom_call", output_to_operand_aliasing={{6}: (1, {}), {7}: (2, {}), {8}: (3, {})} | custom-call | flops 704643072 | bytes 29360128 | tf_op jit(solution)/shard_map/forward/pallas_call | solution.py:282
  42.9 0.1 collective-permute-start.7
  43.0 2.8 %collective-permute-start.8 = (bf16[2,16,1792]{2,1,0:T(8,128)(2,1)S(1)}, bf16[2,16,1792]{2,1,0:T(8,128)(2,1)S(1)}, u32[]{:S(2)}, u32[]{:S(2)}) collective-permute-start(bf16[2,16,1792]{2,1,0:T(8,128)(2,1)S(1)} %get-tuple-element.44), channel_id=1, source_target_pairs={{0,16},{8,24},{16,0},{24,8},{1,17},{9,25},{17,1},{25,9},{2,18},{10... | collective-permute-start | bytes 344072 | tf_op jit(solution)/shard_map/ppermute | solution.py:246
  45.7 1.6 %collective-permute-start.9 = (bf16[2,16,1792]{2,1,0:T(8,128)(2,1)S(1)}, bf16[2,16,1792]{2,1,0:T(8,128)(2,1)S(1)}, u32[]{:S(2)}, u32[]{:S(2)}) collective-permute-start(bf16[2,16,1792]{2,1,0:T(8,128)(2,1)S(1)} %get-tuple-element.45), channel_id=1, source_target_pairs={{0,24},{8,16},{16,8},{24,0},{1,25},{9,17},{17,9},{25,1},{2,26},{10... | collective-permute-start | bytes 344072 | tf_op jit(solution)/shard_map/ppermute | solution.py:246
  47.3 7.7 %backward.1 = (f32[8,4096]{1,0:T(8,128)S(1)}, bf16[8,4096]{1,0:T(8,128)(2,1)S(1)}) custom-call(bf16[2,16,1792]{2,1,0:T(8,128)(2,1)S(1)} %get-tuple-element.36.refs_0_, bf16[2048,1792]{1,0:T(8,128)(2,1)S(1)} %get-tuple-element.37.refs_1_, bf16[2048,1792]{1,0:T(8,128)(2,1)S(1)} %get-tuple-element.38.refs_2_, bf16[2048,1792]{1,0:T(8,128)(2,1)S(1)} %get-tuple-element.39.refs_3_, ...), custom_call_target="tpu_custom_call" | custom-call | flops 469762048 | bytes 29360128 | tf_op jit(solution)/shard_map/backward/pallas_call | solution.py:305
  55.0 0.0 collective-permute-done.8.refs_1_.refs_4_
  55.1 0.1 collective-permute-start.10
  55.1 1.2 %collective-permute-done.10 = bf16[8,4096]{1,0:T(8,128)(2,1)S(1)} collective-permute-done((bf16[8,4096]{1,0:T(8,128)(2,1)S(1)}, bf16[8,4096]{1,0:T(8,128)(2,1)S(1)}, u32[]{:S(2)}, u32[]{:S(2)}) %collective-permute-start.10) | collective-permute-done | bytes 65568 | tf_op jit(solution)/shard_map/ppermute | solution.py:246
  56.5 1.9 %collective-permute-start.13 = (bf16[2,4096]{1,0:T(2,128)(2,1)S(1)}, bf16[2,4096]{1,0:T(2,128)(2,1)S(1)}, u32[]{:S(2)}, u32[]{:S(2)}) collective-permute-start(bf16[2,4096]{1,0:T(2,128)(2,1)S(1)} %get-tuple-element.52), channel_id=1, source_target_pairs={{0,6},{1,7},{2,4},{3,5},{4,2},{5,3},{6,0},{7,1},{8,14},{9,15},{10,... | collective-permute-start | bytes 49160 | tf_op jit(solution)/shard_map/ppermute | solution.py:246
  58.3 0.5 collective-permute-start.12
  58.8 1.2 %collective-permute-start.11 = (bf16[2,4096]{1,0:T(2,128)(2,1)S(1)}, bf16[2,4096]{1,0:T(2,128)(2,1)S(1)}, u32[]{:S(2)}, u32[]{:S(2)}) collective-permute-start(bf16[2,4096]{1,0:T(2,128)(2,1)S(1)} %get-tuple-element.54), channel_id=1, source_target_pairs={{0,2},{1,3},{2,0},{3,1},{4,6},{5,7},{6,4},{7,5},{8,10},{9,11},{10,... | collective-permute-start | bytes 49160 | tf_op jit(solution)/shard_map/ppermute | solution.py:246
  60.0 8.0 %product.1 = (f32[3072,1792]{1,0:T(8,128)}, f32[8,128]{1,0:T(8,128)S(1)}) custom-call(bf16[2,16,4096]{2,1,0:T(8,128)(2,1)S(1)} %get-tuple-element.32.refs_0_, bf16[48,3072]{1,0:T(8,128)(2,1)S(1)} %get-tuple-element.46.refs_1_, bf16[2,16,1792]{2,1,0:T(8,128)(2,1)S(1)} %get-tuple-element.47.refs_2_, ...), custom_call_target="tpu_custom_call" | custom-call | flops 704643072 | bytes 22020096 | tf_op jit(solution)/shard_map/product/pallas_call | solution.py:335
  68.1 0.7 final_sum.1
  (20 shorter events, 0.2 us)
Async XLA Ops:
  0.6 0.7 %copy-start = (bf16[2,4096]{1,0:T(2,128)(2,1)S(1)}, bf16[2,4096]{1,0:T(2,128)(2,1)}, u32[]{:S(2)}) copy-start(bf16[2,4096]{1,0:T(2,128)(2,1)} %refs_0_.7) | copy-start | bytes 49156
  1.3 0.7 %copy-start.3 = (bf16[2,4096]{1,0:T(2,128)(2,1)S(1)}, bf16[2,4096]{1,0:T(2,128)(2,1)}, u32[]{:S(2)}) copy-start(bf16[2,4096]{1,0:T(2,128)(2,1)} %refs_1_.5) | copy-start | bytes 49156
  2.1 9.5 %collective-permute-start = (bf16[2,3072]{1,0:T(2,128)(2,1)S(1)}, bf16[2,3072]{1,0:T(2,128)(2,1)S(1)}, u32[]{:S(2)}, u32[]{:S(2)}) collective-permute-start(bf16[2,3072]{1,0:T(2,128)(2,1)S(1)} %get-tuple-element.26), channel_id=1, source_target_pairs={{0,8},{8,0},{16,24},{24,16},{1,9},{9,1},{17,25},{25,17},{2,10},{10... | collective-permute-start | bytes 36872 | tf_op jit(solution)/shard_map/ppermute | solution.py:246
  5.2 6.4 %collective-permute-start.1 = (bf16[2,3072]{1,0:T(2,128)(2,1)S(1)}, bf16[2,3072]{1,0:T(2,128)(2,1)S(1)}, u32[]{:S(2)}, u32[]{:S(2)}) collective-permute-start(bf16[2,3072]{1,0:T(2,128)(2,1)S(1)} %get-tuple-element.27), channel_id=1, source_target_pairs={{0,16},{8,24},{16,0},{24,8},{1,17},{9,25},{17,1},{25,9},{2,18},{10... | collective-permute-start | bytes 36872 | tf_op jit(solution)/shard_map/ppermute | solution.py:246
  7.8 5.5 %collective-permute-start.2 = (bf16[2,3072]{1,0:T(2,128)(2,1)S(1)}, bf16[2,3072]{1,0:T(2,128)(2,1)S(1)}, u32[]{:S(2)}, u32[]{:S(2)}) collective-permute-start(bf16[2,3072]{1,0:T(2,128)(2,1)S(1)} %get-tuple-element.28), channel_id=1, source_target_pairs={{0,24},{8,16},{16,8},{24,0},{1,25},{9,17},{17,9},{25,1},{2,26},{10... | collective-permute-start | bytes 36872 | tf_op jit(solution)/shard_map/ppermute | solution.py:246
  7.8 0.7 %copy-start.1 = (bf16[2,4096]{1,0:T(2,128)(2,1)S(1)}, bf16[2,4096]{1,0:T(2,128)(2,1)}, u32[]{:S(2)}) copy-start(bf16[2,4096]{1,0:T(2,128)(2,1)} %refs_0_.7) | copy-start | bytes 49156
  8.5 4.8 %copy-start.2 = (bf16[2,4096]{1,0:T(2,128)(2,1)S(1)}, bf16[2,4096]{1,0:T(2,128)(2,1)}, u32[]{:S(2)}) copy-start(bf16[2,4096]{1,0:T(2,128)(2,1)} %refs_0_.7) | copy-start | bytes 49156
  8.5 4.8 %copy-start.4 = (bf16[2,4096]{1,0:T(2,128)(2,1)S(1)}, bf16[2,4096]{1,0:T(2,128)(2,1)}, u32[]{:S(2)}) copy-start(bf16[2,4096]{1,0:T(2,128)(2,1)} %refs_1_.5) | copy-start | bytes 49156
  13.3 6.7 %collective-permute-start.5 = (bf16[2,17408]{1,0:T(2,128)(2,1)S(1)}, bf16[2,17408]{1,0:T(2,128)(2,1)S(1)}, u32[]{:S(2)}, u32[]{:S(2)}) collective-permute-start(bf16[2,17408]{1,0:T(2,128)(2,1)S(1)} %join.1.refs_0_), channel_id=1, source_target_pairs={{0,6},{1,7},{2,4},{3,5},{4,2},{5,3},{6,0},{7,1},{8,14},{9,15},{10,... | collective-permute-start | bytes 208904 | tf_op jit(solution)/shard_map/ppermute | solution.py:246
  15.8 4.3 %collective-permute-start.4 = (bf16[2,17408]{1,0:T(2,128)(2,1)S(1)}, bf16[2,17408]{1,0:T(2,128)(2,1)S(1)}, u32[]{:S(2)}, u32[]{:S(2)}) collective-permute-start(bf16[2,17408]{1,0:T(2,128)(2,1)S(1)} %join.1.refs_0_), channel_id=1, source_target_pairs={{0,4},{1,5},{2,6},{3,7},{4,0},{5,1},{6,2},{7,3},{8,12},{9,13},{10,... | collective-permute-start | bytes 208904 | tf_op jit(solution)/shard_map/ppermute | solution.py:246
  16.3 4.3 %collective-permute-start.3 = (bf16[2,17408]{1,0:T(2,128)(2,1)S(1)}, bf16[2,17408]{1,0:T(2,128)(2,1)S(1)}, u32[]{:S(2)}, u32[]{:S(2)}) collective-permute-start(bf16[2,17408]{1,0:T(2,128)(2,1)S(1)} %join.1.refs_0_), channel_id=1, source_target_pairs={{0,2},{1,3},{2,0},{3,1},{4,6},{5,7},{6,4},{7,5},{8,10},{9,11},{10,... | collective-permute-start | bytes 208904 | tf_op jit(solution)/shard_map/ppermute | solution.py:246
  20.6 3.2 %collective-permute-start.6 = (bf16[4,2,17408]{2,1,0:T(2,128)(2,1)S(1)}, bf16[4,2,17408]{2,1,0:T(2,128)(2,1)S(1)}, u32[]{:S(2)}, u32[]{:S(2)}) collective-permute-start(bf16[4,2,17408]{2,1,0:T(2,128)(2,1)S(1)} %stack.1.plane), channel_id=1, source_target_pairs={{0,1},{1,0},{2,3},{3,2},{4,5},{5,4},{6,7},{7,6},{8,9},{9,8},{10,11... | collective-permute-start | bytes 835592 | tf_op jit(solution)/shard_map/ppermute | solution.py:246
  42.9 12.1 %collective-permute-start.7 = (bf16[2,16,1792]{2,1,0:T(8,128)(2,1)S(1)}, bf16[2,16,1792]{2,1,0:T(8,128)(2,1)S(1)}, u32[]{:S(2)}, u32[]{:S(2)}) collective-permute-start(bf16[2,16,1792]{2,1,0:T(8,128)(2,1)S(1)} %get-tuple-element.43), channel_id=1, source_target_pairs={{0,8},{8,0},{16,24},{24,16},{1,9},{9,1},{17,25},{25,17},{2,10},{10... | collective-permute-start | bytes 344072 | tf_op jit(solution)/shard_map/ppermute | solution.py:246
  43.0 12.0 %collective-permute-start.8 = (bf16[2,16,1792]{2,1,0:T(8,128)(2,1)S(1)}, bf16[2,16,1792]{2,1,0:T(8,128)(2,1)S(1)}, u32[]{:S(2)}, u32[]{:S(2)}) collective-permute-start(bf16[2,16,1792]{2,1,0:T(8,128)(2,1)S(1)} %get-tuple-element.44), channel_id=1, source_target_pairs={{0,16},{8,24},{16,0},{24,8},{1,17},{9,25},{17,1},{25,9},{2,18},{10... | collective-permute-start | bytes 344072 | tf_op jit(solution)/shard_map/ppermute | solution.py:246
  45.7 9.3 %collective-permute-start.9 = (bf16[2,16,1792]{2,1,0:T(8,128)(2,1)S(1)}, bf16[2,16,1792]{2,1,0:T(8,128)(2,1)S(1)}, u32[]{:S(2)}, u32[]{:S(2)}) collective-permute-start(bf16[2,16,1792]{2,1,0:T(8,128)(2,1)S(1)} %get-tuple-element.45), channel_id=1, source_target_pairs={{0,24},{8,16},{16,8},{24,0},{1,25},{9,17},{17,9},{25,1},{2,26},{10... | collective-permute-start | bytes 344072 | tf_op jit(solution)/shard_map/ppermute | solution.py:246
  55.1 1.3 %collective-permute-start.10 = (bf16[8,4096]{1,0:T(8,128)(2,1)S(1)}, bf16[8,4096]{1,0:T(8,128)(2,1)S(1)}, u32[]{:S(2)}, u32[]{:S(2)}) collective-permute-start(bf16[8,4096]{1,0:T(8,128)(2,1)S(1)} %hold.1), channel_id=1, source_target_pairs={{0,1},{1,0},{2,3},{3,2},{4,5},{5,4},{6,7},{7,6},{8,9},{9,8},{10,11... | collective-permute-start | bytes 196616 | tf_op jit(solution)/shard_map/ppermute | solution.py:246
  56.5 11.6 %collective-permute-start.13 = (bf16[2,4096]{1,0:T(2,128)(2,1)S(1)}, bf16[2,4096]{1,0:T(2,128)(2,1)S(1)}, u32[]{:S(2)}, u32[]{:S(2)}) collective-permute-start(bf16[2,4096]{1,0:T(2,128)(2,1)S(1)} %get-tuple-element.52), channel_id=1, source_target_pairs={{0,6},{1,7},{2,4},{3,5},{4,2},{5,3},{6,0},{7,1},{8,14},{9,15},{10,... | collective-permute-start | bytes 49160 | tf_op jit(solution)/shard_map/ppermute | solution.py:246
  58.3 9.7 %collective-permute-start.12 = (bf16[2,4096]{1,0:T(2,128)(2,1)S(1)}, bf16[2,4096]{1,0:T(2,128)(2,1)S(1)}, u32[]{:S(2)}, u32[]{:S(2)}) collective-permute-start(bf16[2,4096]{1,0:T(2,128)(2,1)S(1)} %get-tuple-element.53), channel_id=1, source_target_pairs={{0,4},{1,5},{2,6},{3,7},{4,0},{5,1},{6,2},{7,3},{8,12},{9,13},{10,... | collective-permute-start | bytes 49160 | tf_op jit(solution)/shard_map/ppermute | solution.py:246
  58.8 9.2 %collective-permute-start.11 = (bf16[2,4096]{1,0:T(2,128)(2,1)S(1)}, bf16[2,4096]{1,0:T(2,128)(2,1)S(1)}, u32[]{:S(2)}, u32[]{:S(2)}) collective-permute-start(bf16[2,4096]{1,0:T(2,128)(2,1)S(1)} %get-tuple-element.54), channel_id=1, source_target_pairs={{0,2},{1,3},{2,0},{3,1},{4,6},{5,7},{6,4},{7,5},{8,10},{9,11},{10,... | collective-permute-start | bytes 49160 | tf_op jit(solution)/shard_map/ppermute | solution.py:246

commit v3 on v2

--- a/solution.py
+++ b/solution.py
@@ -57,16 +57,15 @@
     return grad_normed, weight_grads
 
 
-def far_kernel(n_dp, normed, cotangent, *far):
-    unit = normed.shape[1] // n_dp
-    for step, out in enumerate(far, 1):
-        owner = lax.axis_index("dp") ^ step
-        for j in range(3):
-            index = 3 * owner + j
-            columns = pl.ds(pl.multiple_of(lax.rem(index, n_dp) * unit, unit), unit)
-            out[:, j * unit : (j + 1) * unit] = jnp.where(
-                index >= 2 * n_dp, cotangent[:, columns], normed[:, columns]
-            )
+def join_kernel(normed, cotangent, out, sem):
+    copies = [
+        pltpu.make_async_copy(source, out.at[i], sem.at[i])
+        for i, source in enumerate((normed, cotangent))
+    ]
+    for copy in copies:
+        copy.start()
+    for copy in copies:
+        copy.wait()
 
 
 def load_kernel(first, weight, after, out, token, sem):
@@ -92,14 +91,6 @@
         ),
         name=name,
     )(weight, after)
-
-
-def join_kernel(*refs):
-    *pieces, after, out = refs
-    start = 0
-    for piece in pieces:
-        out[:, start : start + piece.shape[1]] = piece[...]
-        start += piece.shape[1]
 
 
 def stack_kernel(*refs):
@@ -120,91 +111,87 @@
     )(*pieces, after)
 
 
-def arrange_kernel(plane, other, after, tokens, far, wide):
-    own = plane.shape[1]
-    group, width = tokens.shape[1:]
-    block = far.shape[1]
-    for slot in range(plane.shape[0]):
-        for half, source in enumerate((plane, other)):
-            start = (half * plane.shape[0] + slot) * own
-            wide[start : start + own] = source[slot].astype(F32)
+def arrange_kernel(n_dp, plane, other, after, tokens, *refs):
+    *columns, wide = refs
+    own = plane.shape[2]
+    unit = tokens.shape[2] // n_dp
     for i in range(2):
-        tokens[i] = wide[:, i * width : (i + 1) * width].astype(BF)
-    for i in range(far.shape[0] // group):
-        start = 2 * width + i * block
-        far[i * group : (i + 1) * group] = wide[:, start : start + block].astype(BF)
-
-
-def forward_kernel(n_dp, chunk, tokens, gate_a, gate_b, up_a, up, down, *refs):
-    *packs, grads_out, up_b, _, _, _, gate_pre, up_pre, grads, down_rows, up_sem, down_sem = refs
-    half = gate_a.shape[0]
-    columns = gate_a.shape[1]
-    up_copy = pltpu.make_async_copy(up.at[pl.ds(half, half)], up_b, up_sem)
-    up_copy.start()
+        for slot in range(plane.shape[0]):
+            for half, source in enumerate((plane, other)):
+                start = (half * plane.shape[0] + slot) * own
+                wide[i, start : start + own] = source[slot, i].astype(F32)
+        tokens[i] = wide[i].astype(BF)
+    for step, out in enumerate(columns):
+        owner = lax.axis_index("dp") ^ step
+        for j in range(3):
+            index = 3 * owner + j
+            part = pl.ds(pl.multiple_of(lax.rem(index, n_dp) * unit, unit), unit)
+            out[:, j * unit : (j + 1) * unit] = tokens[lax.div(index, 2 * n_dp), :, part]
+
+
+def forward_kernel(chunk, tokens, gate_a, gate_b, down, up_hbm, grads, up, _a, _b, gate_pre, grad_hidden, sem):
+    half, columns = gate_a.shape
     parts = [slice(start, start + chunk) for start in range(0, columns, chunk)]
-    down_copies = [
+    copies = [
         pltpu.make_async_copy(
-            down.at[pl.ds(part.start, chunk)], down_rows.at[pl.ds(part.start, chunk)], down_sem.at[i]
+            up_hbm.at[pl.ds(i * half, half)], up.at[pl.ds(i * half, half)], sem.at[i]
         )
-        for i, part in enumerate(parts)
+        for i in range(2)
     ]
-    for copy in down_copies:
+    for copy in copies:
         copy.start()
     for part in parts:
         gate_pre[:, part] = dot(tokens[0, :, :half], gate_a[:, part], NN) + dot(
             tokens[0, :, half:], gate_b[:, part], NN
         )
-        up_pre[:, part] = dot(tokens[0, :, :half], up_a[:, part], NN)
-    up_copy.wait()
     for part in parts:
-        up_pre[:, part] += dot(tokens[0, :, half:], up_b[:, part], NN)
-    for part, copy in zip(parts, down_copies):
+        grad_hidden[:, part] = dot(tokens[1], down[part, :], NT)
+    for copy in copies:
         copy.wait()
-        grad_hidden = dot(tokens[1], down_rows[part, :], NT)
+    for part in parts:
+        up_part = dot(tokens[0], up[:, part], NN)
         gate_part = gate_pre[:, part]
-        up_part = up_pre[:, part]
         sigma = jax.nn.sigmoid(gate_part)
         activated = gate_part * sigma
         grads[0, :, part] = (
-            grad_hidden * up_part * sigma * (1.0 + gate_part * (1.0 - sigma))
+            grad_hidden[:, part] * up_part * sigma * (1.0 + gate_part * (1.0 - sigma))
         ).astype(BF)
-        grads[1, :, part] = (grad_hidden * activated).astype(BF)
+        grads[1, :, part] = (grad_hidden[:, part] * activated).astype(BF)
         grads[2, :, part] = (activated * up_part).astype(BF)
-    grads_out[...] = grads[:2]
-    for step, pack in enumerate(packs):
+
+
+def pack_kernel(n_dp, grads, *refs):
+    for step, pack in enumerate(refs[-n_dp:]):
         owner = lax.axis_index("dp") ^ step
         pack[0] = grads[lax.div(3 * owner, n_dp)]
         pack[1] = grads[lax.div(3 * owner + 2, n_dp)]
 
 
-def backward_kernel(chunk, grads, gate_a, gate_b, up_a, up_b, keep, send):
+def backward_kernel(chunk, grads, gate_a, gate_b, up_all, keep, send):
     half = gate_a.shape[0]
     rows = keep.shape[0]
-    for gate, up, base in ((gate_a, up_a, 0), (gate_b, up_b, half)):
+    for gate, base in ((gate_a, 0), (gate_b, half)):
         for start in range(0, half, chunk):
             part = slice(start, start + chunk)
-            total = dot(grads[0], gate[part, :], NT) + dot(grads[1], up[part, :], NT)
+            total = dot(grads[0], gate[part, :], NT) + dot(
+                grads[1], up_all[base + start : base + start + chunk, :], NT
+            )
             keep[:, base + start : base + start + chunk] = total[:rows]
             send[:, base + start : base + start + chunk] = total[rows:].astype(BF)
 
 
-def product_kernel(n_dp, pieces, tokens, far, *refs):
-    *packs, out, token, columns, grads, result, sem = refs
-    group = tokens.shape[1]
-    unit = tokens.shape[2] // n_dp
+def product_kernel(n_dp, pieces, *refs):
+    sources, packs = refs[:n_dp], refs[n_dp : 2 * n_dp]
+    out, token, columns, grads, result, sem = refs[2 * n_dp :]
+    group, block = sources[0].shape
+    unit = block // 3
     d = lax.axis_index("dp")
     token[...] = jnp.zeros(token.shape, token.dtype)
-    for slot, pack in enumerate(packs):
+    for slot in range(n_dp):
+        rows = slice(slot * group, (slot + 1) * group)
+        columns[rows] = sources[slot][...]
         for m in range(2):
-            grads[m, slot * group : (slot + 1) * group] = pack[m]
-    for j in range(3):
-        index = 3 * d + j
-        source = pl.ds(pl.multiple_of(lax.rem(index, n_dp) * unit, unit), unit)
-        part = slice(j * unit, (j + 1) * unit)
-        columns[:group, part] = jnp.where(
-            index >= 2 * n_dp, tokens[1, :, source], tokens[0, :, source]
-        )
-    columns[group:] = far[...]
+            grads[m, rows] = packs[slot][m]
     copies = []
     for i, (start, count) in enumerate(pieces):
         j = start // unit
@@ -245,61 +232,66 @@
     def permute(array, axis, step):
         return lax.ppermute(array, axis, xor_pairs(mesh_shape[axis == "node"], step))
 
-    far = pl.pallas_call(
-        lambda *refs: far_kernel(n_dp, *refs),
-        out_shape=[jax.ShapeDtypeStruct((own, block), BF) for s in groups],
-        in_specs=[VMEM_SPEC] * 2,
-        out_specs=[VMEM_SPEC] * len(groups),
+    mine = pl.pallas_call(
+        join_kernel,
+        out_shape=jax.ShapeDtypeStruct((2, own, width), BF),
+        in_specs=[HBM_SPEC] * 2,
+        out_specs=VMEM_SPEC,
+        scratch_shapes=[pltpu.SemaphoreType.DMA((2,))],
         compiler_params=pltpu.CompilerParams(vmem_limit_bytes=1 << 20),
-        name="far_columns",
-    )(normed, cotangent)
-    far = [permute(piece, "dp", s) for s, piece in zip(groups, far)]
-    gate_hbm, up_hbm, down_hbm = (in_hbm(w) for w in (gate_weight, up_weight, down_weight))
-    gate_a, token = load_rows(gate_hbm, 0, half, normed, "load_gate_a")
-    tall = 2 * width + len(groups) * block
-    mine = glue(join_kernel, (own, tall), [normed, cotangent, *far], token, "join")
+        name="join",
+    )(in_hbm(normed), in_hbm(cotangent))
+    gate_hbm, up_hbm = in_hbm(gate_weight), in_hbm(up_weight)
     plane = [mine] + [permute(mine, "node", s) for s in chips]
+    gate_a, token = load_rows(gate_hbm, 0, half, in_hbm(normed), "load_gate_a")
+    plane = glue(stack_kernel, (len(plane), 2, own, width), plane, token, "stack")
+    other = permute(plane, "node", 1)
     gate_b, token = load_rows(gate_hbm, half, half, token, "load_gate_b")
-    plane = glue(stack_kernel, (len(plane), own, tall), plane, token, "stack")
-    other = permute(plane, "node", 1)
-    up_a, token = load_rows(up_hbm, 0, half, token, "load_up_a")
-    tokens, far = pl.pallas_call(
-        arrange_kernel,
-        out_shape=(
-            jax.ShapeDtypeStruct((2, group, width), BF),
-            jax.ShapeDtypeStruct(((n_dp - 1) * group, block), BF),
-        ),
+    piece = jax.ShapeDtypeStruct((group, block), BF)
+    tokens, *columns = pl.pallas_call(
+        lambda *refs: arrange_kernel(n_dp, *refs),
+        out_shape=[jax.ShapeDtypeStruct((2, group, width), BF)] + [piece] * n_dp,
         in_specs=[VMEM_SPEC] * 2 + [ANY_SPEC],
-        out_specs=(VMEM_SPEC, VMEM_SPEC),
-        scratch_shapes=[pltpu.VMEM((group, tall), F32)],
+        out_specs=[VMEM_SPEC] * (n_dp + 1),
+        scratch_shapes=[pltpu.VMEM((2, group, width), F32)],
         compiler_params=pltpu.CompilerParams(vmem_limit_bytes=4 << 20),
         cost_estimate=pl.CostEstimate(flops=0, bytes_accessed=1 << 20, transcendentals=0),
         name="arrange",
     )(plane, other, token)
-
-    pack = jax.ShapeDtypeStruct((2, group, hidden), BF)
+    columns = [columns[0]] + [permute(columns[s], "dp", s) for s in groups]
+
     chunk = 256
-    *packs, grads, up_b, gate_a, gate_b, up_a = pl.pallas_call(
-        lambda *refs: forward_kernel(n_dp, chunk, *refs),
-        out_shape=[pack] * (n_dp + 1) + [pltpu.VMEM((half, hidden), BF)] * 4,
-        in_specs=[VMEM_SPEC] * 4 + [HBM_SPEC] * 2,
-        out_specs=[VMEM_SPEC] * (n_dp + 5),
-        input_output_aliases={1: n_dp + 2, 2: n_dp + 3, 3: n_dp + 4},
+    grads, up, gate_a, gate_b = pl.pallas_call(
+        lambda *refs: forward_kernel(chunk, *refs),
+        out_shape=[
+            jax.ShapeDtypeStruct((3, group, hidden), BF),
+            pltpu.VMEM((width, hidden), BF),
+            pltpu.VMEM((half, hidden), BF),
+            pltpu.VMEM((half, hidden), BF),
+        ],
+        in_specs=[VMEM_SPEC] * 4 + [HBM_SPEC],
+        out_specs=[VMEM_SPEC] * 4,
+        input_output_aliases={1: 2, 2: 3},
         scratch_shapes=[
             pltpu.VMEM((group, hidden), F32),
             pltpu.VMEM((group, hidden), F32),
-            pltpu.VMEM((3, group, hidden), BF),
-            pltpu.VMEM((hidden, width), BF),
-            pltpu.SemaphoreType.DMA,
-            pltpu.SemaphoreType.DMA((hidden // chunk,)),
+            pltpu.SemaphoreType.DMA((2,)),
         ],
-        compiler_params=pltpu.CompilerParams(vmem_limit_bytes=20 << 20),
+        compiler_params=pltpu.CompilerParams(vmem_limit_bytes=4 << 20),
         cost_estimate=pl.CostEstimate(
             flops=6 * group * width * hidden, bytes_accessed=2 * weight_bytes, transcendentals=0
         ),
         name="forward",
-    )(tokens, in_vmem(gate_a), in_vmem(gate_b), in_vmem(up_a), up_hbm, down_hbm)
-
+    )(tokens, in_vmem(gate_a), in_vmem(gate_b), in_vmem(down_weight), up_hbm)
+
+    packs = pl.pallas_call(
+        lambda *refs: pack_kernel(n_dp, *refs),
+        out_shape=[jax.ShapeDtypeStruct((2, group, hidden), BF)] * n_dp,
+        in_specs=[VMEM_SPEC] + [ANY_SPEC] * (n_dp - 1),
+        out_specs=[VMEM_SPEC] * n_dp,
+        compiler_params=pltpu.CompilerParams(vmem_limit_bytes=1 << 20),
+        name="pack",
+    )(grads, *columns[1:])
     packs = [packs[0]] + [permute(packs[s], "dp", s) for s in groups]
 
     keep, send = pl.pallas_call(
@@ -308,14 +300,14 @@
             jax.ShapeDtypeStruct((group // 2, width), F32),
             jax.ShapeDtypeStruct((group // 2, width), BF),
         ),
-        in_specs=[VMEM_SPEC] * 5,
+        in_specs=[VMEM_SPEC] * 4,
         out_specs=(VMEM_SPEC, VMEM_SPEC),
         compiler_params=pltpu.CompilerParams(vmem_limit_bytes=4 << 20),
         cost_estimate=pl.CostEstimate(
             flops=4 * group * width * hidden, bytes_accessed=2 * weight_bytes, transcendentals=0
         ),
         name="backward",
-    )(grads, in_vmem(gate_a), in_vmem(gate_b), in_vmem(up_a), in_vmem(up_b))
+    )(grads, in_vmem(gate_a), in_vmem(gate_b), in_vmem(up))
 
     send = pl.pallas_call(
         hold_kernel,
@@ -338,7 +330,7 @@
             pltpu.HBM((block, hidden), F32),
             jax.ShapeDtypeStruct((8, 128), F32),
         ),
-        in_specs=[VMEM_SPEC] * (n_dp + 2),
+        in_specs=[VMEM_SPEC] * (2 * n_dp),
         out_specs=(HBM_SPEC, VMEM_SPEC),
         scratch_shapes=[
             pltpu.VMEM((n_dp * group, block), BF),
@@ -353,7 +345,7 @@
             transcendentals=0,
         ),
         name="product",
-    )(tokens, far, *packs)
+    )(*columns, *packs)
     grad_normed = pl.pallas_call(
         lambda *refs: final_kernel(own, *refs),
         out_shape=jax.ShapeDtypeStruct((own, width), BF),

time: 69.2 us -> 56.3 us (0.81)
  Pallas kernels: 44.7 us -> 35 us
  local copies, waits for them, and re-layouts: 2.2 us -> 0.07 us
  waiting for transfers between devices: 3.57 us -> 2.79 us
    pallas_call x3 -> x4, Pallas kernels: 19.1 us -> 12.3 us  [the longest x1 11.3 us: shards_group(): pl.pallas_call(lambda *refs: forward_kernel(chunk, *refs), out_shape=[jax...]
    pallas_call x3 -> x2, Pallas kernels: 9.3 us -> 6.34 us  [load_rows(): pl.pallas_call(lambda *refs: load_kernel(first, *refs), out_shape=(pltpu....]
    unnamed x10 -> x8, local copies, waits for them, and re-layouts: 2.15 us -> 0.02 us
    ppermute x14, waiting for transfers between devices: 3.57 us -> 2.79 us  [permute(): lax.ppermute(array, axis, xor_pairs(mesh_shape[axis == 'node'], step))]
  transfers between devices with their start and end apart: 14 -> 14, of which waited for: 4 -> 4; matrix products, arithmetic and copies ran while one was open for 0% -> 0% of each run, Pallas kernels for 36% -> 60%
where the time goes in v3:
time: 56.3 us; the launch traced here: 55.9 us
  Pallas kernels  35 us (62%)
  starting transfers between devices  17.2 us (31%)
  waiting for transfers between devices  2.79 us (5%)
  between operations  0.83 us (1%)
    ppermute x14, starting transfers between devices, permute(): lax.ppermute(array, axis, xor_pairs(mesh_shape[axis == 'node'], step))  17.2 us
    pallas_call x1, Pallas kernels, shards_group(): pl.pallas_call(lambda *refs: forward_kernel(chunk, *refs), out_shape=[jax...  11.3 us
    pallas_call x1, Pallas kernels, shards_group(): pl.pallas_call(lambda *refs: product_kernel(n_dp, cuts, *refs), out_shape...  8.01 us
    pallas_call x1, Pallas kernels, shards_group(): pl.pallas_call(lambda *refs: backward_kernel(chunk, *refs), out_shape=(ja...  7.65 us
    pallas_call x2, Pallas kernels, load_rows(): pl.pallas_call(lambda *refs: load_kernel(first, *refs), out_shape=(pltpu....  6.34 us
    ppermute x14, waiting for transfers between devices, permute(): lax.ppermute(array, axis, xor_pairs(mesh_shape[axis == 'node'], step))  2.79 us
  transfers between devices with their start and end apart: 14, of which 4 were waited for; matrix products, arithmetic and copies ran while one was open for 0% of the time, Pallas kernels for 60%

profile of v3, /device:TPU:0, one launch (start us, length us, event | category | flops | bytes accessed | tf_op | source)
XLA Modules:
  0.0 55.9 jit_solution(14080090171722414033)
XLA Ops:
  0.6 0.8 %join.1.refs_0_ = bf16[2,2,4096]{2,1,0:T(2,128)(2,1)S(1)} custom-call(bf16[2,4096]{1,0:T(2,128)(2,1)} %refs_1_.1, bf16[2,4096]{1,0:T(2,128)(2,1)} %cotangent.1), custom_call_target="tpu_custom_call" | custom-call | tf_op jit(solution)/shard_map/join/pallas_call | solution.py:235
  1.4 0.0 slice-start
  1.4 0.0 slice-start.1
  1.4 4.0 %collective-permute-start.2 = (bf16[2,2,4096]{2,1,0:T(2,128)(2,1)S(1)}, bf16[2,2,4096]{2,1,0:T(2,128)(2,1)S(1)}, u32[]{:S(2)}, u32[]{:S(2)}) collective-permute-start(bf16[2,2,4096]{2,1,0:T(2,128)(2,1)S(1)} %join.1.refs_0_), channel_id=1, source_target_pairs={{0,6},{1,7},{2,4},{3,5},{4,2},{5,3},{6,0},{7,1},{8,14},{9,15},{10,... | collective-permute-start | bytes 98312 | tf_op jit(solution)/shard_map/ppermute | solution.py:233
  5.4 0.5 collective-permute-start.1
  5.9 0.1 collective-permute-start
  6.0 3.1 %load_gate_a.1 = (bf16[2048,1792]{1,0:T(8,128)(2,1)S(1)}, f32[8,128]{1,0:T(8,128)S(1)}) custom-call(bf16[4096,1792]{1,0:T(8,128)(2,1)} %refs_0_.3, bf16[2,4096]{1,0:T(2,128)(2,1)} %refs_1_.1), custom_call_target="tpu_custom_call" | custom-call | bytes 7340032 | tf_op jit(solution)/shard_map/load_gate_a/pallas_call | solution.py:79
  9.1 0.2 collective-permute-done.1.refs_2_
  9.3 0.5 collective-permute-done.refs_1_
  9.8 0.0 slice-start.3
  9.8 0.1 collective-permute-start.3
  9.9 3.2 %load_gate_b.1 = (bf16[2048,1792]{1,0:T(8,128)(2,1)S(1)}, f32[8,128]{1,0:T(8,128)S(1)}) custom-call(bf16[4096,1792]{1,0:T(8,128)(2,1)} %refs_0_.3, f32[8,128]{1,0:T(8,128)S(1)} %get-tuple-element.23.refs_4_.refs_1_), custom_call_target="tpu_custom_call" | custom-call | bytes 7340032 | tf_op jit(solution)/shard_map/load_gate_b/pallas_call | solution.py:79
  13.2 0.0 collective-permute-done.3.refs_1_
  13.2 0.2 arrange.1
  13.4 1.7 %collective-permute-start.4 = (bf16[16,3072]{1,0:T(8,128)(2,1)S(1)}, bf16[16,3072]{1,0:T(8,128)(2,1)S(1)}, u32[]{:S(2)}, u32[]{:S(2)}) collective-permute-start(bf16[16,3072]{1,0:T(8,128)(2,1)S(1)} %get-tuple-element.34), channel_id=1, source_target_pairs={{0,8},{8,0},{16,24},{24,16},{1,9},{9,1},{17,25},{25,17},{2,10},{10... | collective-permute-start | bytes 294920 | tf_op jit(solution)/shard_map/ppermute | solution.py:233
  15.0 2.6 %collective-permute-start.5 = (bf16[16,3072]{1,0:T(8,128)(2,1)S(1)}, bf16[16,3072]{1,0:T(8,128)(2,1)S(1)}, u32[]{:S(2)}, u32[]{:S(2)}) collective-permute-start(bf16[16,3072]{1,0:T(8,128)(2,1)S(1)} %get-tuple-element.35), channel_id=1, source_target_pairs={{0,16},{8,24},{16,0},{24,8},{1,17},{9,25},{17,1},{25,9},{2,18},{10... | collective-permute-start | bytes 294920 | tf_op jit(solution)/shard_map/ppermute | solution.py:233
  17.6 0.2 collective-permute-start.6
  17.9 11.3 %forward.1 = (bf16[3,16,1792]{2,1,0:T(8,128)(2,1)S(1)}, bf16[4096,1792]{1,0:T(8,128)(2,1)S(1)}, bf16[2048,1792]{1,0:T(8,128)(2,1)S(1)}, bf16[2048,1792]{1,0:T(8,128)(2,1)S(1)}) custom-call(bf16[2,16,4096]{2,1,0:T(8,128)(2,1)S(1)} %get-tuple-element.25.refs_0_, ...), custom_call_target="tpu_custom_call", output_to_operand_aliasing={{2}: (1, {}), {3}: (2, {})} | custom-call | flops 704643072 | bytes 29360128 | tf_op jit(solution)/shard_map/forward/pallas_call | solution.py:264
  29.2 0.0 collective-permute-done.4.refs_1_
  29.2 0.0 collective-permute-done.5.refs_2_
  29.3 0.8 %collective-permute-start.7 = (bf16[2,16,1792]{2,1,0:T(8,128)(2,1)S(1)}, bf16[2,16,1792]{2,1,0:T(8,128)(2,1)S(1)}, u32[]{:S(2)}, u32[]{:S(2)}) collective-permute-start(bf16[2,16,1792]{2,1,0:T(8,128)(2,1)S(1)} %get-tuple-element.37), channel_id=1, source_target_pairs={{0,8},{8,0},{16,24},{24,16},{1,9},{9,1},{17,25},{25,17},{2,10},{10... | collective-permute-start | bytes 344072 | tf_op jit(solution)/shard_map/ppermute | solution.py:233
  30.0 3.5 %collective-permute-start.8 = (bf16[2,16,1792]{2,1,0:T(8,128)(2,1)S(1)}, bf16[2,16,1792]{2,1,0:T(8,128)(2,1)S(1)}, u32[]{:S(2)}, u32[]{:S(2)}) collective-permute-start(bf16[2,16,1792]{2,1,0:T(8,128)(2,1)S(1)} %get-tuple-element.38), channel_id=1, source_target_pairs={{0,16},{8,24},{16,0},{24,8},{1,17},{9,25},{17,1},{25,9},{2,18},{10... | collective-permute-start | bytes 344072 | tf_op jit(solution)/shard_map/ppermute | solution.py:233
  33.5 0.2 collective-permute-start.9
  33.7 7.7 %backward.1 = (f32[8,4096]{1,0:T(8,128)S(1)}, bf16[8,4096]{1,0:T(8,128)(2,1)S(1)}) custom-call(bf16[3,16,1792]{2,1,0:T(8,128)(2,1)S(1)} %get-tuple-element.28.refs_0_, bf16[2048,1792]{1,0:T(8,128)(2,1)S(1)} %get-tuple-element.29.refs_1_, bf16[2048,1792]{1,0:T(8,128)(2,1)S(1)} %get-tuple-element.30.refs_2_, bf16[4096,1792]{1,0:T(8,128)(2,1)S(1)} %get-tuple-element.31.refs_3_), custom_call_target="tpu_custom_call" | custom-call | flops 469762048 | bytes 29360128 | tf_op jit(solution)/shard_map/backward/pallas_call | solution.py:297
  41.4 0.9 %collective-permute-done.8.refs_1_.refs_6_ = bf16[2,16,1792]{2,1,0:T(8,128)(2,1)S(1)} collective-permute-done((bf16[2,16,1792]{2,1,0:T(8,128)(2,1)S(1)}, bf16[2,16,1792]{2,1,0:T(8,128)(2,1)S(1)}, u32[]{:S(2)}, u32[]{:S(2)}) %collective-permute-start.8) | collective-permute-done | bytes 114720 | tf_op jit(solution)/shard_map/ppermute | solution.py:233
  42.3 0.1 collective-permute-start.10
  42.3 1.2 %collective-permute-done.10 = bf16[8,4096]{1,0:T(8,128)(2,1)S(1)} collective-permute-done((bf16[8,4096]{1,0:T(8,128)(2,1)S(1)}, bf16[8,4096]{1,0:T(8,128)(2,1)S(1)}, u32[]{:S(2)}, u32[]{:S(2)}) %collective-permute-start.10) | collective-permute-done | bytes 65568 | tf_op jit(solution)/shard_map/ppermute | solution.py:233
  43.7 2.5 %collective-permute-start.13 = (bf16[2,4096]{1,0:T(2,128)(2,1)S(1)}, bf16[2,4096]{1,0:T(2,128)(2,1)S(1)}, u32[]{:S(2)}, u32[]{:S(2)}) collective-permute-start(bf16[2,4096]{1,0:T(2,128)(2,1)S(1)} %get-tuple-element.46), channel_id=1, source_target_pairs={{0,6},{1,7},{2,4},{3,5},{4,2},{5,3},{6,0},{7,1},{8,14},{9,15},{10,... | collective-permute-start | bytes 49160 | tf_op jit(solution)/shard_map/ppermute | solution.py:233
  46.1 0.5 collective-permute-start.12
  46.6 0.6 %collective-permute-start.11 = (bf16[2,4096]{1,0:T(2,128)(2,1)S(1)}, bf16[2,4096]{1,0:T(2,128)(2,1)S(1)}, u32[]{:S(2)}, u32[]{:S(2)}) collective-permute-start(bf16[2,4096]{1,0:T(2,128)(2,1)S(1)} %get-tuple-element.48), channel_id=1, source_target_pairs={{0,2},{1,3},{2,0},{3,1},{4,6},{5,7},{6,4},{7,5},{8,10},{9,11},{10,... | collective-permute-start | bytes 49160 | tf_op jit(solution)/shard_map/ppermute | solution.py:233
  47.2 8.0 %product.1 = (f32[3072,1792]{1,0:T(8,128)}, f32[8,128]{1,0:T(8,128)S(1)}) custom-call(bf16[16,3072]{1,0:T(8,128)(2,1)S(1)} %get-tuple-element.40.refs_0_, bf16[16,3072]{1,0:T(8,128)(2,1)S(1)} %collective-permute-done.4.refs_1_, bf16[16,3072]{1,0:T(8,128)(2,1)S(1)} %collective-permute-done.5.refs_2_, bf16[16,3072]{1,0:T(8,128)(2,1)S(1)} %collective-permute-done.6.refs_3_, ...), custom_call_target="tpu_custom_call" | custom-call | flops 704643072 | bytes 22020096 | tf_op jit(solution)/shard_map/product/pallas_call | solution.py:327
  55.3 0.7 %final_sum.1 = bf16[2,4096]{1,0:T(2,128)(2,1)} custom-call(f32[8,4096]{1,0:T(8,128)S(1)} %get-tuple-element.45.refs_0_, bf16[2,4096]{1,0:T(2,128)(2,1)S(1)} %collective-permute-done.11.refs_1_, bf16[2,4096]{1,0:T(2,128)(2,1)S(1)} %collective-permute-done.12.refs_2_, bf16[2,4096]{1,0:T(2,128)(2,1)S(1)} %collective-permute-done.13.refs_3_, ...), custom_call_target="tpu_custom_call" | custom-call | tf_op jit(solution)/shard_map/final_sum/pallas_call | solution.py:349
  (18 shorter events, 0.2 us)
Async XLA Ops:
  1.4 16.4 %slice-start = ((s8[14680064]{0:T(1024)(128)(4,1)}), s8[4194304]{0:T(1024)(128)(4,1)S(1)}, s32[]{:S(2)}) async-start(s8[14680064]{0:T(1024)(128)(4,1)} %bitcast), calls=%async_computation | async-start | bytes 8388608
  1.4 16.4 %slice-start.1 = ((s8[14680064]{0:T(1024)(128)(4,1)}), s8[4194304]{0:T(1024)(128)(4,1)S(1)}, s32[]{:S(2)}) async-start(s8[14680064]{0:T(1024)(128)(4,1)} %bitcast), calls=%async_computation.1 | async-start | bytes 8388608
  1.4 7.7 %collective-permute-start.2 = (bf16[2,2,4096]{2,1,0:T(2,128)(2,1)S(1)}, bf16[2,2,4096]{2,1,0:T(2,128)(2,1)S(1)}, u32[]{:S(2)}, u32[]{:S(2)}) collective-permute-start(bf16[2,2,4096]{2,1,0:T(2,128)(2,1)S(1)} %join.1.refs_0_), channel_id=1, source_target_pairs={{0,6},{1,7},{2,4},{3,5},{4,2},{5,3},{6,0},{7,1},{8,14},{9,15},{10,... | collective-permute-start | bytes 98312 | tf_op jit(solution)/shard_map/ppermute | solution.py:233
  5.4 3.9 %collective-permute-start.1 = (bf16[2,2,4096]{2,1,0:T(2,128)(2,1)S(1)}, bf16[2,2,4096]{2,1,0:T(2,128)(2,1)S(1)}, u32[]{:S(2)}, u32[]{:S(2)}) collective-permute-start(bf16[2,2,4096]{2,1,0:T(2,128)(2,1)S(1)} %join.1.refs_0_), channel_id=1, source_target_pairs={{0,4},{1,5},{2,6},{3,7},{4,0},{5,1},{6,2},{7,3},{8,12},{9,13},{10,... | collective-permute-start | bytes 98312 | tf_op jit(solution)/shard_map/ppermute | solution.py:233
  5.9 3.9 %collective-permute-start = (bf16[2,2,4096]{2,1,0:T(2,128)(2,1)S(1)}, bf16[2,2,4096]{2,1,0:T(2,128)(2,1)S(1)}, u32[]{:S(2)}, u32[]{:S(2)}) collective-permute-start(bf16[2,2,4096]{2,1,0:T(2,128)(2,1)S(1)} %join.1.refs_0_), channel_id=1, source_target_pairs={{0,2},{1,3},{2,0},{3,1},{4,6},{5,7},{6,4},{7,5},{8,10},{9,11},{10,... | collective-permute-start | bytes 98312 | tf_op jit(solution)/shard_map/ppermute | solution.py:233
  9.8 8.0 %slice-start.2 = ((s8[14680064]{0:T(1024)(128)(4,1)}), s8[4194304]{0:T(1024)(128)(4,1)S(1)}, s32[]{:S(2)}) async-start(s8[14680064]{0:T(1024)(128)(4,1)} %bitcast), calls=%async_computation.2 | async-start | bytes 8388608
  9.8 8.0 %slice-start.3 = ((s8[14680064]{0:T(1024)(128)(4,1)}), s8[2097152]{0:T(1024)(128)(4,1)S(1)}, s32[]{:S(2)}) async-start(s8[14680064]{0:T(1024)(128)(4,1)} %bitcast), calls=%async_computation.3 | async-start | bytes 4194304
  9.8 3.3 %collective-permute-start.3 = (bf16[4,2,2,4096]{3,2,1,0:T(2,128)(2,1)S(1)}, bf16[4,2,2,4096]{3,2,1,0:T(2,128)(2,1)S(1)}, u32[]{:S(2)}, u32[]{:S(2)}) collective-permute-start(bf16[4,2,2,4096]{3,2,1,0:T(2,128)(2,1)S(1)} %stack.1.refs_0_), channel_id=1, source_target_pairs={{0,1},{1,0},{2,3},{3,2},{4,5},{5,4},{6,7},{7,6},{8,9},{9,8},{10,11... | collective-permute-start | bytes 393224 | tf_op jit(solution)/shard_map/ppermute | solution.py:233
  13.4 15.8 %collective-permute-start.4 = (bf16[16,3072]{1,0:T(8,128)(2,1)S(1)}, bf16[16,3072]{1,0:T(8,128)(2,1)S(1)}, u32[]{:S(2)}, u32[]{:S(2)}) collective-permute-start(bf16[16,3072]{1,0:T(8,128)(2,1)S(1)} %get-tuple-element.34), channel_id=1, source_target_pairs={{0,8},{8,0},{16,24},{24,16},{1,9},{9,1},{17,25},{25,17},{2,10},{10... | collective-permute-start | bytes 294920 | tf_op jit(solution)/shard_map/ppermute | solution.py:233
  15.0 14.2 %collective-permute-start.5 = (bf16[16,3072]{1,0:T(8,128)(2,1)S(1)}, bf16[16,3072]{1,0:T(8,128)(2,1)S(1)}, u32[]{:S(2)}, u32[]{:S(2)}) collective-permute-start(bf16[16,3072]{1,0:T(8,128)(2,1)S(1)} %get-tuple-element.35), channel_id=1, source_target_pairs={{0,16},{8,24},{16,0},{24,8},{1,17},{9,25},{17,1},{25,9},{2,18},{10... | collective-permute-start | bytes 294920 | tf_op jit(solution)/shard_map/ppermute | solution.py:233
  17.6 11.6 %collective-permute-start.6 = (bf16[16,3072]{1,0:T(8,128)(2,1)S(1)}, bf16[16,3072]{1,0:T(8,128)(2,1)S(1)}, u32[]{:S(2)}, u32[]{:S(2)}) collective-permute-start(bf16[16,3072]{1,0:T(8,128)(2,1)S(1)} %get-tuple-element.36), channel_id=1, source_target_pairs={{0,24},{8,16},{16,8},{24,0},{1,25},{9,17},{17,9},{25,1},{2,26},{10... | collective-permute-start | bytes 294920 | tf_op jit(solution)/shard_map/ppermute | solution.py:233
  29.3 12.1 %collective-permute-start.7 = (bf16[2,16,1792]{2,1,0:T(8,128)(2,1)S(1)}, bf16[2,16,1792]{2,1,0:T(8,128)(2,1)S(1)}, u32[]{:S(2)}, u32[]{:S(2)}) collective-permute-start(bf16[2,16,1792]{2,1,0:T(8,128)(2,1)S(1)} %get-tuple-element.37), channel_id=1, source_target_pairs={{0,8},{8,0},{16,24},{24,16},{1,9},{9,1},{17,25},{25,17},{2,10},{10... | collective-permute-start | bytes 344072 | tf_op jit(solution)/shard_map/ppermute | solution.py:233
  30.0 12.2 %collective-permute-start.8 = (bf16[2,16,1792]{2,1,0:T(8,128)(2,1)S(1)}, bf16[2,16,1792]{2,1,0:T(8,128)(2,1)S(1)}, u32[]{:S(2)}, u32[]{:S(2)}) collective-permute-start(bf16[2,16,1792]{2,1,0:T(8,128)(2,1)S(1)} %get-tuple-element.38), channel_id=1, source_target_pairs={{0,16},{8,24},{16,0},{24,8},{1,17},{9,25},{17,1},{25,9},{2,18},{10... | collective-permute-start | bytes 344072 | tf_op jit(solution)/shard_map/ppermute | solution.py:233
  33.5 8.7 %collective-permute-start.9 = (bf16[2,16,1792]{2,1,0:T(8,128)(2,1)S(1)}, bf16[2,16,1792]{2,1,0:T(8,128)(2,1)S(1)}, u32[]{:S(2)}, u32[]{:S(2)}) collective-permute-start(bf16[2,16,1792]{2,1,0:T(8,128)(2,1)S(1)} %get-tuple-element.39), channel_id=1, source_target_pairs={{0,24},{8,16},{16,8},{24,0},{1,25},{9,17},{17,9},{25,1},{2,26},{10... | collective-permute-start | bytes 344072 | tf_op jit(solution)/shard_map/ppermute | solution.py:233
  42.3 1.3 %collective-permute-start.10 = (bf16[8,4096]{1,0:T(8,128)(2,1)S(1)}, bf16[8,4096]{1,0:T(8,128)(2,1)S(1)}, u32[]{:S(2)}, u32[]{:S(2)}) collective-permute-start(bf16[8,4096]{1,0:T(8,128)(2,1)S(1)} %hold.1), channel_id=1, source_target_pairs={{0,1},{1,0},{2,3},{3,2},{4,5},{5,4},{6,7},{7,6},{8,9},{9,8},{10,11... | collective-permute-start | bytes 196616 | tf_op jit(solution)/shard_map/ppermute | solution.py:233
  43.7 11.6 %collective-permute-start.13 = (bf16[2,4096]{1,0:T(2,128)(2,1)S(1)}, bf16[2,4096]{1,0:T(2,128)(2,1)S(1)}, u32[]{:S(2)}, u32[]{:S(2)}) collective-permute-start(bf16[2,4096]{1,0:T(2,128)(2,1)S(1)} %get-tuple-element.46), channel_id=1, source_target_pairs={{0,6},{1,7},{2,4},{3,5},{4,2},{5,3},{6,0},{7,1},{8,14},{9,15},{10,... | collective-permute-start | bytes 49160 | tf_op jit(solution)/shard_map/ppermute | solution.py:233
  46.1 9.1 %collective-permute-start.12 = (bf16[2,4096]{1,0:T(2,128)(2,1)S(1)}, bf16[2,4096]{1,0:T(2,128)(2,1)S(1)}, u32[]{:S(2)}, u32[]{:S(2)}) collective-permute-start(bf16[2,4096]{1,0:T(2,128)(2,1)S(1)} %get-tuple-element.47), channel_id=1, source_target_pairs={{0,4},{1,5},{2,6},{3,7},{4,0},{5,1},{6,2},{7,3},{8,12},{9,13},{10,... | collective-permute-start | bytes 49160 | tf_op jit(solution)/shard_map/ppermute | solution.py:233
  46.6 8.6 %collective-permute-start.11 = (bf16[2,4096]{1,0:T(2,128)(2,1)S(1)}, bf16[2,4096]{1,0:T(2,128)(2,1)S(1)}, u32[]{:S(2)}, u32[]{:S(2)}) collective-permute-start(bf16[2,4096]{1,0:T(2,128)(2,1)S(1)} %get-tuple-element.48), channel_id=1, source_target_pairs={{0,2},{1,3},{2,0},{3,1},{4,6},{5,7},{6,4},{7,5},{8,10},{9,11},{10,... | collective-permute-start | bytes 49160 | tf_op jit(solution)/shard_map/ppermute | solution.py:233

commit v4 on v3

--- a/solution.py
+++ b/solution.py
@@ -68,29 +68,32 @@
         copy.wait()
 
 
-def load_kernel(first, weight, after, out, token, sem):
-    copy = pltpu.make_async_copy(weight.at[pl.ds(first, out.shape[0])], out, sem)
+def load_kernel(first, count, weight, after, *refs):
+    out, token, sem = refs[-3:]
+    part = pl.ds(first, count)
+    copy = pltpu.make_async_copy(weight.at[part], out.at[part], sem)
     copy.start()
     token[...] = jnp.zeros(token.shape, token.dtype)
     copy.wait()
 
 
-def load_rows(weight, first, count, after, name):
+def load_rows(weight, first, count, after, held, name):
     return pl.pallas_call(
-        lambda *refs: load_kernel(first, *refs),
+        lambda *refs: load_kernel(first, count, *refs),
         out_shape=(
-            pltpu.VMEM((count, weight.shape[1]), weight.dtype),
+            pltpu.VMEM(weight.shape, weight.dtype),
             jax.ShapeDtypeStruct((8, 128), F32),
         ),
-        in_specs=[HBM_SPEC, ANY_SPEC],
+        in_specs=[HBM_SPEC, ANY_SPEC] + [VMEM_SPEC] * len(held),
         out_specs=(VMEM_SPEC, VMEM_SPEC),
+        input_output_aliases={2: 0} if held else {},
         scratch_shapes=[pltpu.SemaphoreType.DMA],
         compiler_params=pltpu.CompilerParams(vmem_limit_bytes=1 << 20),
         cost_estimate=pl.CostEstimate(
             flops=0, bytes_accessed=2 * count * weight.shape[1], transcendentals=0
         ),
         name=name,
-    )(weight, after)
+    )(weight, after, *held)
 
 
 def stack_kernel(*refs):
@@ -111,15 +114,15 @@
     )(*pieces, after)
 
 
-def arrange_kernel(n_dp, plane, other, after, tokens, *refs):
-    *columns, wide = refs
-    own = plane.shape[2]
+def arrange_kernel(n_dp, chips, *refs):
+    sources, (tokens, *columns, wide) = refs[:chips], refs[chips + 1 :]
+    own = sources[0].shape[2]
     unit = tokens.shape[2] // n_dp
     for i in range(2):
-        for slot in range(plane.shape[0]):
-            for half, source in enumerate((plane, other)):
-                start = (half * plane.shape[0] + slot) * own
-                wide[i, start : start + own] = source[slot, i].astype(F32)
+        for slot, source in enumerate(sources):
+            for core in range(2):
+                start = (core * chips + slot) * own
+                wide[i, start : start + own] = source[core, i].astype(F32)
         tokens[i] = wide[i].astype(BF)
     for step, out in enumerate(columns):
         owner = lax.axis_index("dp") ^ step
@@ -129,22 +132,20 @@
             out[:, j * unit : (j + 1) * unit] = tokens[lax.div(index, 2 * n_dp), :, part]
 
 
-def forward_kernel(chunk, tokens, gate_a, gate_b, down, up_hbm, grads, up, _a, _b, gate_pre, grad_hidden, sem):
-    half, columns = gate_a.shape
+def forward_kernel(chunk, tokens, gate, down, up_hbm, grads, up, _, gate_pre, grad_hidden, sem):
+    rows, columns = gate.shape
     parts = [slice(start, start + chunk) for start in range(0, columns, chunk)]
+    piece = rows // sem.shape[0]
     copies = [
         pltpu.make_async_copy(
-            up_hbm.at[pl.ds(i * half, half)], up.at[pl.ds(i * half, half)], sem.at[i]
+            up_hbm.at[pl.ds(i * piece, piece)], up.at[pl.ds(i * piece, piece)], sem.at[i]
         )
-        for i in range(2)
+        for i in range(sem.shape[0])
     ]
     for copy in copies:
-        copy.start()
+        copy.start(priority=1)
     for part in parts:
-        gate_pre[:, part] = dot(tokens[0, :, :half], gate_a[:, part], NN) + dot(
-            tokens[0, :, half:], gate_b[:, part], NN
-        )
-    for part in parts:
+        gate_pre[:, part] = dot(tokens[0], gate[:, part], NN)
         grad_hidden[:, part] = dot(tokens[1], down[part, :], NT)
     for copy in copies:
         copy.wait()
@@ -167,17 +168,13 @@
         pack[1] = grads[lax.div(3 * owner + 2, n_dp)]
 
 
-def backward_kernel(chunk, grads, gate_a, gate_b, up_all, keep, send):
-    half = gate_a.shape[0]
+def backward_kernel(chunk, grads, gate, up, keep, send):
     rows = keep.shape[0]
-    for gate, base in ((gate_a, 0), (gate_b, half)):
-        for start in range(0, half, chunk):
-            part = slice(start, start + chunk)
-            total = dot(grads[0], gate[part, :], NT) + dot(
-                grads[1], up_all[base + start : base + start + chunk, :], NT
-            )
-            keep[:, base + start : base + start + chunk] = total[:rows]
-            send[:, base + start : base + start + chunk] = total[rows:].astype(BF)
+    for start in range(0, gate.shape[0], chunk):
+        part = slice(start, start + chunk)
+        total = dot(grads[0], gate[part, :], NT) + dot(grads[1], up[part, :], NT)
+        keep[:, part] = total[:rows]
+        send[:, part] = total[rows:].astype(BF)
 
 
 def product_kernel(n_dp, pieces, *refs):
@@ -224,7 +221,7 @@
     hidden = gate_weight.shape[1]
     group = own * n_node
     block = 3 * width // n_dp
-    half = width // 2
+    half, quarter = width // 2, width // 4
     chips = range(2, n_node, 2)
     groups = range(1, n_dp)
     weight_bytes = 2 * width * hidden
@@ -242,47 +239,48 @@
         name="join",
     )(in_hbm(normed), in_hbm(cotangent))
     gate_hbm, up_hbm = in_hbm(gate_weight), in_hbm(up_weight)
-    plane = [mine] + [permute(mine, "node", s) for s in chips]
-    gate_a, token = load_rows(gate_hbm, 0, half, in_hbm(normed), "load_gate_a")
-    plane = glue(stack_kernel, (len(plane), 2, own, width), plane, token, "stack")
-    other = permute(plane, "node", 1)
-    gate_b, token = load_rows(gate_hbm, half, half, token, "load_gate_b")
+    other = permute(mine, "node", 1)
+    gate, token = load_rows(gate_hbm, 0, quarter, in_hbm(normed), (), "load_gate_a")
+    pair = glue(stack_kernel, (2, 2, own, width), [mine, other], token, "stack")
+    plane = [pair] + [permute(pair, "node", s) for s in chips]
+    gate, token = load_rows(
+        gate_hbm, quarter, width - quarter, token, (in_vmem(gate),), "load_gate_b"
+    )
     piece = jax.ShapeDtypeStruct((group, block), BF)
     tokens, *columns = pl.pallas_call(
-        lambda *refs: arrange_kernel(n_dp, *refs),
+        lambda *refs: arrange_kernel(n_dp, len(plane), *refs),
         out_shape=[jax.ShapeDtypeStruct((2, group, width), BF)] + [piece] * n_dp,
-        in_specs=[VMEM_SPEC] * 2 + [ANY_SPEC],
+        in_specs=[VMEM_SPEC] * len(plane) + [ANY_SPEC],
         out_specs=[VMEM_SPEC] * (n_dp + 1),
         scratch_shapes=[pltpu.VMEM((2, group, width), F32)],
         compiler_params=pltpu.CompilerParams(vmem_limit_bytes=4 << 20),
         cost_estimate=pl.CostEstimate(flops=0, bytes_accessed=1 << 20, transcendentals=0),
         name="arrange",
-    )(plane, other, token)
+    )(*plane, token)
     columns = [columns[0]] + [permute(columns[s], "dp", s) for s in groups]
 
     chunk = 256
-    grads, up, gate_a, gate_b = pl.pallas_call(
+    grads, up, gate = pl.pallas_call(
         lambda *refs: forward_kernel(chunk, *refs),
         out_shape=[
             jax.ShapeDtypeStruct((3, group, hidden), BF),
             pltpu.VMEM((width, hidden), BF),
-            pltpu.VMEM((half, hidden), BF),
-            pltpu.VMEM((half, hidden), BF),
+            pltpu.VMEM((width, hidden), BF),
         ],
-        in_specs=[VMEM_SPEC] * 4 + [HBM_SPEC],
-        out_specs=[VMEM_SPEC] * 4,
-        input_output_aliases={1: 2, 2: 3},
+        in_specs=[VMEM_SPEC] * 3 + [HBM_SPEC],
+        out_specs=[VMEM_SPEC] * 3,
+        input_output_aliases={1: 2},
         scratch_shapes=[
             pltpu.VMEM((group, hidden), F32),
             pltpu.VMEM((group, hidden), F32),
-            pltpu.SemaphoreType.DMA((2,)),
+            pltpu.SemaphoreType.DMA((8,)),
         ],
         compiler_params=pltpu.CompilerParams(vmem_limit_bytes=4 << 20),
         cost_estimate=pl.CostEstimate(
             flops=6 * group * width * hidden, bytes_accessed=2 * weight_bytes, transcendentals=0
         ),
         name="forward",
-    )(tokens, in_vmem(gate_a), in_vmem(gate_b), in_vmem(down_weight), up_hbm)
+    )(tokens, in_vmem(gate), in_vmem(down_weight), up_hbm)
 
     packs = pl.pallas_call(
         lambda *refs: pack_kernel(n_dp, *refs),
@@ -300,14 +298,14 @@
             jax.ShapeDtypeStruct((group // 2, width), F32),
             jax.ShapeDtypeStruct((group // 2, width), BF),
         ),
-        in_specs=[VMEM_SPEC] * 4,
+        in_specs=[VMEM_SPEC] * 3,
         out_specs=(VMEM_SPEC, VMEM_SPEC),
         compiler_params=pltpu.CompilerParams(vmem_limit_bytes=4 << 20),
         cost_estimate=pl.CostEstimate(
             flops=4 * group * width * hidden, bytes_accessed=2 * weight_bytes, transcendentals=0
         ),
         name="backward",
-    )(grads, in_vmem(gate_a), in_vmem(gate_b), in_vmem(up))
+    )(grads, in_vmem(gate), in_vmem(up))
 
     send = pl.pallas_call(
         hold_kernel,

time: 56.3 us -> 52.6 us (0.934)
  Pallas kernels: 35 us -> 32.3 us
  waiting for transfers between devices: 2.79 us -> 1.56 us
    pallas_call x1, Pallas kernels: 11.3 us -> 8.52 us  [shards_group(): pl.pallas_call(lambda *refs: forward_kernel(chunk, *refs), out_shape=[jax...]
    ppermute x14, waiting for transfers between devices: 2.79 us -> 1.56 us  [permute(): lax.ppermute(array, axis, xor_pairs(mesh_shape[axis == 'node'], step))]
  transfers between devices with their start and end apart: 14 -> 14, of which waited for: 4 -> 2; matrix products, arithmetic and copies ran while one was open for 0% -> 0% of each run, Pallas kernels for 60% -> 59%
where the time goes in v4:
time: 52.6 us; the launch traced here: 52.2 us
  Pallas kernels  32.3 us (61%)
  starting transfers between devices  17.4 us (33%)
  waiting for transfers between devices  1.56 us (3%)
  between operations  0.83 us (2%)
    ppermute x14, starting transfers between devices, permute(): lax.ppermute(array, axis, xor_pairs(mesh_shape[axis == 'node'], step))  17.4 us
    pallas_call x1, Pallas kernels, shards_group(): pl.pallas_call(lambda *refs: forward_kernel(chunk, *refs), out_shape=[jax...  8.52 us
    pallas_call x1, Pallas kernels, shards_group(): pl.pallas_call(lambda *refs: product_kernel(n_dp, cuts, *refs), out_shape...  8.01 us
    pallas_call x1, Pallas kernels, shards_group(): pl.pallas_call(lambda *refs: backward_kernel(chunk, *refs), out_shape=(ja...  7.65 us
    pallas_call x2, Pallas kernels, load_rows(): pl.pallas_call(lambda *refs: load_kernel(first, count, *refs), out_shape=...  6.48 us
    ppermute x14, waiting for transfers between devices, permute(): lax.ppermute(array, axis, xor_pairs(mesh_shape[axis == 'node'], step))  1.56 us
  transfers between devices with their start and end apart: 14, of which 2 were waited for; matrix products, arithmetic and copies ran while one was open for 0% of the time, Pallas kernels for 59%

profile of v4, /device:TPU:0, one launch (start us, length us, event | category | flops | bytes accessed | tf_op | source)
XLA Modules:
  0.0 52.2 jit_solution(12586446942223123951)
XLA Ops:
  0.6 0.8 %join.1.refs_0_ = bf16[2,2,4096]{2,1,0:T(2,128)(2,1)S(1)} custom-call(bf16[2,4096]{1,0:T(2,128)(2,1)} %refs_1_.1, bf16[2,4096]{1,0:T(2,128)(2,1)} %cotangent.1), custom_call_target="tpu_custom_call" | custom-call | tf_op jit(solution)/shard_map/join/pallas_call | solution.py:232
  1.4 0.5 collective-permute-start
  1.9 2.2 %load_gate_a.1 = (bf16[4096,1792]{1,0:T(8,128)(2,1)S(1)}, f32[8,128]{1,0:T(8,128)S(1)}) custom-call(bf16[4096,1792]{1,0:T(8,128)(2,1)} %refs_0_.3, bf16[2,4096]{1,0:T(2,128)(2,1)} %refs_1_.1), custom_call_target="tpu_custom_call" | custom-call | bytes 3670016 | tf_op jit(solution)/shard_map/load_gate_a/pallas_call | solution.py:81
  4.1 0.0 collective-permute-done.refs_1_
  4.1 3.5 %collective-permute-start.3 = (bf16[2,2,2,4096]{3,2,1,0:T(2,128)(2,1)S(1)}, bf16[2,2,2,4096]{3,2,1,0:T(2,128)(2,1)S(1)}, u32[]{:S(2)}, u32[]{:S(2)}) collective-permute-start(bf16[2,2,2,4096]{3,2,1,0:T(2,128)(2,1)S(1)} %stack.1.refs_0_), channel_id=1, source_target_pairs={{0,6},{1,7},{2,4},{3,5},{4,2},{5,3},{6,0},{7,1},{8,14},{9,15},{10,... | collective-permute-start | bytes 196616 | tf_op jit(solution)/shard_map/ppermute | solution.py:230
  7.7 0.5 collective-permute-start.2
  8.2 0.1 collective-permute-start.1
  8.3 4.3 %load_gate_b.1 = (bf16[4096,1792]{1,0:T(8,128)(2,1)S(1)}, f32[8,128]{1,0:T(8,128)S(1)}) custom-call(bf16[4096,1792]{1,0:T(8,128)(2,1)} %refs_0_.3, f32[8,128]{1,0:T(8,128)S(1)} %get-tuple-element.22.refs_2_.refs_1_, bf16[4096,1792]{1,0:T(8,128)(2,1)S(1)} %get-tuple-element.23.refs_2_), custom_call_target="tpu_custom_call", output_to_operand_aliasing={{0}: (2, {})} | custom-call | bytes 11010048 | tf_op jit(solution)/shard_map/load_gate_b/pallas_call | solution.py:81
  12.6 0.0 collective-permute-done.3.refs_3_
  12.6 0.0 collective-permute-done.2.refs_2_
  12.7 0.0 collective-permute-done.1.refs_1_
  12.7 0.2 arrange.1
  12.9 2.0 %collective-permute-start.4 = (bf16[16,3072]{1,0:T(8,128)(2,1)S(1)}, bf16[16,3072]{1,0:T(8,128)(2,1)S(1)}, u32[]{:S(2)}, u32[]{:S(2)}) collective-permute-start(bf16[16,3072]{1,0:T(8,128)(2,1)S(1)} %get-tuple-element.32), channel_id=1, source_target_pairs={{0,8},{8,0},{16,24},{24,16},{1,9},{9,1},{17,25},{25,17},{2,10},{10... | collective-permute-start | bytes 294920 | tf_op jit(solution)/shard_map/ppermute | solution.py:230
  14.9 2.6 %collective-permute-start.5 = (bf16[16,3072]{1,0:T(8,128)(2,1)S(1)}, bf16[16,3072]{1,0:T(8,128)(2,1)S(1)}, u32[]{:S(2)}, u32[]{:S(2)}) collective-permute-start(bf16[16,3072]{1,0:T(8,128)(2,1)S(1)} %get-tuple-element.33), channel_id=1, source_target_pairs={{0,16},{8,24},{16,0},{24,8},{1,17},{9,25},{17,1},{25,9},{2,18},{10... | collective-permute-start | bytes 294920 | tf_op jit(solution)/shard_map/ppermute | solution.py:230
  17.5 0.0 collective-permute-start.6
  17.5 8.5 %forward.1 = (bf16[3,16,1792]{2,1,0:T(8,128)(2,1)S(1)}, bf16[4096,1792]{1,0:T(8,128)(2,1)S(1)}, bf16[4096,1792]{1,0:T(8,128)(2,1)S(1)}) custom-call(bf16[2,16,4096]{2,1,0:T(8,128)(2,1)S(1)} %get-tuple-element.25.refs_0_, bf16[4096,1792]{1,0:T(8,128)(2,1)S(1)} %get-tuple-element.26.refs_1_, ...), custom_call_target="tpu_custom_call", output_to_operand_aliasing={{2}: (1, {})} | custom-call | flops 704643072 | bytes 29360128 | tf_op jit(solution)/shard_map/forward/pallas_call | solution.py:263
  26.1 0.0 collective-permute-done.4.refs_1_
  26.1 0.0 collective-permute-done.6.refs_3_
  26.2 0.9 %collective-permute-start.7 = (bf16[2,16,1792]{2,1,0:T(8,128)(2,1)S(1)}, bf16[2,16,1792]{2,1,0:T(8,128)(2,1)S(1)}, u32[]{:S(2)}, u32[]{:S(2)}) collective-permute-start(bf16[2,16,1792]{2,1,0:T(8,128)(2,1)S(1)} %get-tuple-element.35), channel_id=1, source_target_pairs={{0,8},{8,0},{16,24},{24,16},{1,9},{9,1},{17,25},{25,17},{2,10},{10... | collective-permute-start | bytes 344072 | tf_op jit(solution)/shard_map/ppermute | solution.py:230
  27.1 3.5 %collective-permute-start.8 = (bf16[2,16,1792]{2,1,0:T(8,128)(2,1)S(1)}, bf16[2,16,1792]{2,1,0:T(8,128)(2,1)S(1)}, u32[]{:S(2)}, u32[]{:S(2)}) collective-permute-start(bf16[2,16,1792]{2,1,0:T(8,128)(2,1)S(1)} %get-tuple-element.36), channel_id=1, source_target_pairs={{0,16},{8,24},{16,0},{24,8},{1,17},{9,25},{17,1},{25,9},{2,18},{10... | collective-permute-start | bytes 344072 | tf_op jit(solution)/shard_map/ppermute | solution.py:230
  30.6 0.0 collective-permute-start.9
  30.6 7.7 %backward.1 = (f32[8,4096]{1,0:T(8,128)S(1)}, bf16[8,4096]{1,0:T(8,128)(2,1)S(1)}) custom-call(bf16[3,16,1792]{2,1,0:T(8,128)(2,1)S(1)} %get-tuple-element.27.refs_0_, bf16[4096,1792]{1,0:T(8,128)(2,1)S(1)} %get-tuple-element.28.refs_1_, bf16[4096,1792]{1,0:T(8,128)(2,1)S(1)} %get-tuple-element.29.refs_2_), custom_call_target="tpu_custom_call" | custom-call | flops 469762048 | bytes 29360128 | tf_op jit(solution)/shard_map/backward/pallas_call | solution.py:295
  38.3 0.3 collective-permute-done.8.refs_1_.refs_6_
  38.6 0.0 collective-permute-done.9.refs_2_.refs_7_
  38.6 0.1 collective-permute-start.10
  38.6 1.2 %collective-permute-done.10 = bf16[8,4096]{1,0:T(8,128)(2,1)S(1)} collective-permute-done((bf16[8,4096]{1,0:T(8,128)(2,1)S(1)}, bf16[8,4096]{1,0:T(8,128)(2,1)S(1)}, u32[]{:S(2)}, u32[]{:S(2)}) %collective-permute-start.10) | collective-permute-done | bytes 65568 | tf_op jit(solution)/shard_map/ppermute | solution.py:230
  40.0 2.5 %collective-permute-start.13 = (bf16[2,4096]{1,0:T(2,128)(2,1)S(1)}, bf16[2,4096]{1,0:T(2,128)(2,1)S(1)}, u32[]{:S(2)}, u32[]{:S(2)}) collective-permute-start(bf16[2,4096]{1,0:T(2,128)(2,1)S(1)} %get-tuple-element.44), channel_id=1, source_target_pairs={{0,6},{1,7},{2,4},{3,5},{4,2},{5,3},{6,0},{7,1},{8,14},{9,15},{10,... | collective-permute-start | bytes 49160 | tf_op jit(solution)/shard_map/ppermute | solution.py:230
  42.5 0.5 collective-permute-start.12
  43.0 0.5 %collective-permute-start.11 = (bf16[2,4096]{1,0:T(2,128)(2,1)S(1)}, bf16[2,4096]{1,0:T(2,128)(2,1)S(1)}, u32[]{:S(2)}, u32[]{:S(2)}) collective-permute-start(bf16[2,4096]{1,0:T(2,128)(2,1)S(1)} %get-tuple-element.46), channel_id=1, source_target_pairs={{0,2},{1,3},{2,0},{3,1},{4,6},{5,7},{6,4},{7,5},{8,10},{9,11},{10,... | collective-permute-start | bytes 49160 | tf_op jit(solution)/shard_map/ppermute | solution.py:230
  43.5 8.0 %product.1 = (f32[3072,1792]{1,0:T(8,128)}, f32[8,128]{1,0:T(8,128)S(1)}) custom-call(bf16[16,3072]{1,0:T(8,128)(2,1)S(1)} %get-tuple-element.38.refs_0_, bf16[16,3072]{1,0:T(8,128)(2,1)S(1)} %collective-permute-done.4.refs_1_, bf16[16,3072]{1,0:T(8,128)(2,1)S(1)} %collective-permute-done.5.refs_2_, bf16[16,3072]{1,0:T(8,128)(2,1)S(1)} %collective-permute-done.6.refs_3_, ...), custom_call_target="tpu_custom_call" | custom-call | flops 704643072 | bytes 22020096 | tf_op jit(solution)/shard_map/product/pallas_call | solution.py:325
  51.5 0.0 collective-permute-done.13.refs_3_
  51.6 0.7 %final_sum.1 = bf16[2,4096]{1,0:T(2,128)(2,1)} custom-call(f32[8,4096]{1,0:T(8,128)S(1)} %get-tuple-element.43.refs_0_, bf16[2,4096]{1,0:T(2,128)(2,1)S(1)} %collective-permute-done.11.refs_1_, bf16[2,4096]{1,0:T(2,128)(2,1)S(1)} %collective-permute-done.12.refs_2_, bf16[2,4096]{1,0:T(2,128)(2,1)S(1)} %collective-permute-done.13.refs_3_, ...), custom_call_target="tpu_custom_call" | custom-call | tf_op jit(solution)/shard_map/final_sum/pallas_call | solution.py:347
  (18 shorter events, 0.2 us)
Async XLA Ops:
  1.4 2.7 %collective-permute-start = (bf16[2,2,4096]{2,1,0:T(2,128)(2,1)S(1)}, bf16[2,2,4096]{2,1,0:T(2,128)(2,1)S(1)}, u32[]{:S(2)}, u32[]{:S(2)}) collective-permute-start(bf16[2,2,4096]{2,1,0:T(2,128)(2,1)S(1)} %join.1.refs_0_), channel_id=1, source_target_pairs={{0,1},{1,0},{2,3},{3,2},{4,5},{5,4},{6,7},{7,6},{8,9},{9,8},{10,11... | collective-permute-start | bytes 98312 | tf_op jit(solution)/shard_map/ppermute | solution.py:230
  1.9 15.6 %slice-start = ((s8[14680064]{0:T(1024)(128)(4,1)}), s8[4194304]{0:T(1024)(128)(4,1)S(1)}, s32[]{:S(2)}) async-start(s8[14680064]{0:T(1024)(128)(4,1)} %bitcast), calls=%async_computation | async-start | bytes 8388608
  1.9 15.6 %slice-start.1 = ((s8[14680064]{0:T(1024)(128)(4,1)}), s8[4194304]{0:T(1024)(128)(4,1)S(1)}, s32[]{:S(2)}) async-start(s8[14680064]{0:T(1024)(128)(4,1)} %bitcast), calls=%async_computation.1 | async-start | bytes 8388608
  4.1 8.5 %collective-permute-start.3 = (bf16[2,2,2,4096]{3,2,1,0:T(2,128)(2,1)S(1)}, bf16[2,2,2,4096]{3,2,1,0:T(2,128)(2,1)S(1)}, u32[]{:S(2)}, u32[]{:S(2)}) collective-permute-start(bf16[2,2,2,4096]{3,2,1,0:T(2,128)(2,1)S(1)} %stack.1.refs_0_), channel_id=1, source_target_pairs={{0,6},{1,7},{2,4},{3,5},{4,2},{5,3},{6,0},{7,1},{8,14},{9,15},{10,... | collective-permute-start | bytes 196616 | tf_op jit(solution)/shard_map/ppermute | solution.py:230
  7.7 5.0 %collective-permute-start.2 = (bf16[2,2,2,4096]{3,2,1,0:T(2,128)(2,1)S(1)}, bf16[2,2,2,4096]{3,2,1,0:T(2,128)(2,1)S(1)}, u32[]{:S(2)}, u32[]{:S(2)}) collective-permute-start(bf16[2,2,2,4096]{3,2,1,0:T(2,128)(2,1)S(1)} %stack.1.refs_0_), channel_id=1, source_target_pairs={{0,4},{1,5},{2,6},{3,7},{4,0},{5,1},{6,2},{7,3},{8,12},{9,13},{10,... | collective-permute-start | bytes 196616 | tf_op jit(solution)/shard_map/ppermute | solution.py:230
  8.2 4.5 %collective-permute-start.1 = (bf16[2,2,2,4096]{3,2,1,0:T(2,128)(2,1)S(1)}, bf16[2,2,2,4096]{3,2,1,0:T(2,128)(2,1)S(1)}, u32[]{:S(2)}, u32[]{:S(2)}) collective-permute-start(bf16[2,2,2,4096]{3,2,1,0:T(2,128)(2,1)S(1)} %stack.1.refs_0_), channel_id=1, source_target_pairs={{0,2},{1,3},{2,0},{3,1},{4,6},{5,7},{6,4},{7,5},{8,10},{9,11},{10,... | collective-permute-start | bytes 196616 | tf_op jit(solution)/shard_map/ppermute | solution.py:230
  8.3 9.2 %slice-start.2 = ((s8[14680064]{0:T(1024)(128)(4,1)}), s8[4194304]{0:T(1024)(128)(4,1)S(1)}, s32[]{:S(2)}) async-start(s8[14680064]{0:T(1024)(128)(4,1)} %bitcast), calls=%async_computation.2 | async-start | bytes 8388608
  8.3 9.2 %slice-start.3 = ((s8[14680064]{0:T(1024)(128)(4,1)}), s8[2097152]{0:T(1024)(128)(4,1)S(1)}, s32[]{:S(2)}) async-start(s8[14680064]{0:T(1024)(128)(4,1)} %bitcast), calls=%async_computation.3 | async-start | bytes 4194304
  12.9 13.2 %collective-permute-start.4 = (bf16[16,3072]{1,0:T(8,128)(2,1)S(1)}, bf16[16,3072]{1,0:T(8,128)(2,1)S(1)}, u32[]{:S(2)}, u32[]{:S(2)}) collective-permute-start(bf16[16,3072]{1,0:T(8,128)(2,1)S(1)} %get-tuple-element.32), channel_id=1, source_target_pairs={{0,8},{8,0},{16,24},{24,16},{1,9},{9,1},{17,25},{25,17},{2,10},{10... | collective-permute-start | bytes 294920 | tf_op jit(solution)/shard_map/ppermute | solution.py:230
  14.9 11.2 %collective-permute-start.5 = (bf16[16,3072]{1,0:T(8,128)(2,1)S(1)}, bf16[16,3072]{1,0:T(8,128)(2,1)S(1)}, u32[]{:S(2)}, u32[]{:S(2)}) collective-permute-start(bf16[16,3072]{1,0:T(8,128)(2,1)S(1)} %get-tuple-element.33), channel_id=1, source_target_pairs={{0,16},{8,24},{16,0},{24,8},{1,17},{9,25},{17,1},{25,9},{2,18},{10... | collective-permute-start | bytes 294920 | tf_op jit(solution)/shard_map/ppermute | solution.py:230
  17.5 8.6 %collective-permute-start.6 = (bf16[16,3072]{1,0:T(8,128)(2,1)S(1)}, bf16[16,3072]{1,0:T(8,128)(2,1)S(1)}, u32[]{:S(2)}, u32[]{:S(2)}) collective-permute-start(bf16[16,3072]{1,0:T(8,128)(2,1)S(1)} %get-tuple-element.34), channel_id=1, source_target_pairs={{0,24},{8,16},{16,8},{24,0},{1,25},{9,17},{17,9},{25,1},{2,26},{10... | collective-permute-start | bytes 294920 | tf_op jit(solution)/shard_map/ppermute | solution.py:230
  26.2 12.1 %collective-permute-start.7 = (bf16[2,16,1792]{2,1,0:T(8,128)(2,1)S(1)}, bf16[2,16,1792]{2,1,0:T(8,128)(2,1)S(1)}, u32[]{:S(2)}, u32[]{:S(2)}) collective-permute-start(bf16[2,16,1792]{2,1,0:T(8,128)(2,1)S(1)} %get-tuple-element.35), channel_id=1, source_target_pairs={{0,8},{8,0},{16,24},{24,16},{1,9},{9,1},{17,25},{25,17},{2,10},{10... | collective-permute-start | bytes 344072 | tf_op jit(solution)/shard_map/ppermute | solution.py:230
  27.1 11.5 %collective-permute-start.8 = (bf16[2,16,1792]{2,1,0:T(8,128)(2,1)S(1)}, bf16[2,16,1792]{2,1,0:T(8,128)(2,1)S(1)}, u32[]{:S(2)}, u32[]{:S(2)}) collective-permute-start(bf16[2,16,1792]{2,1,0:T(8,128)(2,1)S(1)} %get-tuple-element.36), channel_id=1, source_target_pairs={{0,16},{8,24},{16,0},{24,8},{1,17},{9,25},{17,1},{25,9},{2,18},{10... | collective-permute-start | bytes 344072 | tf_op jit(solution)/shard_map/ppermute | solution.py:230
  30.6 8.0 %collective-permute-start.9 = (bf16[2,16,1792]{2,1,0:T(8,128)(2,1)S(1)}, bf16[2,16,1792]{2,1,0:T(8,128)(2,1)S(1)}, u32[]{:S(2)}, u32[]{:S(2)}) collective-permute-start(bf16[2,16,1792]{2,1,0:T(8,128)(2,1)S(1)} %get-tuple-element.37), channel_id=1, source_target_pairs={{0,24},{8,16},{16,8},{24,0},{1,25},{9,17},{17,9},{25,1},{2,26},{10... | collective-permute-start | bytes 344072 | tf_op jit(solution)/shard_map/ppermute | solution.py:230
  38.6 1.3 %collective-permute-start.10 = (bf16[8,4096]{1,0:T(8,128)(2,1)S(1)}, bf16[8,4096]{1,0:T(8,128)(2,1)S(1)}, u32[]{:S(2)}, u32[]{:S(2)}) collective-permute-start(bf16[8,4096]{1,0:T(8,128)(2,1)S(1)} %hold.1), channel_id=1, source_target_pairs={{0,1},{1,0},{2,3},{3,2},{4,5},{5,4},{6,7},{7,6},{8,9},{9,8},{10,11... | collective-permute-start | bytes 196616 | tf_op jit(solution)/shard_map/ppermute | solution.py:230
  40.0 11.6 %collective-permute-start.13 = (bf16[2,4096]{1,0:T(2,128)(2,1)S(1)}, bf16[2,4096]{1,0:T(2,128)(2,1)S(1)}, u32[]{:S(2)}, u32[]{:S(2)}) collective-permute-start(bf16[2,4096]{1,0:T(2,128)(2,1)S(1)} %get-tuple-element.44), channel_id=1, source_target_pairs={{0,6},{1,7},{2,4},{3,5},{4,2},{5,3},{6,0},{7,1},{8,14},{9,15},{10,... | collective-permute-start | bytes 49160 | tf_op jit(solution)/shard_map/ppermute | solution.py:230
  42.5 9.1 %collective-permute-start.12 = (bf16[2,4096]{1,0:T(2,128)(2,1)S(1)}, bf16[2,4096]{1,0:T(2,128)(2,1)S(1)}, u32[]{:S(2)}, u32[]{:S(2)}) collective-permute-start(bf16[2,4096]{1,0:T(2,128)(2,1)S(1)} %get-tuple-element.45), channel_id=1, source_target_pairs={{0,4},{1,5},{2,6},{3,7},{4,0},{5,1},{6,2},{7,3},{8,12},{9,13},{10,... | collective-permute-start | bytes 49160 | tf_op jit(solution)/shard_map/ppermute | solution.py:230
  43.0 8.6 %collective-permute-start.11 = (bf16[2,4096]{1,0:T(2,128)(2,1)S(1)}, bf16[2,4096]{1,0:T(2,128)(2,1)S(1)}, u32[]{:S(2)}, u32[]{:S(2)}) collective-permute-start(bf16[2,4096]{1,0:T(2,128)(2,1)S(1)} %get-tuple-element.46), channel_id=1, source_target_pairs={{0,2},{1,3},{2,0},{3,1},{4,6},{5,7},{6,4},{7,5},{8,10},{9,11},{10,... | collective-permute-start | bytes 49160 | tf_op jit(solution)/shard_map/ppermute | solution.py:230

commit v5 on v4

--- a/solution.py
+++ b/solution.py
@@ -57,17 +57,6 @@
     return grad_normed, weight_grads
 
 
-def join_kernel(normed, cotangent, out, sem):
-    copies = [
-        pltpu.make_async_copy(source, out.at[i], sem.at[i])
-        for i, source in enumerate((normed, cotangent))
-    ]
-    for copy in copies:
-        copy.start()
-    for copy in copies:
-        copy.wait()
-
-
 def load_kernel(first, count, weight, after, *refs):
     out, token, sem = refs[-3:]
     part = pl.ds(first, count)
@@ -96,10 +85,11 @@
     )(weight, after, *held)
 
 
-def stack_kernel(*refs):
-    *pieces, after, out = refs
-    for slot, piece in enumerate(pieces):
-        out[slot] = piece[...]
+def pair_kernel(normed, cotangent, other_normed, other_cotangent, after, out):
+    out[0, 0] = normed[...]
+    out[0, 1] = cotangent[...]
+    out[1, 0] = other_normed[...]
+    out[1, 1] = other_cotangent[...]
 
 
 def glue(kernel, shape, pieces, after, name):
@@ -229,19 +219,12 @@
     def permute(array, axis, step):
         return lax.ppermute(array, axis, xor_pairs(mesh_shape[axis == "node"], step))
 
-    mine = pl.pallas_call(
-        join_kernel,
-        out_shape=jax.ShapeDtypeStruct((2, own, width), BF),
-        in_specs=[HBM_SPEC] * 2,
-        out_specs=VMEM_SPEC,
-        scratch_shapes=[pltpu.SemaphoreType.DMA((2,))],
-        compiler_params=pltpu.CompilerParams(vmem_limit_bytes=1 << 20),
-        name="join",
-    )(in_hbm(normed), in_hbm(cotangent))
     gate_hbm, up_hbm = in_hbm(gate_weight), in_hbm(up_weight)
-    other = permute(mine, "node", 1)
+    others = [permute(array, "node", 1) for array in (normed, cotangent)]
     gate, token = load_rows(gate_hbm, 0, quarter, in_hbm(normed), (), "load_gate_a")
-    pair = glue(stack_kernel, (2, 2, own, width), [mine, other], token, "stack")
+    pair = glue(
+        pair_kernel, (2, 2, own, width), [normed, cotangent, *others], token, "pair"
+    )
     plane = [pair] + [permute(pair, "node", s) for s in chips]
     gate, token = load_rows(
         gate_hbm, quarter, width - quarter, token, (in_vmem(gate),), "load_gate_b"

time: 52.6 us -> 51.9 us (0.987)
  Pallas kernels: 32.3 us -> 31.6 us
    pallas_call x1 -> x0, Pallas kernels: 0.75 us -> none  [shards_group(): pl.pallas_call(join_kernel, out_shape=jax.ShapeDtypeStruct((2, own, width...]
    ppermute x14 -> x15, starting transfers between devices: 17.4 us -> 17.9 us  [permute(): lax.ppermute(array, axis, xor_pairs(mesh_shape[axis == 'node'], step))]
    ppermute x14 -> x15, waiting for transfers between devices: 1.56 us -> 1.29 us  [permute(): lax.ppermute(array, axis, xor_pairs(mesh_shape[axis == 'node'], step))]
  transfers between devices with their start and end apart: 14 -> 15, of which waited for: 2 -> 1; matrix products, arithmetic and copies ran while one was open for 0% -> 0% of each run, Pallas kernels for 59% -> 59%
where the time goes in v5:
time: 51.9 us; the launch traced here: 51.7 us
  Pallas kernels  31.6 us (61%)
  starting transfers between devices  17.9 us (34%)
  waiting for transfers between devices  1.29 us (2%)
  between operations  0.88 us (2%)
    ppermute x15, starting transfers between devices, permute(): lax.ppermute(array, axis, xor_pairs(mesh_shape[axis == 'node'], step))  17.9 us
    pallas_call x1, Pallas kernels, shards_group(): pl.pallas_call(lambda *refs: forward_kernel(chunk, *refs), out_shape=[jax...  8.52 us
    pallas_call x1, Pallas kernels, shards_group(): pl.pallas_call(lambda *refs: product_kernel(n_dp, cuts, *refs), out_shape...  8.01 us
    pallas_call x1, Pallas kernels, shards_group(): pl.pallas_call(lambda *refs: backward_kernel(chunk, *refs), out_shape=(ja...  7.65 us
    pallas_call x2, Pallas kernels, load_rows(): pl.pallas_call(lambda *refs: load_kernel(first, count, *refs), out_shape=...  6.48 us
    ppermute x15, waiting for transfers between devices, permute(): lax.ppermute(array, axis, xor_pairs(mesh_shape[axis == 'node'], step))  1.29 us
  transfers between devices with their start and end apart: 15, of which 1 were waited for; matrix products, arithmetic and copies ran while one was open for 0% of the time, Pallas kernels for 59%

profile of v5, /device:TPU:0, one launch (start us, length us, event | category | flops | bytes accessed | tf_op | source)
XLA Modules:
  0.0 51.7 jit_solution(1005835935963630486)
XLA Ops:
  0.6 0.5 %collective-permute-start.1 = (bf16[2,4096]{1,0:T(2,128)(2,1)}, bf16[2,4096]{1,0:T(2,128)(2,1)S(1)}, u32[]{:S(2)}, u32[]{:S(2)}) collective-permute-start(bf16[2,4096]{1,0:T(2,128)(2,1)} %cotangent.1), channel_id=1, source_target_pairs={{0,1},{1,0},{2,3},{3,2},{4,5},{5,4},{6,7},{7,6},{8,9},{9,8},{10,11... | collective-permute-start | bytes 49160 | tf_op jit(solution)/shard_map/ppermute | solution.py:220
  1.2 0.1 collective-permute-start
  1.2 2.2 %load_gate_a.1 = (bf16[4096,1792]{1,0:T(8,128)(2,1)S(1)}, f32[8,128]{1,0:T(8,128)S(1)}) custom-call(bf16[4096,1792]{1,0:T(8,128)(2,1)} %refs_0_.3, bf16[2,4096]{1,0:T(2,128)(2,1)} %normed.1), custom_call_target="tpu_custom_call" | custom-call | bytes 3670016 | tf_op jit(solution)/shard_map/load_gate_a/pallas_call | solution.py:70
  3.5 0.0 collective-permute-done.1.other_cotangent
  3.5 0.0 collective-permute-done.other_normed
  3.5 3.9 %collective-permute-start.4 = (bf16[2,2,2,4096]{3,2,1,0:T(2,128)(2,1)S(1)}, bf16[2,2,2,4096]{3,2,1,0:T(2,128)(2,1)S(1)}, u32[]{:S(2)}, u32[]{:S(2)}) collective-permute-start(bf16[2,2,2,4096]{3,2,1,0:T(2,128)(2,1)S(1)} %pair.1.refs_0_), channel_id=1, source_target_pairs={{0,6},{1,7},{2,4},{3,5},{4,2},{5,3},{6,0},{7,1},{8,14},{9,15},{10,... | collective-permute-start | bytes 196616 | tf_op jit(solution)/shard_map/ppermute | solution.py:220
  7.5 0.5 collective-permute-start.3
  8.0 0.1 collective-permute-start.2
  8.1 4.3 %load_gate_b.1 = (bf16[4096,1792]{1,0:T(8,128)(2,1)S(1)}, f32[8,128]{1,0:T(8,128)S(1)}) custom-call(bf16[4096,1792]{1,0:T(8,128)(2,1)} %refs_0_.3, f32[8,128]{1,0:T(8,128)S(1)} %get-tuple-element.22.after.refs_1_, bf16[4096,1792]{1,0:T(8,128)(2,1)S(1)} %get-tuple-element.23.refs_2_), custom_call_target="tpu_custom_call", output_to_operand_aliasing={{0}: (2, {})} | custom-call | bytes 11010048 | tf_op jit(solution)/shard_map/load_gate_b/pallas_call | solution.py:70
  12.4 0.0 collective-permute-done.4.refs_3_
  12.4 0.0 collective-permute-done.3.refs_2_
  12.4 0.0 collective-permute-done.2.refs_1_
  12.4 0.2 arrange.1
  12.6 2.0 %collective-permute-start.5 = (bf16[16,3072]{1,0:T(8,128)(2,1)S(1)}, bf16[16,3072]{1,0:T(8,128)(2,1)S(1)}, u32[]{:S(2)}, u32[]{:S(2)}) collective-permute-start(bf16[16,3072]{1,0:T(8,128)(2,1)S(1)} %get-tuple-element.32), channel_id=1, source_target_pairs={{0,8},{8,0},{16,24},{24,16},{1,9},{9,1},{17,25},{25,17},{2,10},{10... | collective-permute-start | bytes 294920 | tf_op jit(solution)/shard_map/ppermute | solution.py:220
  14.7 2.6 %collective-permute-start.6 = (bf16[16,3072]{1,0:T(8,128)(2,1)S(1)}, bf16[16,3072]{1,0:T(8,128)(2,1)S(1)}, u32[]{:S(2)}, u32[]{:S(2)}) collective-permute-start(bf16[16,3072]{1,0:T(8,128)(2,1)S(1)} %get-tuple-element.33), channel_id=1, source_target_pairs={{0,16},{8,24},{16,0},{24,8},{1,17},{9,25},{17,1},{25,9},{2,18},{10... | collective-permute-start | bytes 294920 | tf_op jit(solution)/shard_map/ppermute | solution.py:220
  17.3 0.0 collective-permute-start.7
  17.3 8.5 %forward.1 = (bf16[3,16,1792]{2,1,0:T(8,128)(2,1)S(1)}, bf16[4096,1792]{1,0:T(8,128)(2,1)S(1)}, bf16[4096,1792]{1,0:T(8,128)(2,1)S(1)}) custom-call(bf16[2,16,4096]{2,1,0:T(8,128)(2,1)S(1)} %get-tuple-element.25.refs_0_, bf16[4096,1792]{1,0:T(8,128)(2,1)S(1)} %get-tuple-element.26.refs_1_, ...), custom_call_target="tpu_custom_call", output_to_operand_aliasing={{2}: (1, {})} | custom-call | flops 704643072 | bytes 29360128 | tf_op jit(solution)/shard_map/forward/pallas_call | solution.py:246
  25.9 0.0 collective-permute-done.7.refs_3_
  25.9 0.9 %collective-permute-start.8 = (bf16[2,16,1792]{2,1,0:T(8,128)(2,1)S(1)}, bf16[2,16,1792]{2,1,0:T(8,128)(2,1)S(1)}, u32[]{:S(2)}, u32[]{:S(2)}) collective-permute-start(bf16[2,16,1792]{2,1,0:T(8,128)(2,1)S(1)} %get-tuple-element.35), channel_id=1, source_target_pairs={{0,8},{8,0},{16,24},{24,16},{1,9},{9,1},{17,25},{25,17},{2,10},{10... | collective-permute-start | bytes 344072 | tf_op jit(solution)/shard_map/ppermute | solution.py:220
  26.9 3.5 %collective-permute-start.9 = (bf16[2,16,1792]{2,1,0:T(8,128)(2,1)S(1)}, bf16[2,16,1792]{2,1,0:T(8,128)(2,1)S(1)}, u32[]{:S(2)}, u32[]{:S(2)}) collective-permute-start(bf16[2,16,1792]{2,1,0:T(8,128)(2,1)S(1)} %get-tuple-element.36), channel_id=1, source_target_pairs={{0,16},{8,24},{16,0},{24,8},{1,17},{9,25},{17,1},{25,9},{2,18},{10... | collective-permute-start | bytes 344072 | tf_op jit(solution)/shard_map/ppermute | solution.py:220
  30.4 0.0 collective-permute-start.10
  30.4 7.7 %backward.1 = (f32[8,4096]{1,0:T(8,128)S(1)}, bf16[8,4096]{1,0:T(8,128)(2,1)S(1)}) custom-call(bf16[3,16,1792]{2,1,0:T(8,128)(2,1)S(1)} %get-tuple-element.27.refs_0_, bf16[4096,1792]{1,0:T(8,128)(2,1)S(1)} %get-tuple-element.28.refs_1_, bf16[4096,1792]{1,0:T(8,128)(2,1)S(1)} %get-tuple-element.29.refs_2_), custom_call_target="tpu_custom_call" | custom-call | flops 469762048 | bytes 29360128 | tf_op jit(solution)/shard_map/backward/pallas_call | solution.py:278
  38.0 0.0 collective-permute-done.9.refs_1_.refs_6_
  38.1 0.1 collective-permute-start.11
  38.2 1.2 %collective-permute-done.11 = bf16[8,4096]{1,0:T(8,128)(2,1)S(1)} collective-permute-done((bf16[8,4096]{1,0:T(8,128)(2,1)S(1)}, bf16[8,4096]{1,0:T(8,128)(2,1)S(1)}, u32[]{:S(2)}, u32[]{:S(2)}) %collective-permute-start.11) | collective-permute-done | bytes 65568 | tf_op jit(solution)/shard_map/ppermute | solution.py:220
  39.5 2.7 %collective-permute-start.14 = (bf16[2,4096]{1,0:T(2,128)(2,1)S(1)}, bf16[2,4096]{1,0:T(2,128)(2,1)S(1)}, u32[]{:S(2)}, u32[]{:S(2)}) collective-permute-start(bf16[2,4096]{1,0:T(2,128)(2,1)S(1)} %get-tuple-element.44), channel_id=1, source_target_pairs={{0,6},{1,7},{2,4},{3,5},{4,2},{5,3},{6,0},{7,1},{8,14},{9,15},{10,... | collective-permute-start | bytes 49160 | tf_op jit(solution)/shard_map/ppermute | solution.py:220
  42.2 0.5 collective-permute-start.13
  42.7 0.3 collective-permute-start.12
  43.0 8.0 %product.1 = (f32[3072,1792]{1,0:T(8,128)}, f32[8,128]{1,0:T(8,128)S(1)}) custom-call(bf16[16,3072]{1,0:T(8,128)(2,1)S(1)} %get-tuple-element.38.refs_0_, bf16[16,3072]{1,0:T(8,128)(2,1)S(1)} %collective-permute-done.5.refs_1_, bf16[16,3072]{1,0:T(8,128)(2,1)S(1)} %collective-permute-done.6.refs_2_, bf16[16,3072]{1,0:T(8,128)(2,1)S(1)} %collective-permute-done.7.refs_3_, ...), custom_call_target="tpu_custom_call" | custom-call | flops 704643072 | bytes 22020096 | tf_op jit(solution)/shard_map/product/pallas_call | solution.py:308
  51.1 0.0 collective-permute-done.13.refs_2_
  51.1 0.0 collective-permute-done.12.refs_1_
  51.1 0.7 %final_sum.1 = bf16[2,4096]{1,0:T(2,128)(2,1)} custom-call(f32[8,4096]{1,0:T(8,128)S(1)} %get-tuple-element.43.refs_0_, bf16[2,4096]{1,0:T(2,128)(2,1)S(1)} %collective-permute-done.12.refs_1_, bf16[2,4096]{1,0:T(2,128)(2,1)S(1)} %collective-permute-done.13.refs_2_, bf16[2,4096]{1,0:T(2,128)(2,1)S(1)} %collective-permute-done.14.refs_3_, ...), custom_call_target="tpu_custom_call" | custom-call | tf_op jit(solution)/shard_map/final_sum/pallas_call | solution.py:330
  (23 shorter events, 0.2 us)
Async XLA Ops:
  0.6 2.8 %copy-start.1 = (bf16[2,4096]{1,0:T(2,128)(2,1)S(1)}, bf16[2,4096]{1,0:T(2,128)(2,1)}, u32[]{:S(2)}) copy-start(bf16[2,4096]{1,0:T(2,128)(2,1)} %cotangent.1) | copy-start | bytes 49156
  0.6 2.8 %copy-start = (bf16[2,4096]{1,0:T(2,128)(2,1)S(1)}, bf16[2,4096]{1,0:T(2,128)(2,1)}, u32[]{:S(2)}) copy-start(bf16[2,4096]{1,0:T(2,128)(2,1)} %normed.1) | copy-start | bytes 49156
  0.6 2.8 %collective-permute-start.1 = (bf16[2,4096]{1,0:T(2,128)(2,1)}, bf16[2,4096]{1,0:T(2,128)(2,1)S(1)}, u32[]{:S(2)}, u32[]{:S(2)}) collective-permute-start(bf16[2,4096]{1,0:T(2,128)(2,1)} %cotangent.1), channel_id=1, source_target_pairs={{0,1},{1,0},{2,3},{3,2},{4,5},{5,4},{6,7},{7,6},{8,9},{9,8},{10,11... | collective-permute-start | bytes 49160 | tf_op jit(solution)/shard_map/ppermute | solution.py:220
  1.2 2.3 %collective-permute-start = (bf16[2,4096]{1,0:T(2,128)(2,1)}, bf16[2,4096]{1,0:T(2,128)(2,1)S(1)}, u32[]{:S(2)}, u32[]{:S(2)}) collective-permute-start(bf16[2,4096]{1,0:T(2,128)(2,1)} %normed.1), channel_id=1, source_target_pairs={{0,1},{1,0},{2,3},{3,2},{4,5},{5,4},{6,7},{7,6},{8,9},{9,8},{10,11... | collective-permute-start | bytes 49160 | tf_op jit(solution)/shard_map/ppermute | solution.py:220
  1.2 16.0 %slice-start = ((s8[14680064]{0:T(1024)(128)(4,1)}), s8[4194304]{0:T(1024)(128)(4,1)S(1)}, s32[]{:S(2)}) async-start(s8[14680064]{0:T(1024)(128)(4,1)} %bitcast), calls=%async_computation | async-start | bytes 8388608
  1.2 16.0 %slice-start.1 = ((s8[14680064]{0:T(1024)(128)(4,1)}), s8[4194304]{0:T(1024)(128)(4,1)S(1)}, s32[]{:S(2)}) async-start(s8[14680064]{0:T(1024)(128)(4,1)} %bitcast), calls=%async_computation.1 | async-start | bytes 8388608
  3.5 8.9 %collective-permute-start.4 = (bf16[2,2,2,4096]{3,2,1,0:T(2,128)(2,1)S(1)}, bf16[2,2,2,4096]{3,2,1,0:T(2,128)(2,1)S(1)}, u32[]{:S(2)}, u32[]{:S(2)}) collective-permute-start(bf16[2,2,2,4096]{3,2,1,0:T(2,128)(2,1)S(1)} %pair.1.refs_0_), channel_id=1, source_target_pairs={{0,6},{1,7},{2,4},{3,5},{4,2},{5,3},{6,0},{7,1},{8,14},{9,15},{10,... | collective-permute-start | bytes 196616 | tf_op jit(solution)/shard_map/ppermute | solution.py:220
  7.5 5.0 %collective-permute-start.3 = (bf16[2,2,2,4096]{3,2,1,0:T(2,128)(2,1)S(1)}, bf16[2,2,2,4096]{3,2,1,0:T(2,128)(2,1)S(1)}, u32[]{:S(2)}, u32[]{:S(2)}) collective-permute-start(bf16[2,2,2,4096]{3,2,1,0:T(2,128)(2,1)S(1)} %pair.1.refs_0_), channel_id=1, source_target_pairs={{0,4},{1,5},{2,6},{3,7},{4,0},{5,1},{6,2},{7,3},{8,12},{9,13},{10,... | collective-permute-start | bytes 196616 | tf_op jit(solution)/shard_map/ppermute | solution.py:220
  8.0 4.5 %collective-permute-start.2 = (bf16[2,2,2,4096]{3,2,1,0:T(2,128)(2,1)S(1)}, bf16[2,2,2,4096]{3,2,1,0:T(2,128)(2,1)S(1)}, u32[]{:S(2)}, u32[]{:S(2)}) collective-permute-start(bf16[2,2,2,4096]{3,2,1,0:T(2,128)(2,1)S(1)} %pair.1.refs_0_), channel_id=1, source_target_pairs={{0,2},{1,3},{2,0},{3,1},{4,6},{5,7},{6,4},{7,5},{8,10},{9,11},{10,... | collective-permute-start | bytes 196616 | tf_op jit(solution)/shard_map/ppermute | solution.py:220
  8.1 9.2 %slice-start.2 = ((s8[14680064]{0:T(1024)(128)(4,1)}), s8[4194304]{0:T(1024)(128)(4,1)S(1)}, s32[]{:S(2)}) async-start(s8[14680064]{0:T(1024)(128)(4,1)} %bitcast), calls=%async_computation.2 | async-start | bytes 8388608
  8.1 9.2 %slice-start.3 = ((s8[14680064]{0:T(1024)(128)(4,1)}), s8[2097152]{0:T(1024)(128)(4,1)S(1)}, s32[]{:S(2)}) async-start(s8[14680064]{0:T(1024)(128)(4,1)} %bitcast), calls=%async_computation.3 | async-start | bytes 4194304
  12.6 13.2 %collective-permute-start.5 = (bf16[16,3072]{1,0:T(8,128)(2,1)S(1)}, bf16[16,3072]{1,0:T(8,128)(2,1)S(1)}, u32[]{:S(2)}, u32[]{:S(2)}) collective-permute-start(bf16[16,3072]{1,0:T(8,128)(2,1)S(1)} %get-tuple-element.32), channel_id=1, source_target_pairs={{0,8},{8,0},{16,24},{24,16},{1,9},{9,1},{17,25},{25,17},{2,10},{10... | collective-permute-start | bytes 294920 | tf_op jit(solution)/shard_map/ppermute | solution.py:220
  14.7 11.2 %collective-permute-start.6 = (bf16[16,3072]{1,0:T(8,128)(2,1)S(1)}, bf16[16,3072]{1,0:T(8,128)(2,1)S(1)}, u32[]{:S(2)}, u32[]{:S(2)}) collective-permute-start(bf16[16,3072]{1,0:T(8,128)(2,1)S(1)} %get-tuple-element.33), channel_id=1, source_target_pairs={{0,16},{8,24},{16,0},{24,8},{1,17},{9,25},{17,1},{25,9},{2,18},{10... | collective-permute-start | bytes 294920 | tf_op jit(solution)/shard_map/ppermute | solution.py:220
  17.3 8.6 %collective-permute-start.7 = (bf16[16,3072]{1,0:T(8,128)(2,1)S(1)}, bf16[16,3072]{1,0:T(8,128)(2,1)S(1)}, u32[]{:S(2)}, u32[]{:S(2)}) collective-permute-start(bf16[16,3072]{1,0:T(8,128)(2,1)S(1)} %get-tuple-element.34), channel_id=1, source_target_pairs={{0,24},{8,16},{16,8},{24,0},{1,25},{9,17},{17,9},{25,1},{2,26},{10... | collective-permute-start | bytes 294920 | tf_op jit(solution)/shard_map/ppermute | solution.py:220
  25.9 12.1 %collective-permute-start.8 = (bf16[2,16,1792]{2,1,0:T(8,128)(2,1)S(1)}, bf16[2,16,1792]{2,1,0:T(8,128)(2,1)S(1)}, u32[]{:S(2)}, u32[]{:S(2)}) collective-permute-start(bf16[2,16,1792]{2,1,0:T(8,128)(2,1)S(1)} %get-tuple-element.35), channel_id=1, source_target_pairs={{0,8},{8,0},{16,24},{24,16},{1,9},{9,1},{17,25},{25,17},{2,10},{10... | collective-permute-start | bytes 344072 | tf_op jit(solution)/shard_map/ppermute | solution.py:220
  26.9 11.2 %collective-permute-start.9 = (bf16[2,16,1792]{2,1,0:T(8,128)(2,1)S(1)}, bf16[2,16,1792]{2,1,0:T(8,128)(2,1)S(1)}, u32[]{:S(2)}, u32[]{:S(2)}) collective-permute-start(bf16[2,16,1792]{2,1,0:T(8,128)(2,1)S(1)} %get-tuple-element.36), channel_id=1, source_target_pairs={{0,16},{8,24},{16,0},{24,8},{1,17},{9,25},{17,1},{25,9},{2,18},{10... | collective-permute-start | bytes 344072 | tf_op jit(solution)/shard_map/ppermute | solution.py:220
  30.4 7.7 %collective-permute-start.10 = (bf16[2,16,1792]{2,1,0:T(8,128)(2,1)S(1)}, bf16[2,16,1792]{2,1,0:T(8,128)(2,1)S(1)}, u32[]{:S(2)}, u32[]{:S(2)}) collective-permute-start(bf16[2,16,1792]{2,1,0:T(8,128)(2,1)S(1)} %get-tuple-element.37), channel_id=1, source_target_pairs={{0,24},{8,16},{16,8},{24,0},{1,25},{9,17},{17,9},{25,1},{2,26},{10... | collective-permute-start | bytes 344072 | tf_op jit(solution)/shard_map/ppermute | solution.py:220
  38.1 1.3 %collective-permute-start.11 = (bf16[8,4096]{1,0:T(8,128)(2,1)S(1)}, bf16[8,4096]{1,0:T(8,128)(2,1)S(1)}, u32[]{:S(2)}, u32[]{:S(2)}) collective-permute-start(bf16[8,4096]{1,0:T(8,128)(2,1)S(1)} %hold.1), channel_id=1, source_target_pairs={{0,1},{1,0},{2,3},{3,2},{4,5},{5,4},{6,7},{7,6},{8,9},{9,8},{10,11... | collective-permute-start | bytes 196616 | tf_op jit(solution)/shard_map/ppermute | solution.py:220
  39.5 11.6 %collective-permute-start.14 = (bf16[2,4096]{1,0:T(2,128)(2,1)S(1)}, bf16[2,4096]{1,0:T(2,128)(2,1)S(1)}, u32[]{:S(2)}, u32[]{:S(2)}) collective-permute-start(bf16[2,4096]{1,0:T(2,128)(2,1)S(1)} %get-tuple-element.44), channel_id=1, source_target_pairs={{0,6},{1,7},{2,4},{3,5},{4,2},{5,3},{6,0},{7,1},{8,14},{9,15},{10,... | collective-permute-start | bytes 49160 | tf_op jit(solution)/shard_map/ppermute | solution.py:220
  42.2 8.9 %collective-permute-start.13 = (bf16[2,4096]{1,0:T(2,128)(2,1)S(1)}, bf16[2,4096]{1,0:T(2,128)(2,1)S(1)}, u32[]{:S(2)}, u32[]{:S(2)}) collective-permute-start(bf16[2,4096]{1,0:T(2,128)(2,1)S(1)} %get-tuple-element.45), channel_id=1, source_target_pairs={{0,4},{1,5},{2,6},{3,7},{4,0},{5,1},{6,2},{7,3},{8,12},{9,13},{10,... | collective-permute-start | bytes 49160 | tf_op jit(solution)/shard_map/ppermute | solution.py:220
  42.7 8.4 %collective-permute-start.12 = (bf16[2,4096]{1,0:T(2,128)(2,1)S(1)}, bf16[2,4096]{1,0:T(2,128)(2,1)S(1)}, u32[]{:S(2)}, u32[]{:S(2)}) collective-permute-start(bf16[2,4096]{1,0:T(2,128)(2,1)S(1)} %get-tuple-element.46), channel_id=1, source_target_pairs={{0,2},{1,3},{2,0},{3,1},{4,6},{5,7},{6,4},{7,5},{8,10},{9,11},{10,... | collective-permute-start | bytes 49160 | tf_op jit(solution)/shard_map/ppermute | solution.py:220

commit v6 on v5

--- a/solution.py
+++ b/solution.py
@@ -188,7 +188,7 @@
         copy = pltpu.make_async_copy(
             result.at[pl.ds(start, count)], out.at[pl.ds(start, count)], sem.at[i]
         )
-        copy.start()
+        copy.start(priority=i % 2)
         copies.append(copy)
     for copy in copies:
         copy.wait()
@@ -304,7 +304,7 @@
         for slot, s in enumerate(chips, 1)
     ]
 
-    cuts = [(start, 256) for start in range(0, block, 256)]
+    cuts = [(0, 128), (128, 128)] + [(start, 256) for start in range(256, block, 256)]
     weight_grads, token = pl.pallas_call(
         lambda *refs: product_kernel(n_dp, cuts, *refs),
         out_shape=(

time: 51.9 us -> 51.8 us (level)
  no operation moved by 1% of the time
where the time goes in v6:
time: 51.8 us; the launch traced here: 51.6 us
  Pallas kernels  31.5 us (61%)
  starting transfers between devices  17.9 us (35%)
  waiting for transfers between devices  1.29 us (2%)
  between operations  0.88 us (2%)
    ppermute x15, starting transfers between devices, permute(): lax.ppermute(array, axis, xor_pairs(mesh_shape[axis == 'node'], step))  17.9 us
    pallas_call x1, Pallas kernels, shards_group(): pl.pallas_call(lambda *refs: forward_kernel(chunk, *refs), out_shape=[jax...  8.52 us
    pallas_call x1, Pallas kernels, shards_group(): pl.pallas_call(lambda *refs: product_kernel(n_dp, cuts, *refs), out_shape...  7.9 us
    pallas_call x1, Pallas kernels, shards_group(): pl.pallas_call(lambda *refs: backward_kernel(chunk, *refs), out_shape=(ja...  7.65 us
    pallas_call x2, Pallas kernels, load_rows(): pl.pallas_call(lambda *refs: load_kernel(first, count, *refs), out_shape=...  6.48 us
    ppermute x15, waiting for transfers between devices, permute(): lax.ppermute(array, axis, xor_pairs(mesh_shape[axis == 'node'], step))  1.29 us
  transfers between devices with their start and end apart: 15, of which 1 were waited for; matrix products, arithmetic and copies ran while one was open for 0% of the time, Pallas kernels for 59%

profile of v6, /device:TPU:0, one launch (start us, length us, event | category | flops | bytes accessed | tf_op | source)
XLA Modules:
  0.0 51.6 jit_solution(5825859309873528925)
XLA Ops:
  0.6 0.5 %collective-permute-start.1 = (bf16[2,4096]{1,0:T(2,128)(2,1)}, bf16[2,4096]{1,0:T(2,128)(2,1)S(1)}, u32[]{:S(2)}, u32[]{:S(2)}) collective-permute-start(bf16[2,4096]{1,0:T(2,128)(2,1)} %cotangent.1), channel_id=1, source_target_pairs={{0,1},{1,0},{2,3},{3,2},{4,5},{5,4},{6,7},{7,6},{8,9},{9,8},{10,11... | collective-permute-start | bytes 49160 | tf_op jit(solution)/shard_map/ppermute | solution.py:220
  1.2 0.1 collective-permute-start
  1.2 2.2 %load_gate_a.1 = (bf16[4096,1792]{1,0:T(8,128)(2,1)S(1)}, f32[8,128]{1,0:T(8,128)S(1)}) custom-call(bf16[4096,1792]{1,0:T(8,128)(2,1)} %refs_0_.3, bf16[2,4096]{1,0:T(2,128)(2,1)} %normed.1), custom_call_target="tpu_custom_call" | custom-call | bytes 3670016 | tf_op jit(solution)/shard_map/load_gate_a/pallas_call | solution.py:70
  3.5 0.0 collective-permute-done.1.other_cotangent
  3.5 0.0 collective-permute-done.other_normed
  3.5 3.9 %collective-permute-start.4 = (bf16[2,2,2,4096]{3,2,1,0:T(2,128)(2,1)S(1)}, bf16[2,2,2,4096]{3,2,1,0:T(2,128)(2,1)S(1)}, u32[]{:S(2)}, u32[]{:S(2)}) collective-permute-start(bf16[2,2,2,4096]{3,2,1,0:T(2,128)(2,1)S(1)} %pair.1.refs_0_), channel_id=1, source_target_pairs={{0,6},{1,7},{2,4},{3,5},{4,2},{5,3},{6,0},{7,1},{8,14},{9,15},{10,... | collective-permute-start | bytes 196616 | tf_op jit(solution)/shard_map/ppermute | solution.py:220
  7.5 0.5 collective-permute-start.3
  8.0 0.1 collective-permute-start.2
  8.1 4.3 %load_gate_b.1 = (bf16[4096,1792]{1,0:T(8,128)(2,1)S(1)}, f32[8,128]{1,0:T(8,128)S(1)}) custom-call(bf16[4096,1792]{1,0:T(8,128)(2,1)} %refs_0_.3, f32[8,128]{1,0:T(8,128)S(1)} %get-tuple-element.22.after.refs_1_, bf16[4096,1792]{1,0:T(8,128)(2,1)S(1)} %get-tuple-element.23.refs_2_), custom_call_target="tpu_custom_call", output_to_operand_aliasing={{0}: (2, {})} | custom-call | bytes 11010048 | tf_op jit(solution)/shard_map/load_gate_b/pallas_call | solution.py:70
  12.4 0.0 collective-permute-done.4.refs_3_
  12.4 0.0 collective-permute-done.3.refs_2_
  12.4 0.0 collective-permute-done.2.refs_1_
  12.4 0.2 arrange.1
  12.6 2.0 %collective-permute-start.5 = (bf16[16,3072]{1,0:T(8,128)(2,1)S(1)}, bf16[16,3072]{1,0:T(8,128)(2,1)S(1)}, u32[]{:S(2)}, u32[]{:S(2)}) collective-permute-start(bf16[16,3072]{1,0:T(8,128)(2,1)S(1)} %get-tuple-element.32), channel_id=1, source_target_pairs={{0,8},{8,0},{16,24},{24,16},{1,9},{9,1},{17,25},{25,17},{2,10},{10... | collective-permute-start | bytes 294920 | tf_op jit(solution)/shard_map/ppermute | solution.py:220
  14.7 2.6 %collective-permute-start.6 = (bf16[16,3072]{1,0:T(8,128)(2,1)S(1)}, bf16[16,3072]{1,0:T(8,128)(2,1)S(1)}, u32[]{:S(2)}, u32[]{:S(2)}) collective-permute-start(bf16[16,3072]{1,0:T(8,128)(2,1)S(1)} %get-tuple-element.33), channel_id=1, source_target_pairs={{0,16},{8,24},{16,0},{24,8},{1,17},{9,25},{17,1},{25,9},{2,18},{10... | collective-permute-start | bytes 294920 | tf_op jit(solution)/shard_map/ppermute | solution.py:220
  17.3 0.0 collective-permute-start.7
  17.3 8.5 %forward.1 = (bf16[3,16,1792]{2,1,0:T(8,128)(2,1)S(1)}, bf16[4096,1792]{1,0:T(8,128)(2,1)S(1)}, bf16[4096,1792]{1,0:T(8,128)(2,1)S(1)}) custom-call(bf16[2,16,4096]{2,1,0:T(8,128)(2,1)S(1)} %get-tuple-element.25.refs_0_, bf16[4096,1792]{1,0:T(8,128)(2,1)S(1)} %get-tuple-element.26.refs_1_, ...), custom_call_target="tpu_custom_call", output_to_operand_aliasing={{2}: (1, {})} | custom-call | flops 704643072 | bytes 29360128 | tf_op jit(solution)/shard_map/forward/pallas_call | solution.py:246
  25.9 0.0 collective-permute-done.7.refs_3_
  25.9 0.9 %collective-permute-start.8 = (bf16[2,16,1792]{2,1,0:T(8,128)(2,1)S(1)}, bf16[2,16,1792]{2,1,0:T(8,128)(2,1)S(1)}, u32[]{:S(2)}, u32[]{:S(2)}) collective-permute-start(bf16[2,16,1792]{2,1,0:T(8,128)(2,1)S(1)} %get-tuple-element.35), channel_id=1, source_target_pairs={{0,8},{8,0},{16,24},{24,16},{1,9},{9,1},{17,25},{25,17},{2,10},{10... | collective-permute-start | bytes 344072 | tf_op jit(solution)/shard_map/ppermute | solution.py:220
  26.9 3.5 %collective-permute-start.9 = (bf16[2,16,1792]{2,1,0:T(8,128)(2,1)S(1)}, bf16[2,16,1792]{2,1,0:T(8,128)(2,1)S(1)}, u32[]{:S(2)}, u32[]{:S(2)}) collective-permute-start(bf16[2,16,1792]{2,1,0:T(8,128)(2,1)S(1)} %get-tuple-element.36), channel_id=1, source_target_pairs={{0,16},{8,24},{16,0},{24,8},{1,17},{9,25},{17,1},{25,9},{2,18},{10... | collective-permute-start | bytes 344072 | tf_op jit(solution)/shard_map/ppermute | solution.py:220
  30.4 0.0 collective-permute-start.10
  30.4 7.7 %backward.1 = (f32[8,4096]{1,0:T(8,128)S(1)}, bf16[8,4096]{1,0:T(8,128)(2,1)S(1)}) custom-call(bf16[3,16,1792]{2,1,0:T(8,128)(2,1)S(1)} %get-tuple-element.27.refs_0_, bf16[4096,1792]{1,0:T(8,128)(2,1)S(1)} %get-tuple-element.28.refs_1_, bf16[4096,1792]{1,0:T(8,128)(2,1)S(1)} %get-tuple-element.29.refs_2_), custom_call_target="tpu_custom_call" | custom-call | flops 469762048 | bytes 29360128 | tf_op jit(solution)/shard_map/backward/pallas_call | solution.py:278
  38.0 0.0 collective-permute-done.9.refs_1_.refs_6_
  38.1 0.1 collective-permute-start.11
  38.2 1.2 %collective-permute-done.11 = bf16[8,4096]{1,0:T(8,128)(2,1)S(1)} collective-permute-done((bf16[8,4096]{1,0:T(8,128)(2,1)S(1)}, bf16[8,4096]{1,0:T(8,128)(2,1)S(1)}, u32[]{:S(2)}, u32[]{:S(2)}) %collective-permute-start.11) | collective-permute-done | bytes 65568 | tf_op jit(solution)/shard_map/ppermute | solution.py:220
  39.5 2.7 %collective-permute-start.14 = (bf16[2,4096]{1,0:T(2,128)(2,1)S(1)}, bf16[2,4096]{1,0:T(2,128)(2,1)S(1)}, u32[]{:S(2)}, u32[]{:S(2)}) collective-permute-start(bf16[2,4096]{1,0:T(2,128)(2,1)S(1)} %get-tuple-element.44), channel_id=1, source_target_pairs={{0,6},{1,7},{2,4},{3,5},{4,2},{5,3},{6,0},{7,1},{8,14},{9,15},{10,... | collective-permute-start | bytes 49160 | tf_op jit(solution)/shard_map/ppermute | solution.py:220
  42.2 0.5 collective-permute-start.13
  42.7 0.3 collective-permute-start.12
  43.0 7.9 %product.1 = (f32[3072,1792]{1,0:T(8,128)}, f32[8,128]{1,0:T(8,128)S(1)}) custom-call(bf16[16,3072]{1,0:T(8,128)(2,1)S(1)} %get-tuple-element.38.refs_0_, bf16[16,3072]{1,0:T(8,128)(2,1)S(1)} %collective-permute-done.5.refs_1_, bf16[16,3072]{1,0:T(8,128)(2,1)S(1)} %collective-permute-done.6.refs_2_, bf16[16,3072]{1,0:T(8,128)(2,1)S(1)} %collective-permute-done.7.refs_3_, ...), custom_call_target="tpu_custom_call" | custom-call | flops 704643072 | bytes 22020096 | tf_op jit(solution)/shard_map/product/pallas_call | solution.py:308
  50.9 0.0 collective-permute-done.14.refs_3_
  51.0 0.0 collective-permute-done.12.refs_1_
  51.0 0.7 %final_sum.1 = bf16[2,4096]{1,0:T(2,128)(2,1)} custom-call(f32[8,4096]{1,0:T(8,128)S(1)} %get-tuple-element.43.refs_0_, bf16[2,4096]{1,0:T(2,128)(2,1)S(1)} %collective-permute-done.12.refs_1_, bf16[2,4096]{1,0:T(2,128)(2,1)S(1)} %collective-permute-done.13.refs_2_, bf16[2,4096]{1,0:T(2,128)(2,1)S(1)} %collective-permute-done.14.refs_3_, ...), custom_call_target="tpu_custom_call" | custom-call | tf_op jit(solution)/shard_map/final_sum/pallas_call | solution.py:330
  (23 shorter events, 0.2 us)
Async XLA Ops:
  0.6 2.8 %copy-start.1 = (bf16[2,4096]{1,0:T(2,128)(2,1)S(1)}, bf16[2,4096]{1,0:T(2,128)(2,1)}, u32[]{:S(2)}) copy-start(bf16[2,4096]{1,0:T(2,128)(2,1)} %cotangent.1) | copy-start | bytes 49156
  0.6 2.8 %copy-start = (bf16[2,4096]{1,0:T(2,128)(2,1)S(1)}, bf16[2,4096]{1,0:T(2,128)(2,1)}, u32[]{:S(2)}) copy-start(bf16[2,4096]{1,0:T(2,128)(2,1)} %normed.1) | copy-start | bytes 49156
  0.6 2.8 %collective-permute-start.1 = (bf16[2,4096]{1,0:T(2,128)(2,1)}, bf16[2,4096]{1,0:T(2,128)(2,1)S(1)}, u32[]{:S(2)}, u32[]{:S(2)}) collective-permute-start(bf16[2,4096]{1,0:T(2,128)(2,1)} %cotangent.1), channel_id=1, source_target_pairs={{0,1},{1,0},{2,3},{3,2},{4,5},{5,4},{6,7},{7,6},{8,9},{9,8},{10,11... | collective-permute-start | bytes 49160 | tf_op jit(solution)/shard_map/ppermute | solution.py:220
  1.2 2.3 %collective-permute-start = (bf16[2,4096]{1,0:T(2,128)(2,1)}, bf16[2,4096]{1,0:T(2,128)(2,1)S(1)}, u32[]{:S(2)}, u32[]{:S(2)}) collective-permute-start(bf16[2,4096]{1,0:T(2,128)(2,1)} %normed.1), channel_id=1, source_target_pairs={{0,1},{1,0},{2,3},{3,2},{4,5},{5,4},{6,7},{7,6},{8,9},{9,8},{10,11... | collective-permute-start | bytes 49160 | tf_op jit(solution)/shard_map/ppermute | solution.py:220
  1.2 16.0 %slice-start = ((s8[14680064]{0:T(1024)(128)(4,1)}), s8[4194304]{0:T(1024)(128)(4,1)S(1)}, s32[]{:S(2)}) async-start(s8[14680064]{0:T(1024)(128)(4,1)} %bitcast), calls=%async_computation | async-start | bytes 8388608
  1.2 16.0 %slice-start.1 = ((s8[14680064]{0:T(1024)(128)(4,1)}), s8[4194304]{0:T(1024)(128)(4,1)S(1)}, s32[]{:S(2)}) async-start(s8[14680064]{0:T(1024)(128)(4,1)} %bitcast), calls=%async_computation.1 | async-start | bytes 8388608
  3.5 8.9 %collective-permute-start.4 = (bf16[2,2,2,4096]{3,2,1,0:T(2,128)(2,1)S(1)}, bf16[2,2,2,4096]{3,2,1,0:T(2,128)(2,1)S(1)}, u32[]{:S(2)}, u32[]{:S(2)}) collective-permute-start(bf16[2,2,2,4096]{3,2,1,0:T(2,128)(2,1)S(1)} %pair.1.refs_0_), channel_id=1, source_target_pairs={{0,6},{1,7},{2,4},{3,5},{4,2},{5,3},{6,0},{7,1},{8,14},{9,15},{10,... | collective-permute-start | bytes 196616 | tf_op jit(solution)/shard_map/ppermute | solution.py:220
  7.5 5.0 %collective-permute-start.3 = (bf16[2,2,2,4096]{3,2,1,0:T(2,128)(2,1)S(1)}, bf16[2,2,2,4096]{3,2,1,0:T(2,128)(2,1)S(1)}, u32[]{:S(2)}, u32[]{:S(2)}) collective-permute-start(bf16[2,2,2,4096]{3,2,1,0:T(2,128)(2,1)S(1)} %pair.1.refs_0_), channel_id=1, source_target_pairs={{0,4},{1,5},{2,6},{3,7},{4,0},{5,1},{6,2},{7,3},{8,12},{9,13},{10,... | collective-permute-start | bytes 196616 | tf_op jit(solution)/shard_map/ppermute | solution.py:220
  8.0 4.5 %collective-permute-start.2 = (bf16[2,2,2,4096]{3,2,1,0:T(2,128)(2,1)S(1)}, bf16[2,2,2,4096]{3,2,1,0:T(2,128)(2,1)S(1)}, u32[]{:S(2)}, u32[]{:S(2)}) collective-permute-start(bf16[2,2,2,4096]{3,2,1,0:T(2,128)(2,1)S(1)} %pair.1.refs_0_), channel_id=1, source_target_pairs={{0,2},{1,3},{2,0},{3,1},{4,6},{5,7},{6,4},{7,5},{8,10},{9,11},{10,... | collective-permute-start | bytes 196616 | tf_op jit(solution)/shard_map/ppermute | solution.py:220
  8.1 9.2 %slice-start.2 = ((s8[14680064]{0:T(1024)(128)(4,1)}), s8[4194304]{0:T(1024)(128)(4,1)S(1)}, s32[]{:S(2)}) async-start(s8[14680064]{0:T(1024)(128)(4,1)} %bitcast), calls=%async_computation.2 | async-start | bytes 8388608
  8.1 9.2 %slice-start.3 = ((s8[14680064]{0:T(1024)(128)(4,1)}), s8[2097152]{0:T(1024)(128)(4,1)S(1)}, s32[]{:S(2)}) async-start(s8[14680064]{0:T(1024)(128)(4,1)} %bitcast), calls=%async_computation.3 | async-start | bytes 4194304
  12.6 13.2 %collective-permute-start.5 = (bf16[16,3072]{1,0:T(8,128)(2,1)S(1)}, bf16[16,3072]{1,0:T(8,128)(2,1)S(1)}, u32[]{:S(2)}, u32[]{:S(2)}) collective-permute-start(bf16[16,3072]{1,0:T(8,128)(2,1)S(1)} %get-tuple-element.32), channel_id=1, source_target_pairs={{0,8},{8,0},{16,24},{24,16},{1,9},{9,1},{17,25},{25,17},{2,10},{10... | collective-permute-start | bytes 294920 | tf_op jit(solution)/shard_map/ppermute | solution.py:220
  14.7 11.2 %collective-permute-start.6 = (bf16[16,3072]{1,0:T(8,128)(2,1)S(1)}, bf16[16,3072]{1,0:T(8,128)(2,1)S(1)}, u32[]{:S(2)}, u32[]{:S(2)}) collective-permute-start(bf16[16,3072]{1,0:T(8,128)(2,1)S(1)} %get-tuple-element.33), channel_id=1, source_target_pairs={{0,16},{8,24},{16,0},{24,8},{1,17},{9,25},{17,1},{25,9},{2,18},{10... | collective-permute-start | bytes 294920 | tf_op jit(solution)/shard_map/ppermute | solution.py:220
  17.3 8.6 %collective-permute-start.7 = (bf16[16,3072]{1,0:T(8,128)(2,1)S(1)}, bf16[16,3072]{1,0:T(8,128)(2,1)S(1)}, u32[]{:S(2)}, u32[]{:S(2)}) collective-permute-start(bf16[16,3072]{1,0:T(8,128)(2,1)S(1)} %get-tuple-element.34), channel_id=1, source_target_pairs={{0,24},{8,16},{16,8},{24,0},{1,25},{9,17},{17,9},{25,1},{2,26},{10... | collective-permute-start | bytes 294920 | tf_op jit(solution)/shard_map/ppermute | solution.py:220
  25.9 12.1 %collective-permute-start.8 = (bf16[2,16,1792]{2,1,0:T(8,128)(2,1)S(1)}, bf16[2,16,1792]{2,1,0:T(8,128)(2,1)S(1)}, u32[]{:S(2)}, u32[]{:S(2)}) collective-permute-start(bf16[2,16,1792]{2,1,0:T(8,128)(2,1)S(1)} %get-tuple-element.35), channel_id=1, source_target_pairs={{0,8},{8,0},{16,24},{24,16},{1,9},{9,1},{17,25},{25,17},{2,10},{10... | collective-permute-start | bytes 344072 | tf_op jit(solution)/shard_map/ppermute | solution.py:220
  26.9 11.2 %collective-permute-start.9 = (bf16[2,16,1792]{2,1,0:T(8,128)(2,1)S(1)}, bf16[2,16,1792]{2,1,0:T(8,128)(2,1)S(1)}, u32[]{:S(2)}, u32[]{:S(2)}) collective-permute-start(bf16[2,16,1792]{2,1,0:T(8,128)(2,1)S(1)} %get-tuple-element.36), channel_id=1, source_target_pairs={{0,16},{8,24},{16,0},{24,8},{1,17},{9,25},{17,1},{25,9},{2,18},{10... | collective-permute-start | bytes 344072 | tf_op jit(solution)/shard_map/ppermute | solution.py:220
  30.4 7.7 %collective-permute-start.10 = (bf16[2,16,1792]{2,1,0:T(8,128)(2,1)S(1)}, bf16[2,16,1792]{2,1,0:T(8,128)(2,1)S(1)}, u32[]{:S(2)}, u32[]{:S(2)}) collective-permute-start(bf16[2,16,1792]{2,1,0:T(8,128)(2,1)S(1)} %get-tuple-element.37), channel_id=1, source_target_pairs={{0,24},{8,16},{16,8},{24,0},{1,25},{9,17},{17,9},{25,1},{2,26},{10... | collective-permute-start | bytes 344072 | tf_op jit(solution)/shard_map/ppermute | solution.py:220
  38.1 1.3 %collective-permute-start.11 = (bf16[8,4096]{1,0:T(8,128)(2,1)S(1)}, bf16[8,4096]{1,0:T(8,128)(2,1)S(1)}, u32[]{:S(2)}, u32[]{:S(2)}) collective-permute-start(bf16[8,4096]{1,0:T(8,128)(2,1)S(1)} %hold.1), channel_id=1, source_target_pairs={{0,1},{1,0},{2,3},{3,2},{4,5},{5,4},{6,7},{7,6},{8,9},{9,8},{10,11... | collective-permute-start | bytes 196616 | tf_op jit(solution)/shard_map/ppermute | solution.py:220
  39.5 11.5 %collective-permute-start.14 = (bf16[2,4096]{1,0:T(2,128)(2,1)S(1)}, bf16[2,4096]{1,0:T(2,128)(2,1)S(1)}, u32[]{:S(2)}, u32[]{:S(2)}) collective-permute-start(bf16[2,4096]{1,0:T(2,128)(2,1)S(1)} %get-tuple-element.44), channel_id=1, source_target_pairs={{0,6},{1,7},{2,4},{3,5},{4,2},{5,3},{6,0},{7,1},{8,14},{9,15},{10,... | collective-permute-start | bytes 49160 | tf_op jit(solution)/shard_map/ppermute | solution.py:220
  42.2 8.8 %collective-permute-start.13 = (bf16[2,4096]{1,0:T(2,128)(2,1)S(1)}, bf16[2,4096]{1,0:T(2,128)(2,1)S(1)}, u32[]{:S(2)}, u32[]{:S(2)}) collective-permute-start(bf16[2,4096]{1,0:T(2,128)(2,1)S(1)} %get-tuple-element.45), channel_id=1, source_target_pairs={{0,4},{1,5},{2,6},{3,7},{4,0},{5,1},{6,2},{7,3},{8,12},{9,13},{10,... | collective-permute-start | bytes 49160 | tf_op jit(solution)/shard_map/ppermute | solution.py:220
  42.7 8.3 %collective-permute-start.12 = (bf16[2,4096]{1,0:T(2,128)(2,1)S(1)}, bf16[2,4096]{1,0:T(2,128)(2,1)S(1)}, u32[]{:S(2)}, u32[]{:S(2)}) collective-permute-start(bf16[2,4096]{1,0:T(2,128)(2,1)S(1)} %get-tuple-element.46), channel_id=1, source_target_pairs={{0,2},{1,3},{2,0},{3,1},{4,6},{5,7},{6,4},{7,5},{8,10},{9,11},{10,... | collective-permute-start | bytes 49160 | tf_op jit(solution)/shard_map/ppermute | solution.py:220

commit v7 on v5

--- a/solution.py
+++ b/solution.py
@@ -59,11 +59,16 @@
 
 def load_kernel(first, count, weight, after, *refs):
     out, token, sem = refs[-3:]
-    part = pl.ds(first, count)
-    copy = pltpu.make_async_copy(weight.at[part], out.at[part], sem)
-    copy.start()
+    piece = count // sem.shape[0]
+    copies = []
+    for i in range(sem.shape[0]):
+        part = pl.ds(first + i * piece, piece)
+        copies.append(pltpu.make_async_copy(weight.at[part], out.at[part], sem.at[i]))
+    for copy in copies:
+        copy.start(priority=1)
     token[...] = jnp.zeros(token.shape, token.dtype)
-    copy.wait()
+    for copy in copies:
+        copy.wait()
 
 
 def load_rows(weight, first, count, after, held, name):
@@ -76,7 +81,7 @@
         in_specs=[HBM_SPEC, ANY_SPEC] + [VMEM_SPEC] * len(held),
         out_specs=(VMEM_SPEC, VMEM_SPEC),
         input_output_aliases={2: 0} if held else {},
-        scratch_shapes=[pltpu.SemaphoreType.DMA],
+        scratch_shapes=[pltpu.SemaphoreType.DMA((8,))],
         compiler_params=pltpu.CompilerParams(vmem_limit_bytes=1 << 20),
         cost_estimate=pl.CostEstimate(
             flops=0, bytes_accessed=2 * count * weight.shape[1], transcendentals=0
@@ -211,7 +216,7 @@
     hidden = gate_weight.shape[1]
     group = own * n_node
     block = 3 * width // n_dp
-    half, quarter = width // 2, width // 4
+    half, quarter = width // 2, width // 8
     chips = range(2, n_node, 2)
     groups = range(1, n_dp)
     weight_bytes = 2 * width * hidden

time: 51.9 us -> 52.1 us (level)
  no operation moved by 1% of the time
where the time goes in v7:
time: 52.1 us; the launch traced here: 51.9 us
  Pallas kernels  31.8 us (61%)
  starting transfers between devices  17.9 us (34%)
  waiting for transfers between devices  1.29 us (2%)
  between operations  0.88 us (2%)
    ppermute x15, starting transfers between devices, permute(): lax.ppermute(array, axis, xor_pairs(mesh_shape[axis == 'node'], step))  17.9 us
    pallas_call x1, Pallas kernels, shards_group(): pl.pallas_call(lambda *refs: forward_kernel(chunk, *refs), out_shape=[jax...  8.52 us
    pallas_call x1, Pallas kernels, shards_group(): pl.pallas_call(lambda *refs: product_kernel(n_dp, cuts, *refs), out_shape...  8.01 us
    pallas_call x1, Pallas kernels, shards_group(): pl.pallas_call(lambda *refs: backward_kernel(chunk, *refs), out_shape=(ja...  7.65 us
    pallas_call x2, Pallas kernels, load_rows(): pl.pallas_call(lambda *refs: load_kernel(first, count, *refs), out_shape=...  6.68 us
    ppermute x15, waiting for transfers between devices, permute(): lax.ppermute(array, axis, xor_pairs(mesh_shape[axis == 'node'], step))  1.29 us
  transfers between devices with their start and end apart: 15, of which 1 were waited for; matrix products, arithmetic and copies ran while one was open for 0% of the time, Pallas kernels for 59%

profile of v7, /device:TPU:0, one launch (start us, length us, event | category | flops | bytes accessed | tf_op | source)
XLA Modules:
  0.0 51.9 jit_solution(10227262383068149131)
XLA Ops:
  0.6 0.5 collective-permute-start.1
  1.2 0.1 collective-permute-start
  1.2 1.8 %load_gate_a.1 = (bf16[4096,1792]{1,0:T(8,128)(2,1)S(1)}, f32[8,128]{1,0:T(8,128)S(1)}) custom-call(bf16[4096,1792]{1,0:T(8,128)(2,1)} %refs_0_.3, bf16[2,4096]{1,0:T(2,128)(2,1)} %normed.1), custom_call_target="tpu_custom_call" | custom-call | bytes 1835008 | tf_op jit(solution)/shard_map/load_gate_a/pallas_call | solution.py:75
  3.0 0.0 collective-permute-done.1.other_cotangent
  3.0 0.0 collective-permute-done.other_normed
  3.1 3.9 %collective-permute-start.4 = (bf16[2,2,2,4096]{3,2,1,0:T(2,128)(2,1)S(1)}, bf16[2,2,2,4096]{3,2,1,0:T(2,128)(2,1)S(1)}, u32[]{:S(2)}, u32[]{:S(2)}) collective-permute-start(bf16[2,2,2,4096]{3,2,1,0:T(2,128)(2,1)S(1)} %pair.1.refs_0_), channel_id=1, source_target_pairs={{0,6},{1,7},{2,4},{3,5},{4,2},{5,3},{6,0},{7,1},{8,14},{9,15},{10,... | collective-permute-start | bytes 196616 | tf_op jit(solution)/shard_map/ppermute | solution.py:225
  7.0 0.5 collective-permute-start.3
  7.5 0.1 collective-permute-start.2
  7.7 4.9 %load_gate_b.1 = (bf16[4096,1792]{1,0:T(8,128)(2,1)S(1)}, f32[8,128]{1,0:T(8,128)S(1)}) custom-call(bf16[4096,1792]{1,0:T(8,128)(2,1)} %refs_0_.3, f32[8,128]{1,0:T(8,128)S(1)} %get-tuple-element.22.after.refs_1_, bf16[4096,1792]{1,0:T(8,128)(2,1)S(1)} %get-tuple-element.23.refs_2_), custom_call_target="tpu_custom_call", output_to_operand_aliasing={{0}: (2, {})} | custom-call | bytes 12845056 | tf_op jit(solution)/shard_map/load_gate_b/pallas_call | solution.py:75
  12.6 0.0 collective-permute-done.4.refs_3_
  12.6 0.0 collective-permute-done.3.refs_2_
  12.6 0.0 collective-permute-done.2.refs_1_
  12.6 0.2 arrange.1
  12.8 2.0 %collective-permute-start.5 = (bf16[16,3072]{1,0:T(8,128)(2,1)S(1)}, bf16[16,3072]{1,0:T(8,128)(2,1)S(1)}, u32[]{:S(2)}, u32[]{:S(2)}) collective-permute-start(bf16[16,3072]{1,0:T(8,128)(2,1)S(1)} %get-tuple-element.32), channel_id=1, source_target_pairs={{0,8},{8,0},{16,24},{24,16},{1,9},{9,1},{17,25},{25,17},{2,10},{10... | collective-permute-start | bytes 294920 | tf_op jit(solution)/shard_map/ppermute | solution.py:225
  14.9 2.6 %collective-permute-start.6 = (bf16[16,3072]{1,0:T(8,128)(2,1)S(1)}, bf16[16,3072]{1,0:T(8,128)(2,1)S(1)}, u32[]{:S(2)}, u32[]{:S(2)}) collective-permute-start(bf16[16,3072]{1,0:T(8,128)(2,1)S(1)} %get-tuple-element.33), channel_id=1, source_target_pairs={{0,16},{8,24},{16,0},{24,8},{1,17},{9,25},{17,1},{25,9},{2,18},{10... | collective-permute-start | bytes 294920 | tf_op jit(solution)/shard_map/ppermute | solution.py:225
  17.5 0.0 collective-permute-start.7
  17.5 8.5 %forward.1 = (bf16[3,16,1792]{2,1,0:T(8,128)(2,1)S(1)}, bf16[4096,1792]{1,0:T(8,128)(2,1)S(1)}, bf16[4096,1792]{1,0:T(8,128)(2,1)S(1)}) custom-call(bf16[2,16,4096]{2,1,0:T(8,128)(2,1)S(1)} %get-tuple-element.25.refs_0_, bf16[4096,1792]{1,0:T(8,128)(2,1)S(1)} %get-tuple-element.26.refs_1_, ...), custom_call_target="tpu_custom_call", output_to_operand_aliasing={{2}: (1, {})} | custom-call | flops 704643072 | bytes 29360128 | tf_op jit(solution)/shard_map/forward/pallas_call | solution.py:251
  26.0 0.0 collective-permute-done.5.refs_1_
  26.1 0.0 collective-permute-done.7.refs_3_
  26.1 0.9 %collective-permute-start.8 = (bf16[2,16,1792]{2,1,0:T(8,128)(2,1)S(1)}, bf16[2,16,1792]{2,1,0:T(8,128)(2,1)S(1)}, u32[]{:S(2)}, u32[]{:S(2)}) collective-permute-start(bf16[2,16,1792]{2,1,0:T(8,128)(2,1)S(1)} %get-tuple-element.35), channel_id=1, source_target_pairs={{0,8},{8,0},{16,24},{24,16},{1,9},{9,1},{17,25},{25,17},{2,10},{10... | collective-permute-start | bytes 344072 | tf_op jit(solution)/shard_map/ppermute | solution.py:225
  27.1 3.5 %collective-permute-start.9 = (bf16[2,16,1792]{2,1,0:T(8,128)(2,1)S(1)}, bf16[2,16,1792]{2,1,0:T(8,128)(2,1)S(1)}, u32[]{:S(2)}, u32[]{:S(2)}) collective-permute-start(bf16[2,16,1792]{2,1,0:T(8,128)(2,1)S(1)} %get-tuple-element.36), channel_id=1, source_target_pairs={{0,16},{8,24},{16,0},{24,8},{1,17},{9,25},{17,1},{25,9},{2,18},{10... | collective-permute-start | bytes 344072 | tf_op jit(solution)/shard_map/ppermute | solution.py:225
  30.6 0.0 collective-permute-start.10
  30.6 7.7 %backward.1 = (f32[8,4096]{1,0:T(8,128)S(1)}, bf16[8,4096]{1,0:T(8,128)(2,1)S(1)}) custom-call(bf16[3,16,1792]{2,1,0:T(8,128)(2,1)S(1)} %get-tuple-element.27.refs_0_, bf16[4096,1792]{1,0:T(8,128)(2,1)S(1)} %get-tuple-element.28.refs_1_, bf16[4096,1792]{1,0:T(8,128)(2,1)S(1)} %get-tuple-element.29.refs_2_), custom_call_target="tpu_custom_call" | custom-call | flops 469762048 | bytes 29360128 | tf_op jit(solution)/shard_map/backward/pallas_call | solution.py:283
  38.2 0.0 collective-permute-done.9.refs_1_.refs_6_
  38.3 0.1 collective-permute-start.11
  38.4 1.2 %collective-permute-done.11 = bf16[8,4096]{1,0:T(8,128)(2,1)S(1)} collective-permute-done((bf16[8,4096]{1,0:T(8,128)(2,1)S(1)}, bf16[8,4096]{1,0:T(8,128)(2,1)S(1)}, u32[]{:S(2)}, u32[]{:S(2)}) %collective-permute-start.11) | collective-permute-done | bytes 65568 | tf_op jit(solution)/shard_map/ppermute | solution.py:225
  39.7 2.7 %collective-permute-start.14 = (bf16[2,4096]{1,0:T(2,128)(2,1)S(1)}, bf16[2,4096]{1,0:T(2,128)(2,1)S(1)}, u32[]{:S(2)}, u32[]{:S(2)}) collective-permute-start(bf16[2,4096]{1,0:T(2,128)(2,1)S(1)} %get-tuple-element.44), channel_id=1, source_target_pairs={{0,6},{1,7},{2,4},{3,5},{4,2},{5,3},{6,0},{7,1},{8,14},{9,15},{10,... | collective-permute-start | bytes 49160 | tf_op jit(solution)/shard_map/ppermute | solution.py:225
  42.4 0.5 collective-permute-start.13
  42.9 0.3 collective-permute-start.12
  43.2 8.0 %product.1 = (f32[3072,1792]{1,0:T(8,128)}, f32[8,128]{1,0:T(8,128)S(1)}) custom-call(bf16[16,3072]{1,0:T(8,128)(2,1)S(1)} %get-tuple-element.38.refs_0_, bf16[16,3072]{1,0:T(8,128)(2,1)S(1)} %collective-permute-done.5.refs_1_, bf16[16,3072]{1,0:T(8,128)(2,1)S(1)} %collective-permute-done.6.refs_2_, bf16[16,3072]{1,0:T(8,128)(2,1)S(1)} %collective-permute-done.7.refs_3_, ...), custom_call_target="tpu_custom_call" | custom-call | flops 704643072 | bytes 22020096 | tf_op jit(solution)/shard_map/product/pallas_call | solution.py:313
  51.3 0.0 collective-permute-done.12.refs_1_
  51.3 0.7 %final_sum.1 = bf16[2,4096]{1,0:T(2,128)(2,1)} custom-call(f32[8,4096]{1,0:T(8,128)S(1)} %get-tuple-element.43.refs_0_, bf16[2,4096]{1,0:T(2,128)(2,1)S(1)} %collective-permute-done.12.refs_1_, bf16[2,4096]{1,0:T(2,128)(2,1)S(1)} %collective-permute-done.13.refs_2_, bf16[2,4096]{1,0:T(2,128)(2,1)S(1)} %collective-permute-done.14.refs_3_, ...), custom_call_target="tpu_custom_call" | custom-call | tf_op jit(solution)/shard_map/final_sum/pallas_call | solution.py:335
  (23 shorter events, 0.2 us)
Async XLA Ops:
  0.6 2.4 %copy-start.1 = (bf16[2,4096]{1,0:T(2,128)(2,1)S(1)}, bf16[2,4096]{1,0:T(2,128)(2,1)}, u32[]{:S(2)}) copy-start(bf16[2,4096]{1,0:T(2,128)(2,1)} %cotangent.1) | copy-start | bytes 49156
  0.6 2.4 %copy-start = (bf16[2,4096]{1,0:T(2,128)(2,1)S(1)}, bf16[2,4096]{1,0:T(2,128)(2,1)}, u32[]{:S(2)}) copy-start(bf16[2,4096]{1,0:T(2,128)(2,1)} %normed.1) | copy-start | bytes 49156
  0.6 2.4 %collective-permute-start.1 = (bf16[2,4096]{1,0:T(2,128)(2,1)}, bf16[2,4096]{1,0:T(2,128)(2,1)S(1)}, u32[]{:S(2)}, u32[]{:S(2)}) collective-permute-start(bf16[2,4096]{1,0:T(2,128)(2,1)} %cotangent.1), channel_id=1, source_target_pairs={{0,1},{1,0},{2,3},{3,2},{4,5},{5,4},{6,7},{7,6},{8,9},{9,8},{10,11... | collective-permute-start | bytes 49160 | tf_op jit(solution)/shard_map/ppermute | solution.py:225
  1.2 1.9 %collective-permute-start = (bf16[2,4096]{1,0:T(2,128)(2,1)}, bf16[2,4096]{1,0:T(2,128)(2,1)S(1)}, u32[]{:S(2)}, u32[]{:S(2)}) collective-permute-start(bf16[2,4096]{1,0:T(2,128)(2,1)} %normed.1), channel_id=1, source_target_pairs={{0,1},{1,0},{2,3},{3,2},{4,5},{5,4},{6,7},{7,6},{8,9},{9,8},{10,11... | collective-permute-start | bytes 49160 | tf_op jit(solution)/shard_map/ppermute | solution.py:225
  1.2 16.2 %slice-start = ((s8[14680064]{0:T(1024)(128)(4,1)}), s8[4194304]{0:T(1024)(128)(4,1)S(1)}, s32[]{:S(2)}) async-start(s8[14680064]{0:T(1024)(128)(4,1)} %bitcast), calls=%async_computation | async-start | bytes 8388608
  1.2 16.2 %slice-start.1 = ((s8[14680064]{0:T(1024)(128)(4,1)}), s8[4194304]{0:T(1024)(128)(4,1)S(1)}, s32[]{:S(2)}) async-start(s8[14680064]{0:T(1024)(128)(4,1)} %bitcast), calls=%async_computation.1 | async-start | bytes 8388608
  3.1 9.5 %collective-permute-start.4 = (bf16[2,2,2,4096]{3,2,1,0:T(2,128)(2,1)S(1)}, bf16[2,2,2,4096]{3,2,1,0:T(2,128)(2,1)S(1)}, u32[]{:S(2)}, u32[]{:S(2)}) collective-permute-start(bf16[2,2,2,4096]{3,2,1,0:T(2,128)(2,1)S(1)} %pair.1.refs_0_), channel_id=1, source_target_pairs={{0,6},{1,7},{2,4},{3,5},{4,2},{5,3},{6,0},{7,1},{8,14},{9,15},{10,... | collective-permute-start | bytes 196616 | tf_op jit(solution)/shard_map/ppermute | solution.py:225
  7.0 5.6 %collective-permute-start.3 = (bf16[2,2,2,4096]{3,2,1,0:T(2,128)(2,1)S(1)}, bf16[2,2,2,4096]{3,2,1,0:T(2,128)(2,1)S(1)}, u32[]{:S(2)}, u32[]{:S(2)}) collective-permute-start(bf16[2,2,2,4096]{3,2,1,0:T(2,128)(2,1)S(1)} %pair.1.refs_0_), channel_id=1, source_target_pairs={{0,4},{1,5},{2,6},{3,7},{4,0},{5,1},{6,2},{7,3},{8,12},{9,13},{10,... | collective-permute-start | bytes 196616 | tf_op jit(solution)/shard_map/ppermute | solution.py:225
  7.5 5.1 %collective-permute-start.2 = (bf16[2,2,2,4096]{3,2,1,0:T(2,128)(2,1)S(1)}, bf16[2,2,2,4096]{3,2,1,0:T(2,128)(2,1)S(1)}, u32[]{:S(2)}, u32[]{:S(2)}) collective-permute-start(bf16[2,2,2,4096]{3,2,1,0:T(2,128)(2,1)S(1)} %pair.1.refs_0_), channel_id=1, source_target_pairs={{0,2},{1,3},{2,0},{3,1},{4,6},{5,7},{6,4},{7,5},{8,10},{9,11},{10,... | collective-permute-start | bytes 196616 | tf_op jit(solution)/shard_map/ppermute | solution.py:225
  7.7 9.8 %slice-start.2 = ((s8[14680064]{0:T(1024)(128)(4,1)}), s8[4194304]{0:T(1024)(128)(4,1)S(1)}, s32[]{:S(2)}) async-start(s8[14680064]{0:T(1024)(128)(4,1)} %bitcast), calls=%async_computation.2 | async-start | bytes 8388608
  7.7 9.8 %slice-start.3 = ((s8[14680064]{0:T(1024)(128)(4,1)}), s8[2097152]{0:T(1024)(128)(4,1)S(1)}, s32[]{:S(2)}) async-start(s8[14680064]{0:T(1024)(128)(4,1)} %bitcast), calls=%async_computation.3 | async-start | bytes 4194304
  12.8 13.2 %collective-permute-start.5 = (bf16[16,3072]{1,0:T(8,128)(2,1)S(1)}, bf16[16,3072]{1,0:T(8,128)(2,1)S(1)}, u32[]{:S(2)}, u32[]{:S(2)}) collective-permute-start(bf16[16,3072]{1,0:T(8,128)(2,1)S(1)} %get-tuple-element.32), channel_id=1, source_target_pairs={{0,8},{8,0},{16,24},{24,16},{1,9},{9,1},{17,25},{25,17},{2,10},{10... | collective-permute-start | bytes 294920 | tf_op jit(solution)/shard_map/ppermute | solution.py:225
  14.9 11.2 %collective-permute-start.6 = (bf16[16,3072]{1,0:T(8,128)(2,1)S(1)}, bf16[16,3072]{1,0:T(8,128)(2,1)S(1)}, u32[]{:S(2)}, u32[]{:S(2)}) collective-permute-start(bf16[16,3072]{1,0:T(8,128)(2,1)S(1)} %get-tuple-element.33), channel_id=1, source_target_pairs={{0,16},{8,24},{16,0},{24,8},{1,17},{9,25},{17,1},{25,9},{2,18},{10... | collective-permute-start | bytes 294920 | tf_op jit(solution)/shard_map/ppermute | solution.py:225
  17.5 8.6 %collective-permute-start.7 = (bf16[16,3072]{1,0:T(8,128)(2,1)S(1)}, bf16[16,3072]{1,0:T(8,128)(2,1)S(1)}, u32[]{:S(2)}, u32[]{:S(2)}) collective-permute-start(bf16[16,3072]{1,0:T(8,128)(2,1)S(1)} %get-tuple-element.34), channel_id=1, source_target_pairs={{0,24},{8,16},{16,8},{24,0},{1,25},{9,17},{17,9},{25,1},{2,26},{10... | collective-permute-start | bytes 294920 | tf_op jit(solution)/shard_map/ppermute | solution.py:225
  26.1 12.1 %collective-permute-start.8 = (bf16[2,16,1792]{2,1,0:T(8,128)(2,1)S(1)}, bf16[2,16,1792]{2,1,0:T(8,128)(2,1)S(1)}, u32[]{:S(2)}, u32[]{:S(2)}) collective-permute-start(bf16[2,16,1792]{2,1,0:T(8,128)(2,1)S(1)} %get-tuple-element.35), channel_id=1, source_target_pairs={{0,8},{8,0},{16,24},{24,16},{1,9},{9,1},{17,25},{25,17},{2,10},{10... | collective-permute-start | bytes 344072 | tf_op jit(solution)/shard_map/ppermute | solution.py:225
  27.1 11.2 %collective-permute-start.9 = (bf16[2,16,1792]{2,1,0:T(8,128)(2,1)S(1)}, bf16[2,16,1792]{2,1,0:T(8,128)(2,1)S(1)}, u32[]{:S(2)}, u32[]{:S(2)}) collective-permute-start(bf16[2,16,1792]{2,1,0:T(8,128)(2,1)S(1)} %get-tuple-element.36), channel_id=1, source_target_pairs={{0,16},{8,24},{16,0},{24,8},{1,17},{9,25},{17,1},{25,9},{2,18},{10... | collective-permute-start | bytes 344072 | tf_op jit(solution)/shard_map/ppermute | solution.py:225
  30.6 7.7 %collective-permute-start.10 = (bf16[2,16,1792]{2,1,0:T(8,128)(2,1)S(1)}, bf16[2,16,1792]{2,1,0:T(8,128)(2,1)S(1)}, u32[]{:S(2)}, u32[]{:S(2)}) collective-permute-start(bf16[2,16,1792]{2,1,0:T(8,128)(2,1)S(1)} %get-tuple-element.37), channel_id=1, source_target_pairs={{0,24},{8,16},{16,8},{24,0},{1,25},{9,17},{17,9},{25,1},{2,26},{10... | collective-permute-start | bytes 344072 | tf_op jit(solution)/shard_map/ppermute | solution.py:225
  38.3 1.3 %collective-permute-start.11 = (bf16[8,4096]{1,0:T(8,128)(2,1)S(1)}, bf16[8,4096]{1,0:T(8,128)(2,1)S(1)}, u32[]{:S(2)}, u32[]{:S(2)}) collective-permute-start(bf16[8,4096]{1,0:T(8,128)(2,1)S(1)} %hold.1), channel_id=1, source_target_pairs={{0,1},{1,0},{2,3},{3,2},{4,5},{5,4},{6,7},{7,6},{8,9},{9,8},{10,11... | collective-permute-start | bytes 196616 | tf_op jit(solution)/shard_map/ppermute | solution.py:225
  39.7 11.6 %collective-permute-start.14 = (bf16[2,4096]{1,0:T(2,128)(2,1)S(1)}, bf16[2,4096]{1,0:T(2,128)(2,1)S(1)}, u32[]{:S(2)}, u32[]{:S(2)}) collective-permute-start(bf16[2,4096]{1,0:T(2,128)(2,1)S(1)} %get-tuple-element.44), channel_id=1, source_target_pairs={{0,6},{1,7},{2,4},{3,5},{4,2},{5,3},{6,0},{7,1},{8,14},{9,15},{10,... | collective-permute-start | bytes 49160 | tf_op jit(solution)/shard_map/ppermute | solution.py:225
  42.4 8.9 %collective-permute-start.13 = (bf16[2,4096]{1,0:T(2,128)(2,1)S(1)}, bf16[2,4096]{1,0:T(2,128)(2,1)S(1)}, u32[]{:S(2)}, u32[]{:S(2)}) collective-permute-start(bf16[2,4096]{1,0:T(2,128)(2,1)S(1)} %get-tuple-element.45), channel_id=1, source_target_pairs={{0,4},{1,5},{2,6},{3,7},{4,0},{5,1},{6,2},{7,3},{8,12},{9,13},{10,... | collective-permute-start | bytes 49160 | tf_op jit(solution)/shard_map/ppermute | solution.py:225
  42.9 8.4 %collective-permute-start.12 = (bf16[2,4096]{1,0:T(2,128)(2,1)S(1)}, bf16[2,4096]{1,0:T(2,128)(2,1)S(1)}, u32[]{:S(2)}, u32[]{:S(2)}) collective-permute-start(bf16[2,4096]{1,0:T(2,128)(2,1)S(1)} %get-tuple-element.46), channel_id=1, source_target_pairs={{0,2},{1,3},{2,0},{3,1},{4,6},{5,7},{6,4},{7,5},{8,10},{9,11},{10,... | collective-permute-start | bytes 49160 | tf_op jit(solution)/shard_map/ppermute | solution.py:225
